TPU v7x, 32 devices: a whole 2x2x4 slice. The times are simulated.
32 devices in a mesh: group: 4 (over y, x), dom: 8 (over z, core).
Axes of the slice: x: 2, y: 2, z: 4, core: 2. Of those that a mesh axis runs over, the one named last changes fastest.
Arguments:
- feats: bfloat16 [65536, 128], P(('group', 'dom')), may hold values from -6 to 6
- coords: bfloat16 [3, 65536], P(None, ('group', 'dom')), may hold values from 0 to 1
- msg_cot: bfloat16 [65536, 128], P(('group', 'dom')), may hold values from -6 to 6
- send_list: int32 [32, 4, 2], P(('group', 'dom')), may hold values from 0 to 15
- tiles: int32 [32, 96, 2], P(('group', 'dom')), may hold values from 0 to 23, as said below
- tile_count: int32 [32], P(('group', 'dom')), may hold values from 24 to 96, as said below
- wavevec: int32 [512, 3], replicated, may hold values from -4 to 4
- w_rad_a: bfloat16 [128, 128], replicated, may hold values from -0.5 to 0.5
- w_rad_b: bfloat16 [128, 128], replicated, may hold values from -0.5 to 0.5
- w_charge: bfloat16 [128, 128], replicated, may hold values from -0.5 to 0.5
- w_long: bfloat16 [128, 128], replicated, may hold values from -0.5 to 0.5
- norm_gain: float32 [128], replicated, may hold values from 0.1 to 1.9
- w_in: bfloat16 [128, 256], replicated, may hold values from -0.5 to 0.5
- w_out: bfloat16 [256, 128], replicated, may hold values from -0.375 to 0.375
Outputs:
- new_feats: bfloat16 [65536, 128], P(('group', 'dom'))
- feat_adjoint: float32 [65536, 128], P(('group', 'dom'))
Inputs may be any that keep to these rules, and one draw needn't show every extreme that they name: In every domain the first 8 tiles have source blocks 16, 17, ... in order, one each; targets are below 16 and sources below 24. `tile_count`: tiles at or after a domain's count are not used; some domain has all 96 live.
All inputs are finite; a program needn't handle non-finite values.
Results may differ from a plain program's by a relative error of at most 0.0067.
Values may be sent and summed in bfloat16 or wider, within the bound.
No kernel may reach another device: no remote copies, remote signals or barrier semaphores. Data moves between devices by JAX's collectives and lax.ppermute only.
A program may use at most 64 MiB of HBM per device.

v0:
```python
import functools

import jax
import jax.numpy as jnp
import numpy as np
from jax import lax
from jax.experimental import pallas as pl
from jax.experimental.pallas import tpu as pltpu
from jax.sharding import PartitionSpec as P

BLK = 128
HB = 2
WMAX = 4
COORD_ROWS = 16

RADIAL_A = 6.0
MSG_SCALE = 1.0 / 32.0
LOG2E = 1.4426950408889634

NT = (((1,), (1,)), ((), ()))
NN = (((1,), (0,)), ((), ()))

VMEM = pltpu.VMEM
SMEM = pltpu.SMEM
BF16 = jnp.bfloat16
F32 = jnp.float32


def dot(a, b, dims=NN):
    return lax.dot_general(a, b, dims, preferred_element_type=F32)


PAIRS = [(0, b) for b in range(1, WMAX + 1)] + [
    (a, b) for a in range(1, WMAX + 1) for b in range(-WMAX, WMAX + 1)
]
NPAIR = len(PAIRS)
BASE_ROWS = 48
HALF = BASE_ROWS + WMAX * 2 * NPAIR


def base_table():
    rows = np.zeros((BASE_ROWS, COORD_ROWS), np.float32)
    for r, (a, b) in enumerate(PAIRS):
        rows[r, 0], rows[r, 1] = a, b
    for m in range(WMAX + 1):
        rows[NPAIR + m, 2] = m
    return rows


def grid_norm2():
    base = (base_table() ** 2).sum(1)
    parts = [base]
    for m in range(1, WMAX + 1):
        parts += [base[:NPAIR] + m * m] * 2
    return np.concatenate(parts).reshape(HALF, 1).astype(np.float32)


def taylor(first, count):
    coef, out = 1.0, []
    for k in range(1, first + 1):
        coef /= k
    power = first
    for _ in range(count):
        out.append(coef)
        coef = -coef / ((power + 1) * (power + 2))
        power += 2
    return out


SIN_COEF = [c * np.pi ** (2 * i + 1) for i, c in enumerate(taylor(1, 7))]
COS_COEF = [c * np.pi ** (2 * i) for i, c in enumerate(taylor(0, 8))]


def horner(z, coefs):
    acc = jnp.full_like(z, coefs[-1])
    for c in coefs[-2::-1]:
        acc = acc * z + c
    return acc


def cos_sin_turns(turns):
    r = turns - jnp.round(turns)
    z = r * r
    s = r * horner(z, SIN_COEF)
    c = horner(z, COS_COEF)
    return 1.0 - 2.0 * (s * s), 2.0 * (s * c)


def trig_chunk(table, xyz16):
    c, s = cos_sin_turns(dot(table, xyz16))
    cos_parts, sin_parts = [c.astype(BF16)], [s.astype(BF16)]
    cp, sp = c[:NPAIR], s[:NPAIR]
    for m in range(1, WMAX + 1):
        cz, sz = c[NPAIR + m : NPAIR + m + 1], s[NPAIR + m : NPAIR + m + 1]
        cc, ss, sc, cs = cp * cz, sp * sz, sp * cz, cp * sz
        cos_parts.append(jnp.concatenate([cc - ss, cc + ss], axis=0).astype(BF16))
        sin_parts.append(jnp.concatenate([sc + cs, sc - cs], axis=0).astype(BF16))
    return jnp.concatenate(cos_parts + sin_parts, axis=0)


def coords16(xyz):
    return jnp.concatenate(
        [xyz.astype(F32), jnp.zeros((COORD_ROWS - 3, xyz.shape[1]), F32)], axis=0
    ).astype(BF16)


def split3(v):
    hi = v.astype(BF16).astype(F32)
    mid = (v - hi).astype(BF16).astype(F32)
    return hi, mid, (v - hi) - mid


def rows_near(xyz):
    x = xyz.astype(F32)
    hi, mid, lo = split3(jnp.sum(x * x, axis=0, keepdims=True))
    one = jnp.ones_like(hi)
    return jnp.concatenate(
        [-2.0 * x, hi, mid, lo, one, one, one, jnp.zeros((7, x.shape[1]), F32)], axis=0
    ).astype(BF16)


def rows_far(xyz):
    x = xyz.astype(F32)
    hi, mid, lo = split3(jnp.sum(x * x, axis=0, keepdims=True))
    one = jnp.ones_like(hi)
    return jnp.concatenate(
        [x, one, one, one, hi, mid, lo, jnp.zeros((7, x.shape[1]), F32)], axis=0
    ).astype(BF16)


def select_kernel(lists_ref, order_ref, feats_ref, coords_ref, *rest):
    outs = rest[:4]
    for slot in range(4):
        direction = order_ref[slot]
        pieces = []
        for h in range(HB):
            b = lists_ref[0, direction, h]
            start = pl.multiple_of(b * BLK, BLK)
            outs[slot][pl.ds(h * BLK, BLK), :] = feats_ref[pl.ds(start, BLK), :]
            pieces.append(coords_ref[:, pl.ds(start, BLK)].astype(F32))
            pieces.append(jnp.zeros((COORD_ROWS // HB - 3, BLK), F32))
        outs[slot][pl.ds(HB * BLK, COORD_ROWS), :] = jnp.concatenate(pieces, axis=0).astype(BF16)


def struct_kernel(chunk, flip_ref, feats_ref, coords_ref, w_ref, table_ref, keep_ref, send_ref, total_ref):
    atoms = feats_ref.shape[0]
    table = table_ref[...].astype(BF16)
    w = w_ref[...]
    for first in range(0, atoms, chunk):
        charges = dot(feats_ref[pl.ds(first, chunk), :], w).astype(BF16)
        trig = trig_chunk(table, coords16(coords_ref[:, pl.ds(first, chunk)]))
        part = dot(trig, charges)
        if first == 0:
            total_ref[...] = part
        else:
            total_ref[...] += part
    mine = pl.multiple_of(flip_ref[0] * HALF, 8)
    other = pl.multiple_of((1 - flip_ref[0]) * HALF, 8)
    keep_ref[...] = total_ref[pl.ds(mine, HALF), :]
    send_ref[...] = total_ref[pl.ds(other, HALF), :].astype(BF16)


def tile_kernel(
    unroll,
    order_ref,
    tiles_ref,
    count_ref,
    feats_ref,
    coords_ref,
    cot_ref,
    wa_ref,
    wb_ref,
    got0,
    got1,
    got2,
    got3,
    msg_ref,
    own_ref,
    held0,
    held1,
    held2,
    held3,
    proj_ref,
    cotp_ref,
    far_ref,
    near_ref,
    grad_ref,
):
    atoms = feats_ref.shape[0]
    nblk = atoms // BLK
    extent = nblk + 4 * HB
    gots = (got0, got1, got2, got3)
    helds = (held0, held1, held2, held3)
    wa, wb = wa_ref[...], wb_ref[...]
    w_cat = jnp.concatenate([wa.astype(F32).T, wb.astype(F32).T], axis=0).astype(BF16)
    w_side = jnp.concatenate([wa, wb], axis=0)

    def source_block(j, feats, xyz):
        both = dot(w_cat, feats, NT).astype(BF16)
        proj_ref[j, :, 0:BLK] = both[:BLK]
        proj_ref[j, :, BLK:] = both[BLK:]
        far_ref[j] = rows_far(xyz).astype(F32).T.astype(BF16)

    for b in range(nblk):
        xyz = coords_ref[:, b * BLK : (b + 1) * BLK]
        source_block(b, feats_ref[b * BLK : (b + 1) * BLK, :], xyz)
        near_ref[b] = rows_near(xyz)
        both = dot(cot_ref[b * BLK : (b + 1) * BLK, :], w_side, NT).astype(BF16)
        cotp_ref[b, 0:BLK, :] = both[:, :BLK]
        cotp_ref[b, BLK:, :] = both[:, BLK:]
    for slot in range(4):
        tail = gots[slot][HB * BLK : HB * BLK + COORD_ROWS, :].astype(F32)
        for h in range(HB):
            j = nblk + order_ref[slot + 4] * HB + h
            at = h * (COORD_ROWS // HB)
            source_block(j, gots[slot][h * BLK : (h + 1) * BLK, :], tail[at : at + 3])

    msg_ref[...] = jnp.zeros_like(msg_ref)
    grad_ref[...] = jnp.zeros_like(grad_ref)

    def group(first, width):
        idx = [(tiles_ref[0, first + u, 0], tiles_ref[0, first + u, 1]) for u in range(width)]
        kers = []
        for i, j in idx:
            d = dot(far_ref[j], near_ref[i])
            a = jnp.exp2(d * (-RADIAL_A * LOG2E))
            a2 = a * a
            b = (a2 * a2) * a
            kers.append((a.astype(BF16), b.astype(BF16)))
        for (i, j), (ka, kb) in zip(idx, kers):
            msg_ref[i] += dot(proj_ref[j], jnp.concatenate([ka, kb], axis=0))
            grad_ref[j] += dot(jnp.concatenate([ka, kb], axis=1), cotp_ref[i])

    count = count_ref[0]
    whole = count // unroll

    @pl.loop(0, whole)
    def _(step):
        group(step * unroll, unroll)

    @pl.loop(whole * unroll, count)
    def _(step):
        group(step, 1)

    for b in range(nblk):
        own_ref[b * BLK : (b + 1) * BLK, :] = grad_ref[b] * MSG_SCALE
    for slot in range(4):
        for h in range(HB):
            j = nblk + order_ref[slot + 4] * HB + h
            helds[slot][h * BLK : (h + 1) * BLK, :] = (grad_ref[j] * MSG_SCALE).astype(BF16)


def update_kernel(
    chunk,
    group_atoms,
    flip_ref,
    mine_ref,
    other_ref,
    wave_ref,
    norm2_ref,
    table_ref,
    feats_ref,
    coords_ref,
    msg_ref,
    w_long_ref,
    gain_ref,
    w_in_ref,
    w_out_ref,
    out_ref,
    mixw_ref,
):
    atoms, width = feats_ref.shape
    pick = (
        lax.broadcasted_iota(jnp.int32, (8, 3), 0) == lax.broadcasted_iota(jnp.int32, (8, 3), 1)
    ).astype(F32).astype(BF16)
    n = dot(pick, wave_ref[...].astype(F32).astype(BF16), NT)
    n0, n1, n2 = n[0:1], n[1:2], n[2:3]
    lead = jnp.where(n0 != 0.0, n0, jnp.where(n1 != 0.0, n1, n2))
    sign = jnp.where(lead < 0.0, -1.0, 1.0)
    n0, n1, n2 = n0 * sign, n1 * sign, n2 * sign
    pair = jnp.where(n0 == 0.0, n1 - 1.0, n0 * (2 * WMAX + 1) + n1 + (2.0 * WMAX - (2 * WMAX + 1)))
    shift = jnp.where(
        n2 == 0.0,
        0.0,
        BASE_ROWS
        + (jnp.abs(n2) - 1.0) * (2 * NPAIR)
        + jnp.where(n2 < 0.0, float(NPAIR), 0.0),
    )
    row = jnp.where((n0 == 0.0) & (n1 == 0.0), NPAIR + n2, pair + shift)
    same = lax.broadcasted_iota(jnp.int32, (HALF, row.shape[1]), 0) == row.astype(jnp.int32)
    times = jnp.sum(same.astype(F32), axis=1, keepdims=True)
    norm2 = norm2_ref[...]
    strength = times * (jnp.exp(-norm2 / 16.0) / (1.0 + norm2) * float(group_atoms) ** (-0.5))

    w_long_t = w_long_ref[...].astype(F32).T.astype(BF16)
    mine = flip_ref[0] == 0
    a, b = mine_ref[...].astype(F32), other_ref[...].astype(F32)
    cos_w = (strength * jnp.where(mine, a, b)).astype(BF16)
    sin_w = (strength * jnp.where(mine, b, a)).astype(BF16)
    mix_w = dot(w_long_t, jnp.concatenate([cos_w, sin_w], axis=0), NT).astype(BF16)

    table = table_ref[...].astype(BF16)
    gain = jnp.broadcast_to(gain_ref[...], (chunk, width)).T
    w_in_t = w_in_ref[...].astype(F32).T.astype(BF16)
    w_out_t = w_out_ref[...].astype(F32).T.astype(BF16)
    for first in range(0, atoms, chunk):
        trig = trig_chunk(table, coords16(coords_ref[:, pl.ds(first, chunk)]))
        mixed = dot(mix_w, trig)
        msg = jnp.concatenate(
            [msg_ref[(first // BLK) + i] for i in range(chunk // BLK)], axis=1
        )
        mixed = mixed + msg * MSG_SCALE + feats_ref[pl.ds(first, chunk), :].astype(F32).T
        scale = lax.rsqrt(jnp.mean(mixed * mixed, axis=0, keepdims=True) + 1e-06)
        normed = (mixed * scale * gain).astype(BF16)
        pre = dot(w_in_t, normed)
        hidden = (pre / (1.0 + jnp.exp(-pre))).astype(BF16)
        out = mixed + dot(w_out_t, hidden)
        out_ref[pl.ds(first, chunk), :] = out.T.astype(BF16)


def adjoint_kernel(lists_ref, order_ref, own_ref, r0, r1, r2, r3, out_ref):
    out_ref[...] = own_ref[...]
    for slot, ref in enumerate((r0, r1, r2, r3)):
        for h in range(HB):
            b = lists_ref[0, order_ref[slot], h]
            at = pl.ds(pl.multiple_of(b * BLK, BLK), BLK)
            out_ref[at, :] += ref[h * BLK : (h + 1) * BLK, :].astype(F32)


def call(kernel, outs, args, specs, scratch=(), flops=0, nbytes=0):
    single = not isinstance(outs, (list, tuple))
    return pl.pallas_call(
        kernel,
        out_shape=outs,
        in_specs=[pl.BlockSpec(memory_space=s) for s in specs],
        out_specs=pl.BlockSpec(memory_space=VMEM)
        if single
        else [pl.BlockSpec(memory_space=VMEM) for _ in outs],
        scratch_shapes=list(scratch),
        compiler_params=pltpu.CompilerParams(vmem_limit_bytes=40 * 1024 * 1024),
        cost_estimate=pl.CostEstimate(flops=flops, bytes_accessed=nbytes, transcendentals=0),
    )(*args)


def exchange(value, axis, partner):
    length = lax.axis_size(axis)
    return lax.ppermute(value, axis, [(i, partner(i) % length) for i in range(length)])


def body(
    feats,
    coords,
    msg_cot,
    send_list,
    tiles,
    tile_count,
    wavevec,
    w_rad_a,
    w_rad_b,
    w_charge,
    w_long,
    norm_gain,
    w_in,
    w_out,
):
    atoms, width = feats.shape
    nblk = atoms // BLK
    extent = nblk + 4 * HB
    domains = lax.axis_size("dom")
    parity = lax.axis_index("dom") % 2
    odd = parity.astype(jnp.int32)
    sds = jax.ShapeDtypeStruct

    order = jnp.stack([odd, 1 - odd, 2 + 0 * odd, 3 + 0 * odd, 1 - odd, odd, 2 + 0 * odd, 3 + 0 * odd])
    pairing = (
        ("dom", lambda i: i ^ 1, lambda i: i ^ 1),
        ("dom", lambda i: i + (1 if i % 2 else -1), lambda i: i + (1 if i % 2 else -1)),
        ("group", lambda i: i + 1, lambda i: i - 1),
        ("group", lambda i: i - 1, lambda i: i + 1),
    )

    sent = call(
        select_kernel,
        [sds((HB * BLK + COORD_ROWS, width), BF16)] * 4,
        (send_list, order, feats, coords),
        (SMEM, SMEM, VMEM, VMEM),
        nbytes=1 << 20,
    )
    got = [exchange(sent[s], pairing[s][0], pairing[s][1]) for s in range(4)]

    table = jnp.asarray(base_table())
    norm2 = jnp.asarray(grid_norm2())
    flip = odd.reshape(1)
    keep, send = call(
        functools.partial(struct_kernel, 256),
        [sds((HALF, width), F32), sds((HALF, width), BF16)],
        (flip, feats, coords, w_charge, table),
        (SMEM, VMEM, VMEM, VMEM, VMEM),
        scratch=[VMEM((2 * HALF, width), F32)],
        flops=2 * 2 * HALF * atoms * width,
        nbytes=1 << 20,
    )
    total = keep + exchange(send, "dom", lambda i: i ^ 1).astype(F32)
    step = 2
    while step < domains:
        total = total + exchange(total.astype(BF16), "dom", lambda i: i ^ step).astype(F32)
        step *= 2
    total = total.astype(BF16)
    other = exchange(total, "dom", lambda i: i ^ 1)

    msg, own, *held = call(
        functools.partial(tile_kernel, 4),
        [sds((nblk, width, BLK), F32), sds((atoms, width), F32)] + [sds((HB * BLK, width), BF16)] * 4,
        (order, tiles, tile_count, feats, coords, msg_cot, w_rad_a, w_rad_b, *got),
        (SMEM, SMEM, SMEM) + (VMEM,) * 9,
        scratch=[
            VMEM((extent, width, 2 * BLK), BF16),
            VMEM((nblk, 2 * BLK, width), BF16),
            VMEM((extent, BLK, COORD_ROWS), BF16),
            VMEM((nblk, COORD_ROWS, BLK), BF16),
            VMEM((extent, BLK, width), F32),
        ],
        flops=8 * tiles.shape[1] * BLK * BLK * width,
        nbytes=4 << 20,
    )
    back = [exchange(held[s], pairing[s][0], pairing[s][2]) for s in range(4)]

    new_feats = call(
        functools.partial(update_kernel, 256, atoms * domains),
        sds((atoms, width), BF16),
        (
            flip, total, other, wavevec, norm2, table, feats, coords, msg, w_long,
            norm_gain.reshape(1, width), w_in, w_out,
        ),
        (SMEM,) + (VMEM,) * 12,
        scratch=[VMEM((8, 128), F32)],
        flops=2 * 2 * HALF * atoms * width,
        nbytes=4 << 20,
    )
    adjoint = call(
        adjoint_kernel,
        sds((atoms, width), F32),
        (send_list, order, own, *back),
        (SMEM, SMEM) + (VMEM,) * 5,
        nbytes=2 << 20,
    )
    return (new_feats, adjoint)


def solution(mesh):
    split = ("group", "dom")
    return jax.shard_map(
        body,
        mesh=mesh,
        in_specs=(
            P(split, None),
            P(None, split),
            P(split, None),
            P(split, None, None),
            P(split, None, None),
            P(split),
            P(),
            P(),
            P(),
            P(),
            P(),
            P(),
            P(),
            P(),
        ),
        out_specs=(P(split, None), P(split, None)),
        check_vma=False,
    )
```

profile of v0, /device:TPU:0, one launch (start us, length us, event | category | flops | bytes accessed | tf_op | source)
XLA Modules:
  0.0 55.2 jit_solution(6079106689115323496)
XLA Ops:
  0.7 0.7 %copy-done.3 = bf16[3,2048]{1,0:T(4,128)(2,1)S(1)} copy-done((bf16[3,2048]{1,0:T(4,128)(2,1)S(1)}, bf16[3,2048]{1,0:T(4,128)(2,1)}, u32[]{:S(2)}) %copy-start.3) | copy-done | bytes 12312
  1.4 1.0 %copy-done = bf16[2048,128]{1,0:T(8,128)(2,1)S(1)} copy-done((bf16[2048,128]{1,0:T(8,128)(2,1)S(1)}, bf16[2048,128]{1,0:T(8,128)(2,1)}, u32[]{:S(2)}) %copy-start) | copy-done | bytes 524312
  2.4 0.7 %copy-done.7 = f32[48,16]{1,0:T(8,128)S(1)} copy-done((f32[48,16]{1,0:T(8,128)S(1)}, f32[48,16]{1,0:T(8,128)}, u32[]{:S(2)}) %copy-start.7) | copy-done | bytes 3096
  3.1 0.8 %copy-done.11 = bf16[128,128]{1,0:T(8,128)(2,1)S(1)} copy-done((bf16[128,128]{1,0:T(8,128)(2,1)S(1)}, bf16[128,128]{1,0:T(8,128)(2,1)}, u32[]{:S(2)}) %copy-start.11) | copy-done | bytes 32792
  3.9 2.2 %shard_map.167 = (f32[368,128]{1,0:T(8,128)S(1)}, bf16[368,128]{1,0:T(8,128)(2,1)S(1)}) custom-call(s32[1]{0:T(128)} %bitcast.flip_ref, bf16[2048,128]{1,0:T(8,128)(2,1)S(1)} %copy-done, bf16[3,2048]{1,0:T(4,128)(2,1)S(1)} %copy-done.3, bf16[128,128]{1,0:T(8,128)(2,1)S(1)} %copy-done.11, f32[48,16]{1,0:T(8,128)S(1)} %copy-done.7), custom_call_target="tpu_custom_call" | custom-call | flops 385875968 | bytes 1048576 | tf_op jit(solution)/shard_map/pallas_call | solution.py:332
  6.1 0.5 collective-permute-start
  6.6 0.9 %collective-permute-done = bf16[368,128]{1,0:T(8,128)(2,1)S(1)} collective-permute-done((bf16[368,128]{1,0:T(8,128)(2,1)S(1)}, bf16[368,128]{1,0:T(8,128)(2,1)S(1)}, u32[]{:S(2)}, u32[]{:S(2)}) %collective-permute-start) | collective-permute-done | bytes 94240 | tf_op jit(solution)/shard_map/ppermute | solution.py:347
  7.6 3.0 %collective-permute-start.1 = (bf16[368,128]{1,0:T(8,128)(2,1)S(1)}, bf16[368,128]{1,0:T(8,128)(2,1)S(1)}, u32[]{:S(2)}, u32[]{:S(2)}) collective-permute-start(bf16[368,128]{1,0:T(8,128)(2,1)S(1)} %fusion), channel_id=1, source_target_pairs={{0,2},{1,3},{2,0},{3,1},{4,6},{5,7},{6,4},{7,5},{8,10},{9,11},{10,... | collective-permute-start | bytes 282632 | tf_op jit(solution)/shard_map/ppermute | solution.py:347
  10.6 3.0 %collective-permute-done.1 = bf16[368,128]{1,0:T(8,128)(2,1)S(1)} collective-permute-done((bf16[368,128]{1,0:T(8,128)(2,1)S(1)}, bf16[368,128]{1,0:T(8,128)(2,1)S(1)}, u32[]{:S(2)}, u32[]{:S(2)}) %collective-permute-start.1) | collective-permute-done | bytes 94240 | tf_op jit(solution)/shard_map/ppermute | solution.py:347
  13.7 2.8 %collective-permute-start.2 = (bf16[368,128]{1,0:T(8,128)(2,1)S(1)}, bf16[368,128]{1,0:T(8,128)(2,1)S(1)}, u32[]{:S(2)}, u32[]{:S(2)}) collective-permute-start(bf16[368,128]{1,0:T(8,128)(2,1)S(1)} %fusion.1), channel_id=1, source_target_pairs={{0,4},{1,5},{2,6},{3,7},{4,0},{5,1},{6,2},{7,3},{8,12},{9,13},{10,... | collective-permute-start | bytes 282632 | tf_op jit(solution)/shard_map/ppermute | solution.py:347
  16.5 0.1 copy.18.lists_ref
  16.6 0.1 stack.10.order_ref
  16.7 0.6 %shard_map.168 = (bf16[272,128]{1,0:T(8,128)(2,1)S(1)}, bf16[272,128]{1,0:T(8,128)(2,1)S(1)}, bf16[272,128]{1,0:T(8,128)(2,1)S(1)}, bf16[272,128]{1,0:T(8,128)(2,1)S(1)}) custom-call(s32[1,4,2]{2,1,0:T(4,128)S(1)} %copy.18.lists_ref, s32[8]{0:T(128)S(1)} %stack.10.order_ref, bf16[2048,128]{1,0:T(8,128)(2,1)S(1)} %copy-done.1, bf16[3,2048]{1,0:T(4,128)(2,1)S(1)} %copy-done.3), custom_call_target="tpu_custom_call" | custom-call | bytes 1048576 | tf_op jit(solution)/shard_map/pallas_call | solution.py:332
  17.3 0.1 collective-permute-start.4
  17.4 1.7 %collective-permute-start.5 = (bf16[272,128]{1,0:T(8,128)(2,1)S(1)}, bf16[272,128]{1,0:T(8,128)(2,1)S(1)}, u32[]{:S(2)}, u32[]{:S(2)}) collective-permute-start(bf16[272,128]{1,0:T(8,128)(2,1)S(1)} %get-tuple-element.17), channel_id=1, source_target_pairs={{0,7},{1,2},{2,1},{3,4},{4,3},{5,6},{6,5},{7,0},{8,15},{9,10},{10,... | collective-permute-start | bytes 208904 | tf_op jit(solution)/shard_map/ppermute | solution.py:347
  19.1 1.5 %collective-permute-start.6 = (bf16[272,128]{1,0:T(8,128)(2,1)S(1)}, bf16[272,128]{1,0:T(8,128)(2,1)S(1)}, u32[]{:S(2)}, u32[]{:S(2)}) collective-permute-start(bf16[272,128]{1,0:T(8,128)(2,1)S(1)} %get-tuple-element.18), channel_id=1, source_target_pairs={{0,8},{8,16},{16,24},{24,0},{1,9},{9,17},{17,25},{25,1},{2,10},{10... | collective-permute-start | bytes 208904 | tf_op jit(solution)/shard_map/ppermute | solution.py:347
  20.6 1.4 %collective-permute-start.7 = (bf16[272,128]{1,0:T(8,128)(2,1)S(1)}, bf16[272,128]{1,0:T(8,128)(2,1)S(1)}, u32[]{:S(2)}, u32[]{:S(2)}) collective-permute-start(bf16[272,128]{1,0:T(8,128)(2,1)S(1)} %get-tuple-element.19), channel_id=1, source_target_pairs={{0,24},{8,0},{16,8},{24,16},{1,25},{9,1},{17,9},{25,17},{2,26},{10... | collective-permute-start | bytes 208904 | tf_op jit(solution)/shard_map/ppermute | solution.py:347
  22.7 0.1 copy.19.tiles_ref
  22.9 0.1 collective-permute-start.3
  23.0 0.1 collective-permute-done.5.got1
  23.1 1.6 %collective-permute-done.6.got2 = bf16[272,128]{1,0:T(8,128)(2,1)S(1)} collective-permute-done((bf16[272,128]{1,0:T(8,128)(2,1)S(1)}, bf16[272,128]{1,0:T(8,128)(2,1)S(1)}, u32[]{:S(2)}, u32[]{:S(2)}) %collective-permute-start.6) | collective-permute-done | bytes 69664 | tf_op jit(solution)/shard_map/ppermute | solution.py:347
  24.7 1.0 %collective-permute-done.7.got3 = bf16[272,128]{1,0:T(8,128)(2,1)S(1)} collective-permute-done((bf16[272,128]{1,0:T(8,128)(2,1)S(1)}, bf16[272,128]{1,0:T(8,128)(2,1)S(1)}, u32[]{:S(2)}, u32[]{:S(2)}) %collective-permute-start.7) | collective-permute-done | bytes 69664 | tf_op jit(solution)/shard_map/ppermute | solution.py:347
  25.7 1.0 %copy-done.10 = bf16[2048,128]{1,0:T(8,128)(2,1)S(1)} copy-done((bf16[2048,128]{1,0:T(8,128)(2,1)S(1)}, bf16[2048,128]{1,0:T(8,128)(2,1)}, u32[]{:S(2)}) %copy-start.10) | copy-done | bytes 524312
  26.7 8.1 %shard_map.169 = (f32[16,128,128]{2,1,0:T(8,128)S(1)}, f32[2048,128]{1,0:T(8,128)S(1)}, bf16[256,128]{1,0:T(8,128)(2,1)}, bf16[256,128]{1,0:T(8,128)(2,1)S(1)}, ...) custom-call(s32[8]{0:T(128)S(1)} %stack.10.order_ref, s32[1,96,2]{2,1,0:T(8,128)S(1)} %copy.19.tiles_ref, ...), custom_call_target="tpu_custom_call" | custom-call | flops 1610612736 | bytes 4194304 | tf_op jit(solution)/shard_map/pallas_call | solution.py:332
  34.9 0.8 %collective-permute-start.8 = (bf16[256,128]{1,0:T(8,128)(2,1)}, bf16[256,128]{1,0:T(8,128)(2,1)S(1)}, u32[]{:S(2)}, u32[]{:S(2)}) collective-permute-start(bf16[256,128]{1,0:T(8,128)(2,1)} %get-tuple-element.22), channel_id=1, source_target_pairs={{0,1},{1,0},{2,3},{3,2},{4,5},{5,4},{6,7},{7,6},{8,9},{9,8},{10,11... | collective-permute-start | bytes 196616 | tf_op jit(solution)/shard_map/ppermute | solution.py:347
  35.7 6.0 %collective-permute-start.10 = (bf16[256,128]{1,0:T(8,128)(2,1)S(1)}, bf16[256,128]{1,0:T(8,128)(2,1)S(1)}, u32[]{:S(2)}, u32[]{:S(2)}) collective-permute-start(bf16[256,128]{1,0:T(8,128)(2,1)S(1)} %get-tuple-element.24), channel_id=1, source_target_pairs={{0,24},{8,0},{16,8},{24,16},{1,25},{9,1},{17,9},{25,17},{2,26},{10... | collective-permute-start | bytes 196616 | tf_op jit(solution)/shard_map/ppermute | solution.py:347
  41.7 0.8 %copy.20.wave_ref = s32[512,3]{1,0:T(8,128)S(1)} copy(s32[512,3]{0,1:T(4,128)} %param.22) | data formatting | bytes 12288 | tf_op args[6]
  42.6 1.5 %collective-permute-done.10.r2 = bf16[256,128]{1,0:T(8,128)(2,1)S(1)} collective-permute-done((bf16[256,128]{1,0:T(8,128)(2,1)S(1)}, bf16[256,128]{1,0:T(8,128)(2,1)S(1)}, u32[]{:S(2)}, u32[]{:S(2)}) %collective-permute-start.10) | collective-permute-done | bytes 65568 | tf_op jit(solution)/shard_map/ppermute | solution.py:347
  44.1 2.8 %collective-permute-done.11.r3 = bf16[256,128]{1,0:T(8,128)(2,1)S(1)} collective-permute-done((bf16[256,128]{1,0:T(8,128)(2,1)S(1)}, bf16[256,128]{1,0:T(8,128)(2,1)S(1)}, u32[]{:S(2)}, u32[]{:S(2)}) %collective-permute-start.11) | collective-permute-done | bytes 65568 | tf_op jit(solution)/shard_map/ppermute | solution.py:347
  46.9 1.7 %shard_map.171 = f32[2048,128]{1,0:T(8,128)} custom-call(s32[1,4,2]{2,1,0:T(4,128)S(1)} %copy.18.lists_ref, s32[8]{0:T(128)S(1)} %stack.10.order_ref, f32[2048,128]{1,0:T(8,128)S(1)} %get-tuple-element.21.own_ref, bf16[256,128]{1,0:T(8,128)(2,1)S(1)} %collective-permute-done.8.r0, bf16[256,128]{1,0:T(8,128)(2,1)S(1)} %collective-permute-done.9.r1, ...), custom_call_target="tpu_custom_call" | custom-call | bytes 2097152 | tf_op jit(solution)/shard_map/pallas_call | solution.py:332
  48.6 0.6 %copy-done.9 = f32[128]{0:T(128)S(1)} copy-done((f32[128]{0:T(128)S(1)}, f32[128]{0:T(128)}, u32[]{:S(2)}) %copy-start.9) | copy-done | bytes 536
  49.2 6.0 %shard_map.170 = bf16[2048,128]{1,0:T(8,128)(2,1)} custom-call(s32[1]{0:T(128)} %bitcast.flip_ref, bf16[368,128]{1,0:T(8,128)(2,1)S(1)} %add_convert_fusion.mine_ref, bf16[368,128]{1,0:T(8,128)(2,1)S(1)} %collective-permute-done.3.other_ref, s32[512,3]{1,0:T(8,128)S(1)} %copy.20.wave_ref, f32[368,1]{1,0:T(8,128)S(1)} %copy-done.2, f32[48,16]{1,0:T(8,128)S(1)} %copy-done.8, ...), custom_call_target="tpu_custom_call" | custom-call | flops 385875968 | bytes 4194304 | tf_op jit(solution)/shard_map/pallas_call | solution.py:332
  (36 shorter events, 0.2 us)
Async XLA Ops:
  0.6 0.7 %copy-start.3 = (bf16[3,2048]{1,0:T(4,128)(2,1)S(1)}, bf16[3,2048]{1,0:T(4,128)(2,1)}, u32[]{:S(2)}) copy-start(bf16[3,2048]{1,0:T(4,128)(2,1)} %coords_ref.7) | copy-start | bytes 36868
  1.3 1.0 %copy-start = (bf16[2048,128]{1,0:T(8,128)(2,1)S(1)}, bf16[2048,128]{1,0:T(8,128)(2,1)}, u32[]{:S(2)}) copy-start(bf16[2048,128]{1,0:T(8,128)(2,1)} %feats_ref.7) | copy-start | bytes 1572868
  2.4 0.7 %copy-start.7 = (f32[48,16]{1,0:T(8,128)S(1)}, f32[48,16]{1,0:T(8,128)}, u32[]{:S(2)}) copy-start(f32[48,16]{1,0:T(8,128)} %constant.26.clone.table_ref) | copy-start | bytes 9220
  3.1 0.8 %copy-start.11 = (bf16[128,128]{1,0:T(8,128)(2,1)S(1)}, bf16[128,128]{1,0:T(8,128)(2,1)}, u32[]{:S(2)}) copy-start(bf16[128,128]{1,0:T(8,128)(2,1)} %w_ref.1) | copy-start | bytes 98308
  6.1 10.6 %copy-start.1 = (bf16[2048,128]{1,0:T(8,128)(2,1)S(1)}, bf16[2048,128]{1,0:T(8,128)(2,1)}, u32[]{:S(2)}) copy-start(bf16[2048,128]{1,0:T(8,128)(2,1)} %feats_ref.7) | copy-start | bytes 1572868
  6.1 1.5 %collective-permute-start = (bf16[368,128]{1,0:T(8,128)(2,1)S(1)}, bf16[368,128]{1,0:T(8,128)(2,1)S(1)}, u32[]{:S(2)}, u32[]{:S(2)}) collective-permute-start(bf16[368,128]{1,0:T(8,128)(2,1)S(1)} %get-tuple-element.15), channel_id=1, source_target_pairs={{0,1},{1,0},{2,3},{3,2},{4,5},{5,4},{6,7},{7,6},{8,9},{9,8},{10,11... | collective-permute-start | bytes 282632 | tf_op jit(solution)/shard_map/ppermute | solution.py:347
  7.6 6.0 %collective-permute-start.1 = (bf16[368,128]{1,0:T(8,128)(2,1)S(1)}, bf16[368,128]{1,0:T(8,128)(2,1)S(1)}, u32[]{:S(2)}, u32[]{:S(2)}) collective-permute-start(bf16[368,128]{1,0:T(8,128)(2,1)S(1)} %fusion), channel_id=1, source_target_pairs={{0,2},{1,3},{2,0},{3,1},{4,6},{5,7},{6,4},{7,5},{8,10},{9,11},{10,... | collective-permute-start | bytes 282632 | tf_op jit(solution)/shard_map/ppermute | solution.py:347
  13.7 2.8 %copy-start.14 = (s32[1,4,2]{1,2,0:T(2,128)S(1)}, s32[1,4,2]{1,2,0:T(2,128)}, u32[]{:S(2)}) copy-start(s32[1,4,2]{1,2,0:T(2,128)} %param.19) | copy-start | bytes 100
  13.7 9.1 %collective-permute-start.2 = (bf16[368,128]{1,0:T(8,128)(2,1)S(1)}, bf16[368,128]{1,0:T(8,128)(2,1)S(1)}, u32[]{:S(2)}, u32[]{:S(2)}) collective-permute-start(bf16[368,128]{1,0:T(8,128)(2,1)S(1)} %fusion.1), channel_id=1, source_target_pairs={{0,4},{1,5},{2,6},{3,7},{4,0},{5,1},{6,2},{7,3},{8,12},{9,13},{10,... | collective-permute-start | bytes 282632 | tf_op jit(solution)/shard_map/ppermute | solution.py:347
  17.3 5.6 %collective-permute-start.4 = (bf16[272,128]{1,0:T(8,128)(2,1)S(1)}, bf16[272,128]{1,0:T(8,128)(2,1)S(1)}, u32[]{:S(2)}, u32[]{:S(2)}) collective-permute-start(bf16[272,128]{1,0:T(8,128)(2,1)S(1)} %get-tuple-element.16), channel_id=1, source_target_pairs={{0,1},{1,0},{2,3},{3,2},{4,5},{5,4},{6,7},{7,6},{8,9},{9,8},{10,11... | collective-permute-start | bytes 208904 | tf_op jit(solution)/shard_map/ppermute | solution.py:347
  17.4 5.7 %collective-permute-start.5 = (bf16[272,128]{1,0:T(8,128)(2,1)S(1)}, bf16[272,128]{1,0:T(8,128)(2,1)S(1)}, u32[]{:S(2)}, u32[]{:S(2)}) collective-permute-start(bf16[272,128]{1,0:T(8,128)(2,1)S(1)} %get-tuple-element.17), channel_id=1, source_target_pairs={{0,7},{1,2},{2,1},{3,4},{4,3},{5,6},{6,5},{7,0},{8,15},{9,10},{10,... | collective-permute-start | bytes 208904 | tf_op jit(solution)/shard_map/ppermute | solution.py:347
  19.1 5.6 %collective-permute-start.6 = (bf16[272,128]{1,0:T(8,128)(2,1)S(1)}, bf16[272,128]{1,0:T(8,128)(2,1)S(1)}, u32[]{:S(2)}, u32[]{:S(2)}) collective-permute-start(bf16[272,128]{1,0:T(8,128)(2,1)S(1)} %get-tuple-element.18), channel_id=1, source_target_pairs={{0,8},{8,16},{16,24},{24,0},{1,9},{9,17},{17,25},{25,1},{2,10},{10... | collective-permute-start | bytes 208904 | tf_op jit(solution)/shard_map/ppermute | solution.py:347
  20.6 2.1 %copy-start.15 = (s32[1,96,2]{1,2,0:T(2,128)S(1)}, s32[1,96,2]{1,2,0:T(2,128)}, u32[]{:S(2)}) copy-start(s32[1,96,2]{1,2,0:T(2,128)} %param.20) | copy-start | bytes 2308
  20.6 5.1 %collective-permute-start.7 = (bf16[272,128]{1,0:T(8,128)(2,1)S(1)}, bf16[272,128]{1,0:T(8,128)(2,1)S(1)}, u32[]{:S(2)}, u32[]{:S(2)}) collective-permute-start(bf16[272,128]{1,0:T(8,128)(2,1)S(1)} %get-tuple-element.19), channel_id=1, source_target_pairs={{0,24},{8,0},{16,8},{24,16},{1,25},{9,1},{17,9},{25,17},{2,26},{10... | collective-permute-start | bytes 208904 | tf_op jit(solution)/shard_map/ppermute | solution.py:347
  22.8 2.9 %copy-start.12 = (bf16[128,128]{1,0:T(8,128)(2,1)S(1)}, bf16[128,128]{1,0:T(8,128)(2,1)}, u32[]{:S(2)}) copy-start(bf16[128,128]{1,0:T(8,128)(2,1)} %wa_ref.1) | copy-start | bytes 98308
  22.8 2.9 %copy-start.13 = (bf16[128,128]{1,0:T(8,128)(2,1)S(1)}, bf16[128,128]{1,0:T(8,128)(2,1)}, u32[]{:S(2)}) copy-start(bf16[128,128]{1,0:T(8,128)(2,1)} %wb_ref.1) | copy-start | bytes 98308
  22.9 25.7 %collective-permute-start.3 = (bf16[368,128]{1,0:T(8,128)(2,1)S(1)}, bf16[368,128]{1,0:T(8,128)(2,1)S(1)}, u32[]{:S(2)}, u32[]{:S(2)}) collective-permute-start(bf16[368,128]{1,0:T(8,128)(2,1)S(1)} %add_convert_fusion.mine_ref), channel_id=1, source_target_pairs={{0,1},{1,0},{2,3},{3,2},{4,5},{5,4},{6,7},{7,6},{8,9},{9,8},{10,11... | collective-permute-start | bytes 282632 | tf_op jit(solution)/shard_map/ppermute | solution.py:347
  25.7 1.0 %copy-start.10 = (bf16[2048,128]{1,0:T(8,128)(2,1)S(1)}, bf16[2048,128]{1,0:T(8,128)(2,1)}, u32[]{:S(2)}) copy-start(bf16[2048,128]{1,0:T(8,128)(2,1)} %cot_ref.1) | copy-start | bytes 1572868
  34.9 7.7 %collective-permute-start.8 = (bf16[256,128]{1,0:T(8,128)(2,1)}, bf16[256,128]{1,0:T(8,128)(2,1)S(1)}, u32[]{:S(2)}, u32[]{:S(2)}) collective-permute-start(bf16[256,128]{1,0:T(8,128)(2,1)} %get-tuple-element.22), channel_id=1, source_target_pairs={{0,1},{1,0},{2,3},{3,2},{4,5},{5,4},{6,7},{7,6},{8,9},{9,8},{10,11... | collective-permute-start | bytes 196616 | tf_op jit(solution)/shard_map/ppermute | solution.py:347
  35.7 6.9 %collective-permute-start.9 = (bf16[256,128]{1,0:T(8,128)(2,1)S(1)}, bf16[256,128]{1,0:T(8,128)(2,1)S(1)}, u32[]{:S(2)}, u32[]{:S(2)}) collective-permute-start(bf16[256,128]{1,0:T(8,128)(2,1)S(1)} %get-tuple-element.23), channel_id=1, source_target_pairs={{0,7},{1,2},{2,1},{3,4},{4,3},{5,6},{6,5},{7,0},{8,15},{9,10},{10,... | collective-permute-start | bytes 196616 | tf_op jit(solution)/shard_map/ppermute | solution.py:347
  35.7 8.4 %collective-permute-start.10 = (bf16[256,128]{1,0:T(8,128)(2,1)S(1)}, bf16[256,128]{1,0:T(8,128)(2,1)S(1)}, u32[]{:S(2)}, u32[]{:S(2)}) collective-permute-start(bf16[256,128]{1,0:T(8,128)(2,1)S(1)} %get-tuple-element.24), channel_id=1, source_target_pairs={{0,24},{8,0},{16,8},{24,16},{1,25},{9,1},{17,9},{25,17},{2,26},{10... | collective-permute-start | bytes 196616 | tf_op jit(solution)/shard_map/ppermute | solution.py:347
  41.7 5.2 %collective-permute-start.11 = (bf16[256,128]{1,0:T(8,128)(2,1)S(1)}, bf16[256,128]{1,0:T(8,128)(2,1)S(1)}, u32[]{:S(2)}, u32[]{:S(2)}) collective-permute-start(bf16[256,128]{1,0:T(8,128)(2,1)S(1)} %get-tuple-element.25), channel_id=1, source_target_pairs={{0,8},{8,16},{16,24},{24,0},{1,9},{9,17},{17,25},{25,1},{2,10},{10... | collective-permute-start | bytes 196616 | tf_op jit(solution)/shard_map/ppermute | solution.py:347
  46.9 1.7 %copy-start.2 = (f32[368,1]{1,0:T(8,128)S(1)}, f32[368,1]{1,0:T(8,128)}, u32[]{:S(2)}) copy-start(f32[368,1]{1,0:T(8,128)} %constant.27.clone.norm2_ref) | copy-start | bytes 4420
  46.9 1.7 %copy-start.4 = (bf16[128,256]{1,0:T(8,128)(2,1)S(1)}, bf16[128,256]{1,0:T(8,128)(2,1)}, u32[]{:S(2)}) copy-start(bf16[128,256]{1,0:T(8,128)(2,1)} %w_in_ref.1) | copy-start | bytes 196612
  46.9 1.7 %copy-start.5 = (bf16[256,128]{1,0:T(8,128)(2,1)S(1)}, bf16[256,128]{1,0:T(8,128)(2,1)}, u32[]{:S(2)}) copy-start(bf16[256,128]{1,0:T(8,128)(2,1)} %w_out_ref.1) | copy-start | bytes 196612
  46.9 1.7 %copy-start.6 = (bf16[128,128]{1,0:T(8,128)(2,1)S(1)}, bf16[128,128]{1,0:T(8,128)(2,1)}, u32[]{:S(2)}) copy-start(bf16[128,128]{1,0:T(8,128)(2,1)} %w_long_ref.1) | copy-start | bytes 98308
  46.9 1.7 %copy-start.8 = (f32[48,16]{1,0:T(8,128)S(1)}, f32[48,16]{1,0:T(8,128)}, u32[]{:S(2)}) copy-start(f32[48,16]{1,0:T(8,128)} %constant.26.clone.table_ref) | copy-start | bytes 9220
  48.5 0.7 %copy-start.9 = (f32[128]{0:T(128)S(1)}, f32[128]{0:T(128)}, u32[]{:S(2)}) copy-start(f32[128]{0:T(128)} %param.27) | copy-start | bytes 1540
where the time goes:
time: 55.8 us; the launch traced here: 55.2 us
  Pallas kernels  18.7 us (34%)
  starting transfers between devices  17.9 us (32%)
  waiting for transfers between devices  11 us (20%)
  local copies, waits for them, and re-layouts  6.05 us (11%)
  between operations  1.48 us (3%)
    pallas_call x5, Pallas kernels, call(): pl.pallas_call(kernel, out_shape=outs, in_specs=[pl.BlockSpec(memory_spac...  18.7 us
    ppermute x12, starting transfers between devices, exchange(): lax.ppermute(value, axis, [(i, partner(i) % length) for i in range(length)])  17.9 us
    ppermute x12, waiting for transfers between devices, exchange(): lax.ppermute(value, axis, [(i, partner(i) % length) for i in range(length)])  11 us
    unnamed x35, local copies, waits for them, and re-layouts  5.97 us
  transfers between devices with their start and end apart: 12, of which 7 were waited for; matrix products, arithmetic and copies ran while one was open for 2% of the time, Pallas kernels for 19%

commit v1 on v0

v1 whole, which is shorter than its diff:
```python
import functools

import jax
import jax.numpy as jnp
import numpy as np
from jax import lax
from jax.experimental import pallas as pl
from jax.experimental.pallas import tpu as pltpu
from jax.sharding import PartitionSpec as P

BLK = 128
HB = 2
WMAX = 4
COORD_ROWS = 16

RADIAL_A = 6.0
MSG_SCALE = 1.0 / 32.0
LOG2E = 1.4426950408889634

NT = (((1,), (1,)), ((), ()))
NN = (((1,), (0,)), ((), ()))

VMEM = pltpu.VMEM
SMEM = pltpu.SMEM
BF16 = jnp.bfloat16
F32 = jnp.float32


def dot(a, b, dims=NN):
    return lax.dot_general(a, b, dims, preferred_element_type=F32)


PAIRS = [(0, b) for b in range(1, WMAX + 1)] + [
    (a, b) for a in range(1, WMAX + 1) for b in range(-WMAX, WMAX + 1)
]
NPAIR = len(PAIRS)
BASE_ROWS = 48
HALF = BASE_ROWS + WMAX * 2 * NPAIR


def base_table():
    rows = np.zeros((BASE_ROWS, COORD_ROWS), np.float32)
    for r, (a, b) in enumerate(PAIRS):
        rows[r, 0], rows[r, 1] = a, b
    for m in range(WMAX + 1):
        rows[NPAIR + m, 2] = m
    return rows


def grid_norm2():
    base = (base_table() ** 2).sum(1)
    parts = [base]
    for m in range(1, WMAX + 1):
        parts += [base[:NPAIR] + m * m] * 2
    return np.concatenate(parts).reshape(HALF, 1).astype(np.float32)


def taylor(first, count):
    coef, out = 1.0, []
    for k in range(1, first + 1):
        coef /= k
    power = first
    for _ in range(count):
        out.append(coef)
        coef = -coef / ((power + 1) * (power + 2))
        power += 2
    return out


SIN_COEF = [c * np.pi ** (2 * i + 1) for i, c in enumerate(taylor(1, 7))]
COS_COEF = [c * np.pi ** (2 * i) for i, c in enumerate(taylor(0, 8))]


def horner(z, coefs):
    acc = jnp.full_like(z, coefs[-1])
    for c in coefs[-2::-1]:
        acc = acc * z + c
    return acc


def cos_sin_turns(turns):
    r = turns - jnp.round(turns)
    z = r * r
    s = r * horner(z, SIN_COEF)
    c = horner(z, COS_COEF)
    return 1.0 - 2.0 * (s * s), 2.0 * (s * c)


def trig_chunk(table, xyz16):
    c, s = cos_sin_turns(dot(table, xyz16))
    cos_parts, sin_parts = [c.astype(BF16)], [s.astype(BF16)]
    cp, sp = c[:NPAIR], s[:NPAIR]
    for m in range(1, WMAX + 1):
        cz, sz = c[NPAIR + m : NPAIR + m + 1], s[NPAIR + m : NPAIR + m + 1]
        cc, ss, sc, cs = cp * cz, sp * sz, sp * cz, cp * sz
        cos_parts.append(jnp.concatenate([cc - ss, cc + ss], axis=0).astype(BF16))
        sin_parts.append(jnp.concatenate([sc + cs, sc - cs], axis=0).astype(BF16))
    return jnp.concatenate(cos_parts + sin_parts, axis=0)


def coords16(xyz):
    return jnp.concatenate(
        [xyz.astype(F32), jnp.zeros((COORD_ROWS - 3, xyz.shape[1]), F32)], axis=0
    ).astype(BF16)


def split3(v):
    hi = v.astype(BF16).astype(F32)
    mid = (v - hi).astype(BF16).astype(F32)
    return hi, mid, (v - hi) - mid


def dist_rows(xyz, near):
    x = xyz.astype(F32)
    hi, mid, lo = split3(jnp.sum(x * x, axis=0, keepdims=True))
    one = jnp.ones_like(hi)
    rest = jnp.zeros((COORD_ROWS - 9, x.shape[1]), F32)
    if near:
        parts = [-2.0 * x, hi, mid, lo, one, one, one, rest]
    else:
        parts = [x, one, one, one, hi, mid, lo, rest]
    return jnp.concatenate(parts, axis=0)


def block(ref, b):
    return ref[b * BLK : (b + 1) * BLK, :]


def load_kernel(n_load, flip_ref, lists_hbm, *refs):
    sources, loaded = refs[:n_load], refs[n_load : 2 * n_load]
    outs, lists_ref, sems = refs[2 * n_load : 2 * n_load + 4], refs[-2], refs[-1]
    copies = [
        pltpu.make_async_copy(src, dst, sems.at[k])
        for k, (src, dst) in enumerate(zip((lists_hbm, *sources), (lists_ref, *loaded)))
    ]
    for copy in copies:
        copy.start()
    for copy in copies[:3]:
        copy.wait()
    feats_ref, coords_ref = loaded[0], loaded[1]
    odd = flip_ref[0]
    for slot, direction in enumerate((odd, 1 - odd, 2, 3)):
        pieces = []
        for h in range(HB):
            b = lists_ref[0, h, direction]
            start = pl.multiple_of(b * BLK, BLK)
            outs[slot][pl.ds(h * BLK, BLK), :] = feats_ref[pl.ds(start, BLK), :]
            pieces.append(coords_ref[:, pl.ds(start, BLK)].astype(F32))
            pieces.append(jnp.zeros((COORD_ROWS // HB - 3, BLK), F32))
        outs[slot][pl.ds(HB * BLK, COORD_ROWS), :] = jnp.concatenate(pieces, axis=0).astype(BF16)
    for copy in copies[3:]:
        copy.wait()


def struct_kernel(
    chunk, flip_ref, feats_ref, coords_ref, w_ref, table_ref, first_ref, keep_ref, send_ref, trig_ref, total_ref
):
    atoms = feats_ref.shape[0]
    table = table_ref[...].astype(BF16)
    w = w_ref[...]
    for first in range(0, atoms, chunk):
        charges = dot(feats_ref[pl.ds(first, chunk), :], w).astype(BF16)
        trig = trig_chunk(table, coords16(coords_ref[:, pl.ds(first, chunk)]))
        trig_ref[:, pl.ds(first, chunk)] = trig
        part = dot(trig, charges)
        if first == 0:
            total_ref[...] = part
        else:
            total_ref[...] += part
    mine = pl.multiple_of(flip_ref[0] * HALF, 8)
    other = pl.multiple_of((1 - flip_ref[0]) * HALF, 8)
    keep_ref[...] = total_ref[pl.ds(mine, HALF), :]
    head = first_ref.shape[0]
    send_ref[0:head, :] = first_ref[...]
    send_ref[head:, :] = total_ref[pl.ds(other, HALF), :].astype(BF16)


def source_block(j, w_cat, feats, far, proj_ref, far_ref):
    both = dot(w_cat, feats, NT).astype(BF16)
    proj_ref[j, :, 0:BLK] = both[:BLK]
    proj_ref[j, :, BLK:] = both[BLK:]
    far_ref[j] = far.T.astype(BF16)


def both_transposed(wa_ref, wb_ref):
    return jnp.concatenate([wa_ref[...].astype(F32).T, wb_ref[...].astype(F32).T], axis=0).astype(BF16)


def local_kernel(
    feats_ref, coords_ref, cot_ref, wa_ref, wb_ref, after_ref, proj_ref, far_ref, near_ref, cotp_ref
):
    nblk = feats_ref.shape[0] // BLK
    w_cat = both_transposed(wa_ref, wb_ref)
    w_side = jnp.concatenate([wa_ref[...], wb_ref[...]], axis=0)
    near = dist_rows(coords_ref[...], True).astype(BF16)
    far = dist_rows(coords_ref[...], False)
    for b in range(nblk):
        at = slice(b * BLK, (b + 1) * BLK)
        source_block(b, w_cat, block(feats_ref, b), far[:, at], proj_ref, far_ref)
        near_ref[b] = near[:, at]
        both = dot(block(cot_ref, b), w_side, NT).astype(BF16)
        cotp_ref[b, 0:BLK, :] = both[:, :BLK]
        cotp_ref[b, BLK:, :] = both[:, BLK:]


def tile_range(
    unroll, first, last, count, tiles_ref, proj_ref, far_ref, near_ref, cotp_ref, msg_ref, grad_ref
):
    spare_i, spare_j = msg_ref.shape[0] - 1, grad_ref.shape[0] - 1
    slots = tiles_ref.shape[2]

    @pl.loop(first, last)
    def _(step):
        idx = []
        for u in range(unroll):
            t = step * unroll + u
            at = jnp.minimum(t, slots - 1)
            i, j, live = tiles_ref[0, 0, at], tiles_ref[0, 1, at], t < count
            idx.append((i, j, jnp.where(live, i, spare_i), jnp.where(live, j, spare_j)))
        kers = []
        for i, j, _, _ in idx:
            d = dot(far_ref[j], near_ref[i])
            a = jnp.exp2(d * (-RADIAL_A * LOG2E))
            a2 = a * a
            b = (a2 * a2) * a
            kers.append((a.astype(BF16), b.astype(BF16)))
        for (i, j, to_i, to_j), (ka, kb) in zip(idx, kers):
            msg_ref[to_i] += dot(proj_ref[j], jnp.concatenate([ka, kb], axis=0))
            grad_ref[to_j] += dot(jnp.concatenate([ka, kb], axis=1), cotp_ref[i])


def groups(count, unroll):
    return (count + unroll - 1) // unroll


def tiles_first_kernel(
    unroll,
    flip_ref,
    tiles_ref,
    count_ref,
    got0,
    got1,
    got2,
    got3,
    wa_ref,
    wb_ref,
    near_ref,
    cotp_ref,
    proj_in,
    far_in,
    after_ref,
    proj_ref,
    far_ref,
    msg_ref,
    grad_ref,
):
    nblk = near_ref.shape[0]
    w_cat = both_transposed(wa_ref, wb_ref)
    odd = flip_ref[0]
    for got, place in zip((got0, got1, got2, got3), (1 - odd, odd, 2, 3)):
        tail = got[HB * BLK : HB * BLK + COORD_ROWS, :].astype(F32)
        for h in range(HB):
            at = h * (COORD_ROWS // HB)
            far = dist_rows(tail[at : at + 3], False)
            source_block(nblk + place * HB + h, w_cat, block(got, h), far, proj_ref, far_ref)
    msg_ref[...] = jnp.zeros_like(msg_ref)
    grad_ref[...] = jnp.zeros_like(grad_ref)
    count = count_ref[0]
    last = groups(count, unroll) // 2
    tile_range(unroll, 0, last, count, tiles_ref, proj_ref, far_ref, near_ref, cotp_ref, msg_ref, grad_ref)


def tiles_second_kernel(
    unroll,
    flip_ref,
    tiles_ref,
    count_ref,
    proj_ref,
    far_ref,
    near_ref,
    cotp_ref,
    msg_in,
    grad_in,
    after_ref,
    msg_ref,
    grad_ref,
    held0,
    held1,
    held2,
    held3,
):
    nblk = near_ref.shape[0]
    count = count_ref[0]
    last = groups(count, unroll)
    tile_range(unroll, last // 2, last, count, tiles_ref, proj_ref, far_ref, near_ref, cotp_ref, msg_ref, grad_ref)
    odd = flip_ref[0]
    for held, place in zip((held0, held1, held2, held3), (1 - odd, odd, 2, 3)):
        for h in range(HB):
            held[h * BLK : (h + 1) * BLK, :] = (grad_ref[nblk + place * HB + h] * MSG_SCALE).astype(BF16)


def prepare_kernel(
    group_atoms,
    wave_ref,
    norm2_ref,
    w_long_ref,
    gain_ref,
    w_in_ref,
    w_out_ref,
    feats_ref,
    after_ref,
    strength_ref,
    w_long_t_ref,
    w_in_t_ref,
    w_out_t_ref,
    gain_t_ref,
    feats_t_ref,
):
    n = wave_ref[...].astype(F32)
    n0, n1, n2 = n[0:1], n[1:2], n[2:3]
    lead = jnp.where(n0 != 0.0, n0, jnp.where(n1 != 0.0, n1, n2))
    sign = jnp.where(lead < 0.0, -1.0, 1.0)
    n0, n1, n2 = n0 * sign, n1 * sign, n2 * sign
    pair = jnp.where(n0 == 0.0, n1 - 1.0, n0 * (2 * WMAX + 1) + n1 + (2.0 * WMAX - (2 * WMAX + 1)))
    shift = jnp.where(
        n2 == 0.0,
        0.0,
        BASE_ROWS
        + (jnp.abs(n2) - 1.0) * (2 * NPAIR)
        + jnp.where(n2 < 0.0, float(NPAIR), 0.0),
    )
    row = jnp.where((n0 == 0.0) & (n1 == 0.0), NPAIR + n2, pair + shift)
    same = lax.broadcasted_iota(jnp.int32, (HALF, row.shape[1]), 0) == row.astype(jnp.int32)
    times = jnp.sum(same.astype(F32), axis=1, keepdims=True)
    norm2 = norm2_ref[...]
    strength = times * (jnp.exp(-norm2 / 16.0) / (1.0 + norm2) * float(group_atoms) ** (-0.5))
    strength_ref[...] = jnp.broadcast_to(strength, strength_ref.shape)
    w_long_t_ref[...] = w_long_ref[...].astype(F32).T.astype(BF16)
    w_in_t_ref[...] = w_in_ref[...].astype(F32).T.astype(BF16)
    w_out_t_ref[...] = w_out_ref[...].astype(F32).T.astype(BF16)
    gain_t_ref[...] = jnp.broadcast_to(gain_ref[...], gain_t_ref.shape).T
    for b in range(feats_ref.shape[0] // BLK):
        feats_t_ref[:, b * BLK : (b + 1) * BLK] = block(feats_ref, b).astype(F32).T.astype(BF16)


def update_kernel(
    chunk,
    flip_ref,
    mine_ref,
    other_ref,
    strength_ref,
    trig_ref,
    feats_t_ref,
    msg_ref,
    w_long_t_ref,
    gain_t_ref,
    w_in_t_ref,
    w_out_t_ref,
    out_ref,
    done_ref,
):
    done_ref[...] = jnp.zeros_like(done_ref)
    atoms = feats_t_ref.shape[1]
    mine = flip_ref[0] == 0
    a = (strength_ref[...] * mine_ref[...].astype(F32)).astype(BF16)
    b = (strength_ref[...] * other_ref[HB * BLK :, :].astype(F32)).astype(BF16)
    weighted = jnp.concatenate([jnp.where(mine, a, b), jnp.where(mine, b, a)], axis=0)
    mix_w = dot(w_long_t_ref[...], weighted, NT).astype(BF16)
    gain = jnp.concatenate([gain_t_ref[...]] * (chunk // BLK), axis=1)
    w_in_t = w_in_t_ref[...]
    w_out_t = w_out_t_ref[...]
    for first in range(0, atoms, chunk):
        at = slice(first, first + chunk)
        msg = jnp.concatenate([msg_ref[(first // BLK) + i] for i in range(chunk // BLK)], axis=1)
        mixed = dot(mix_w, trig_ref[:, at]) + msg * MSG_SCALE + feats_t_ref[:, at].astype(F32)
        scale = lax.rsqrt(jnp.mean(mixed * mixed, axis=0, keepdims=True) + 1e-06)
        normed = (mixed * scale * gain).astype(BF16)
        pre = dot(w_in_t, normed)
        hidden = (pre / (1.0 + jnp.exp(-pre))).astype(BF16)
        out = mixed + dot(w_out_t, hidden)
        out_ref[at, :] = out.T.astype(BF16)


def adjoint_kernel(lists_ref, flip_ref, grad_ref, r0, r1, r2, r3, after_ref, out_ref):
    nblk = out_ref.shape[0] // BLK
    odd = flip_ref[0]
    for b in range(nblk):
        out_ref[b * BLK : (b + 1) * BLK, :] = grad_ref[b] * MSG_SCALE
    for ref, direction in zip((r0, r1, r2, r3), (odd, 1 - odd, 2, 3)):
        for h in range(HB):
            b = lists_ref[0, h, direction]
            at = pl.ds(pl.multiple_of(b * BLK, BLK), BLK)
            out_ref[at, :] += ref[h * BLK : (h + 1) * BLK, :].astype(F32)


def call(kernel, outs, args, specs, scratch=(), us=1.0, aliases=None):
    single = not isinstance(outs, (list, tuple))
    return pl.pallas_call(
        kernel,
        out_shape=outs,
        in_specs=[pl.BlockSpec(memory_space=s) for s in specs],
        out_specs=pl.BlockSpec(memory_space=VMEM)
        if single
        else [pl.BlockSpec(memory_space=VMEM) for _ in outs],
        scratch_shapes=list(scratch),
        input_output_aliases=aliases or {},
        compiler_params=pltpu.CompilerParams(vmem_limit_bytes=24 * 1024 * 1024),
        cost_estimate=pl.CostEstimate(
            flops=int(us * 1.1e9), bytes_accessed=int(us * 3.4e6), transcendentals=0
        ),
    )(*args)


def exchange(value, axis, partner):
    length = lax.axis_size(axis)
    return lax.ppermute(value, axis, [(i, partner(i) % length) for i in range(length)])


def body(
    feats,
    coords,
    msg_cot,
    send_list,
    tiles,
    tile_count,
    wavevec,
    w_rad_a,
    w_rad_b,
    w_charge,
    w_long,
    norm_gain,
    w_in,
    w_out,
):
    atoms, width = feats.shape
    nblk = atoms // BLK
    extent = nblk + 4 * HB
    hidden = w_in.shape[1]
    domains = lax.axis_size("dom")
    flip = (lax.axis_index("dom") % 2).astype(jnp.int32).reshape(1)
    sds = jax.ShapeDtypeStruct
    like = lambda x: sds(x.shape, x.dtype)
    unroll = 16

    near_pair = lambda i: i ^ 1
    far_pair = lambda i: i + (1 if i % 2 else -1)
    up = lambda i: i + 1
    down = lambda i: i - 1
    lists = jnp.swapaxes(send_list, 1, 2)
    tile_rows = jnp.swapaxes(tiles, 1, 2)
    table = jnp.asarray(base_table())
    norm2 = jnp.asarray(grid_norm2())

    loads = tuple(
        pltpu.with_memory_space_constraint(x, pltpu.HBM)
        for x in (feats, coords, msg_cot, table, w_charge)
    )
    loaded = call(
        functools.partial(load_kernel, len(loads)),
        [like(x) for x in loads] + [sds((HB * BLK + COORD_ROWS, width), BF16)] * 4,
        (flip, pltpu.with_memory_space_constraint(lists, pltpu.HBM), *loads),
        (SMEM,) + (pltpu.HBM,) * (1 + len(loads)),
        scratch=[SMEM(lists.shape, lists.dtype), pltpu.SemaphoreType.DMA((1 + len(loads),))],
        us=1.2,
    )
    feats, coords, msg_cot, table, w_charge = loaded[: len(loads)]
    sent = loaded[len(loads) :]
    got1 = exchange(sent[1], "dom", far_pair)
    got2 = exchange(sent[2], "group", up)
    got3 = exchange(sent[3], "group", down)

    keep, send, trig = call(
        functools.partial(struct_kernel, 256),
        [
            sds((HALF, width), F32),
            sds((HB * BLK + COORD_ROWS + HALF, width), BF16),
            sds((2 * HALF, atoms), BF16),
        ],
        (flip, feats, coords, w_charge, table, sent[0]),
        (SMEM,) + (VMEM,) * 5,
        scratch=[VMEM((2 * HALF, width), F32)],
        us=2.3,
    )
    got0 = exchange(send, "dom", near_pair)
    proj, far, near, cotp = call(
        local_kernel,
        [
            sds((extent, width, 2 * BLK), BF16),
            sds((extent, BLK, COORD_ROWS), BF16),
            sds((nblk, COORD_ROWS, BLK), BF16),
            sds((nblk, 2 * BLK, width), BF16),
        ],
        (feats, coords, msg_cot, w_rad_a, w_rad_b, send),
        (VMEM,) * 5 + (pl.ANY,),
        us=1.0,
    )
    total = keep + got0[HB * BLK + COORD_ROWS :].astype(F32)
    sums = [total.astype(BF16)]
    step = 2
    while step < domains:
        total = total + exchange(sums[-1], "dom", lambda i: i ^ step).astype(F32)
        sums.append(total.astype(BF16))
        step *= 2

    proj, far, msg, grad = call(
        functools.partial(tiles_first_kernel, unroll),
        [like(proj), like(far), sds((nblk + 1, width, BLK), F32), sds((extent + 1, BLK, width), F32)],
        (flip, tile_rows, tile_count, got0, got1, got2, got3, w_rad_a, w_rad_b, near, cotp, proj, far, sums[0]),
        (SMEM,) * 3 + (VMEM,) * 10 + (pl.ANY,),
        aliases={11: 0, 12: 1},
        us=3.5,
    )
    msg, grad, *held = call(
        functools.partial(tiles_second_kernel, unroll),
        [like(msg), like(grad)] + [sds((HB * BLK, width), BF16)] * 4,
        (flip, tile_rows, tile_count, proj, far, near, cotp, msg, grad, sums[min(1, len(sums) - 1)]),
        (SMEM,) * 3 + (VMEM,) * 6 + (pl.ANY,),
        aliases={7: 0, 8: 1},
        us=3.5,
    )
    back1 = exchange(held[1], "dom", far_pair)
    back2 = exchange(held[2], "group", down)
    back3 = exchange(held[3], "group", up)
    total = sums[-1]
    last = jnp.concatenate([held[0], total], axis=0)
    back0 = exchange(last, "dom", near_pair)

    strength, w_long_t, w_in_t, w_out_t, gain_t, feats_t = call(
        functools.partial(prepare_kernel, atoms * domains),
        [
            sds((HALF, width), F32),
            sds((width, width), BF16),
            sds((hidden, width), BF16),
            sds((width, hidden), BF16),
            sds((width, BLK), F32),
            sds((width, atoms), BF16),
        ],
        (wavevec.T, norm2, w_long, norm_gain.reshape(1, width), w_in, w_out, feats, last),
        (VMEM,) * 7 + (pl.ANY,),
        us=0.5,
    )
    new_feats, done = call(
        functools.partial(update_kernel, 256),
        [sds((atoms, width), BF16), sds((8, BLK), F32)],
        (flip, total, back0, strength, trig, feats_t, msg, w_long_t, gain_t, w_in_t, w_out_t),
        (SMEM,) + (VMEM,) * 10,
        us=3.4,
    )
    adjoint = call(
        adjoint_kernel,
        sds((atoms, width), F32),
        (lists, flip, grad, back0, back1, back2, back3, done),
        (SMEM, SMEM) + (VMEM,) * 5 + (pl.ANY,),
        us=1.6,
    )
    return (new_feats, adjoint)


def solution(mesh):
    split = ("group", "dom")
    return jax.shard_map(
        body,
        mesh=mesh,
        in_specs=(
            P(split, None),
            P(None, split),
            P(split, None),
            P(split, None, None),
            P(split, None, None),
            P(split),
            P(),
            P(),
            P(),
            P(),
            P(),
            P(),
            P(),
            P(),
        ),
        out_specs=(P(split, None), P(split, None)),
        check_vma=False,
    )
```

time: 55.8 us -> 34.9 us (0.63)
  local copies, waits for them, and re-layouts: 6.05 us -> 0.05 us
  starting transfers between devices: 17.9 us -> 12 us
  Pallas kernels: 18.7 us -> 13.4 us
  waiting for transfers between devices: 11 us -> 7.6 us
    unnamed x35 -> x20, local copies, waits for them, and re-layouts: 5.97 us -> 0.05 us
    ppermute x12 -> x10, starting transfers between devices: 17.9 us -> 12 us  [exchange(): lax.ppermute(value, axis, [(i, partner(i) % length) for i in range(length)])]
    pallas_call x5 -> x8, Pallas kernels: 18.7 us -> 13.4 us  [call(): pl.pallas_call(kernel, out_shape=outs, in_specs=[pl.BlockSpec(memory_spac...]
    ppermute x12 -> x10, waiting for transfers between devices: 11 us -> 7.6 us  [exchange(): lax.ppermute(value, axis, [(i, partner(i) % length) for i in range(length)])]
  transfers between devices with their start and end apart: 12 -> 10, of which waited for: 7 -> 5; matrix products, arithmetic and copies ran while one was open for 2% -> 0% of each run, Pallas kernels for 19% -> 23%
where the time goes in v1:
time: 34.9 us; the launch traced here: 34.7 us
  Pallas kernels  13.4 us (38%)
  starting transfers between devices  12 us (34%)
  waiting for transfers between devices  7.6 us (22%)
  between operations  1.49 us (4%)
    pallas_call x8, Pallas kernels, call(): pl.pallas_call(kernel, out_shape=outs, in_specs=[pl.BlockSpec(memory_spac...  13.4 us
    ppermute x10, starting transfers between devices, exchange(): lax.ppermute(value, axis, [(i, partner(i) % length) for i in range(length)])  12 us
    ppermute x10, waiting for transfers between devices, exchange(): lax.ppermute(value, axis, [(i, partner(i) % length) for i in range(length)])  7.6 us
  transfers between devices with their start and end apart: 10, of which 5 were waited for; matrix products, arithmetic and copies ran while one was open for 0% of the time, Pallas kernels for 23%

profile of v1, /device:TPU:0, one launch (start us, length us, event | category | flops | bytes accessed | tf_op | source)
XLA Modules:
  0.0 34.7 jit_solution(2373393606763007947)
XLA Ops:
  0.6 1.3 %shard_map.167 = (bf16[2048,128]{1,0:T(8,128)(2,1)S(1)}, bf16[3,2048]{1,0:T(4,128)(2,1)S(1)}, bf16[2048,128]{1,0:T(8,128)(2,1)S(1)}, f32[48,16]{1,0:T(8,128)S(1)...) custom-call(s32[1]{0:T(128)} %bitcast.flip_ref, ...), custom_call_target="tpu_custom_call" | custom-call | flops 1320000000 | bytes 4080000 | tf_op jit(solution)/shard_map/pallas_call | solution.py:398
  1.9 0.0 copy-start.2
  1.9 0.0 copy-start.3
  1.9 2.3 %shard_map.168 = (f32[368,128]{1,0:T(8,128)S(1)}, bf16[640,128]{1,0:T(8,128)(2,1)S(1)}, bf16[736,2048]{1,0:T(8,128)(2,1)S(1)}) custom-call(s32[1]{0:T(128)} %bitcast.flip_ref, bf16[2048,128]{1,0:T(8,128)(2,1)S(1)} %get-tuple-element.36.feats_ref, bf16[3,2048]{1,0:T(4,128)(2,1)S(1)} %get-tuple-element.37.coords_ref, ...), custom_call_target="tpu_custom_call" | custom-call | flops 2529999872 | bytes 7819999 | tf_op jit(solution)/shard_map/pallas_call | solution.py:398
  4.3 0.5 %collective-permute-start = (bf16[640,128]{1,0:T(8,128)(2,1)S(1)}, bf16[640,128]{1,0:T(8,128)(2,1)S(1)}, u32[]{:S(2)}, u32[]{:S(2)}) collective-permute-start(bf16[640,128]{1,0:T(8,128)(2,1)S(1)} %get-tuple-element.42.after_ref), channel_id=1, source_target_pairs={{0,1},{1,0},{2,3},{3,2},{4,5},{5,4},{6,7},{7,6},{8,9},{9,8},{10,11... | collective-permute-start | bytes 491528 | tf_op jit(solution)/shard_map/ppermute | solution.py:416
  4.8 4.7 %collective-permute-start.3 = (bf16[272,128]{1,0:T(8,128)(2,1)S(1)}, bf16[272,128]{1,0:T(8,128)(2,1)S(1)}, u32[]{:S(2)}, u32[]{:S(2)}) collective-permute-start(bf16[272,128]{1,0:T(8,128)(2,1)S(1)} %get-tuple-element.43), channel_id=1, source_target_pairs={{0,7},{1,2},{2,1},{3,4},{4,3},{5,6},{6,5},{7,0},{8,15},{9,10},{10,... | collective-permute-start | bytes 208904 | tf_op jit(solution)/shard_map/ppermute | solution.py:416
  9.5 1.5 %collective-permute-start.4 = (bf16[272,128]{1,0:T(8,128)(2,1)S(1)}, bf16[272,128]{1,0:T(8,128)(2,1)S(1)}, u32[]{:S(2)}, u32[]{:S(2)}) collective-permute-start(bf16[272,128]{1,0:T(8,128)(2,1)S(1)} %get-tuple-element.44), channel_id=1, source_target_pairs={{0,8},{8,16},{16,24},{24,0},{1,9},{9,17},{17,25},{25,1},{2,10},{10... | collective-permute-start | bytes 208904 | tf_op jit(solution)/shard_map/ppermute | solution.py:416
  11.0 1.4 %collective-permute-start.5 = (bf16[272,128]{1,0:T(8,128)(2,1)S(1)}, bf16[272,128]{1,0:T(8,128)(2,1)S(1)}, u32[]{:S(2)}, u32[]{:S(2)}) collective-permute-start(bf16[272,128]{1,0:T(8,128)(2,1)S(1)} %get-tuple-element.45), channel_id=1, source_target_pairs={{0,24},{8,0},{16,8},{24,16},{1,25},{9,1},{17,9},{25,17},{2,26},{10... | collective-permute-start | bytes 208904 | tf_op jit(solution)/shard_map/ppermute | solution.py:416
  13.1 0.0 copy-start.6
  13.1 0.8 %shard_map.169 = (bf16[24,128,256]{2,1,0:T(8,128)(2,1)S(1)}, bf16[24,128,16]{2,1,0:T(8,128)(2,1)S(1)}, bf16[16,16,128]{2,1,0:T(8,128)(2,1)S(1)}, bf16[16,256,128]{2,1,0:T(8,128)(2,1)S(1)}) custom-call(bf16[2048,128]{1,0:T(8,128)(2,1)S(1)} %get-tuple-element.36.feats_ref, bf16[3,2048]{1,0:T(4,128)(2,1)S(1)} %get-tuple-element.37.coords_ref, ...), custom_call_target="tpu_custom_call" | custom-call | flops 1100000000 | bytes 3400000 | tf_op jit(solution)/shard_map/pallas_call | solution.py:398
  13.9 0.0 collective-permute-done.got0
  13.9 0.1 collective-permute-start.1
  14.0 0.0 collective-permute-done.3.got1
  14.0 0.7 %collective-permute-done.4.got2 = bf16[272,128]{1,0:T(8,128)(2,1)S(1)} collective-permute-done((bf16[272,128]{1,0:T(8,128)(2,1)S(1)}, bf16[272,128]{1,0:T(8,128)(2,1)S(1)}, u32[]{:S(2)}, u32[]{:S(2)}) %collective-permute-start.4) | collective-permute-done | bytes 69664 | tf_op jit(solution)/shard_map/ppermute | solution.py:416
  14.7 0.8 %collective-permute-done.5.got3 = bf16[272,128]{1,0:T(8,128)(2,1)S(1)} collective-permute-done((bf16[272,128]{1,0:T(8,128)(2,1)S(1)}, bf16[272,128]{1,0:T(8,128)(2,1)S(1)}, u32[]{:S(2)}, u32[]{:S(2)}) %collective-permute-start.5) | collective-permute-done | bytes 69664 | tf_op jit(solution)/shard_map/ppermute | solution.py:416
  15.5 1.9 %shard_map.170 = (bf16[24,128,256]{2,1,0:T(8,128)(2,1)S(1)}, bf16[24,128,16]{2,1,0:T(8,128)(2,1)S(1)}, f32[17,128,128]{2,1,0:T(8,128)S(1)}, f32[25,128,128]{2,1,0:T(8,128)S(1)}) custom-call(s32[1]{0:T(128)} %bitcast.flip_ref, s32[1,2,96]{2,1,0:T(2,128)S(1)} %bitcast.6, s32[1]{0:T(128)S(6)} %copy.26.count_ref, ...), custom_call_target="tpu_custom_call", output_to_operand_aliasing={{0}: (11, {}), {1}: (12, {})} | custom-call | flops 3849999872 | bytes 11900000 | tf_op jit(solution)/shard_map/pallas_call | solution.py:398
  17.5 1.1 %collective-permute-done.1 = bf16[368,128]{1,0:T(8,128)(2,1)S(1)} collective-permute-done((bf16[368,128]{1,0:T(8,128)(2,1)S(1)}, bf16[368,128]{1,0:T(8,128)(2,1)S(1)}, u32[]{:S(2)}, u32[]{:S(2)}) %collective-permute-start.1) | collective-permute-done | bytes 94240 | tf_op jit(solution)/shard_map/ppermute | solution.py:416
  18.6 0.2 collective-permute-start.2
  18.8 0.0 copy-start.8
  18.8 0.0 copy-start.9
  18.9 1.5 %shard_map.171 = (f32[17,128,128]{2,1,0:T(8,128)S(1)}, f32[25,128,128]{2,1,0:T(8,128)S(1)}, bf16[256,128]{1,0:T(8,128)(2,1)S(1)}, bf16[256,128]{1,0:T(8,128)(2,1...) custom-call(s32[1]{0:T(128)} %bitcast.flip_ref, ...), custom_call_target="tpu_custom_call", output_to_operand_aliasing={{0}: (7, {}), {1}: (8, {})} | custom-call | flops 3849999872 | bytes 11900000 | tf_op jit(solution)/shard_map/pallas_call | solution.py:398
  20.4 4.2 %collective-permute-done.2 = bf16[368,128]{1,0:T(8,128)(2,1)S(1)} collective-permute-done((bf16[368,128]{1,0:T(8,128)(2,1)S(1)}, bf16[368,128]{1,0:T(8,128)(2,1)S(1)}, u32[]{:S(2)}, u32[]{:S(2)}) %collective-permute-start.2) | collective-permute-done | bytes 94240 | tf_op jit(solution)/shard_map/ppermute | solution.py:416
  24.6 0.1 add_convert_fusion.mine_ref
  24.7 0.1 collective-permute-start.6
  24.8 1.5 %collective-permute-start.7 = (bf16[256,128]{1,0:T(8,128)(2,1)S(1)}, bf16[256,128]{1,0:T(8,128)(2,1)S(1)}, u32[]{:S(2)}, u32[]{:S(2)}) collective-permute-start(bf16[256,128]{1,0:T(8,128)(2,1)S(1)} %get-tuple-element.66), channel_id=1, source_target_pairs={{0,7},{1,2},{2,1},{3,4},{4,3},{5,6},{6,5},{7,0},{8,15},{9,10},{10,... | collective-permute-start | bytes 196616 | tf_op jit(solution)/shard_map/ppermute | solution.py:416
  26.3 1.6 %collective-permute-start.8 = (bf16[256,128]{1,0:T(8,128)(2,1)S(1)}, bf16[256,128]{1,0:T(8,128)(2,1)S(1)}, u32[]{:S(2)}, u32[]{:S(2)}) collective-permute-start(bf16[256,128]{1,0:T(8,128)(2,1)S(1)} %get-tuple-element.67), channel_id=1, source_target_pairs={{0,24},{8,0},{16,8},{24,16},{1,25},{9,1},{17,9},{25,17},{2,26},{10... | collective-permute-start | bytes 196616 | tf_op jit(solution)/shard_map/ppermute | solution.py:416
  27.9 0.4 %collective-permute-start.9 = (bf16[256,128]{1,0:T(8,128)(2,1)S(1)}, bf16[256,128]{1,0:T(8,128)(2,1)S(1)}, u32[]{:S(2)}, u32[]{:S(2)}) collective-permute-start(bf16[256,128]{1,0:T(8,128)(2,1)S(1)} %get-tuple-element.68), channel_id=1, source_target_pairs={{0,8},{8,16},{16,24},{24,0},{1,9},{9,17},{17,25},{25,1},{2,10},{10... | collective-permute-start | bytes 196616 | tf_op jit(solution)/shard_map/ppermute | solution.py:416
  28.3 0.5 %shard_map.172 = (f32[368,128]{1,0:T(8,128)S(1)}, bf16[128,128]{1,0:T(8,128)(2,1)S(1)}, bf16[256,128]{1,0:T(8,128)(2,1)S(1)}, bf16[128,256]{1,0:T(8,128)(2,1)S(1...) custom-call(s32[3,512]{1,0:T(4,128)S(1)} %bitcast.5, f32[368,1]{1,0:T(8,128)S(1)} %copy-done.9, ...), custom_call_target="tpu_custom_call" | custom-call | flops 550000000 | bytes 1700000 | tf_op jit(solution)/shard_map/pallas_call | solution.py:398
  28.8 0.0 copy-start.7
  28.8 3.5 %shard_map.173 = (bf16[2048,128]{1,0:T(8,128)(2,1)}, f32[8,128]{1,0:T(8,128)S(1)}) custom-call(s32[1]{0:T(128)} %bitcast.flip_ref, bf16[368,128]{1,0:T(8,128)(2,1)S(1)} %add_convert_fusion.mine_ref, bf16[624,128]{1,0:T(8,128)(2,1)S(1)} %collective-permute-done.6.other_ref.r0, f32[368,128]{1,0:T(8,128)S(1)} %get-tuple-element.56.strength_ref, ...), custom_call_target="tpu_custom_call" | custom-call | flops 3740000000 | bytes 11560000 | tf_op jit(solution)/shard_map/pallas_call | solution.py:398
  32.3 0.8 %collective-permute-done.9.r3 = bf16[256,128]{1,0:T(8,128)(2,1)S(1)} collective-permute-done((bf16[256,128]{1,0:T(8,128)(2,1)S(1)}, bf16[256,128]{1,0:T(8,128)(2,1)S(1)}, u32[]{:S(2)}, u32[]{:S(2)}) %collective-permute-start.9) | collective-permute-done | bytes 65568 | tf_op jit(solution)/shard_map/ppermute | solution.py:416
  33.1 1.6 %shard_map.174 = f32[2048,128]{1,0:T(8,128)} custom-call(s32[1,2,4]{2,1,0:T(2,128)S(1)} %bitcast.9, s32[1]{0:T(128)} %bitcast.flip_ref, f32[25,128,128]{2,1,0:T(8,128)S(1)} %get-tuple-element.65.grad_ref, bf16[624,128]{1,0:T(8,128)(2,1)S(1)} %collective-permute-done.6.other_ref.r0, bf16[256,128]{1,0:T(8,128)(2,1)S(1)} %collective-permute-done.7.r1, ...), custom_call_target="tpu_custom_call" | custom-call | flops 1760000000 | bytes 5440000 | tf_op jit(solution)/shard_map/pallas_call | solution.py:398
  (20 shorter events, 0.1 us)
Async XLA Ops:
  1.9 11.2 %copy-start.2 = (bf16[128,128]{1,0:T(8,128)(2,1)S(1)}, bf16[128,128]{1,0:T(8,128)(2,1)}, u32[]{:S(2)}) copy-start(bf16[128,128]{1,0:T(8,128)(2,1)} %wa_ref.3) | copy-start | bytes 98308
  1.9 11.2 %copy-start.3 = (bf16[128,128]{1,0:T(8,128)(2,1)S(1)}, bf16[128,128]{1,0:T(8,128)(2,1)}, u32[]{:S(2)}) copy-start(bf16[128,128]{1,0:T(8,128)(2,1)} %wb_ref.3) | copy-start | bytes 98308
  4.3 9.6 %collective-permute-start = (bf16[640,128]{1,0:T(8,128)(2,1)S(1)}, bf16[640,128]{1,0:T(8,128)(2,1)S(1)}, u32[]{:S(2)}, u32[]{:S(2)}) collective-permute-start(bf16[640,128]{1,0:T(8,128)(2,1)S(1)} %get-tuple-element.42.after_ref), channel_id=1, source_target_pairs={{0,1},{1,0},{2,3},{3,2},{4,5},{5,4},{6,7},{7,6},{8,9},{9,8},{10,11... | collective-permute-start | bytes 491528 | tf_op jit(solution)/shard_map/ppermute | solution.py:416
  4.8 9.2 %collective-permute-start.3 = (bf16[272,128]{1,0:T(8,128)(2,1)S(1)}, bf16[272,128]{1,0:T(8,128)(2,1)S(1)}, u32[]{:S(2)}, u32[]{:S(2)}) collective-permute-start(bf16[272,128]{1,0:T(8,128)(2,1)S(1)} %get-tuple-element.43), channel_id=1, source_target_pairs={{0,7},{1,2},{2,1},{3,4},{4,3},{5,6},{6,5},{7,0},{8,15},{9,10},{10,... | collective-permute-start | bytes 208904 | tf_op jit(solution)/shard_map/ppermute | solution.py:416
  9.5 5.2 %collective-permute-start.4 = (bf16[272,128]{1,0:T(8,128)(2,1)S(1)}, bf16[272,128]{1,0:T(8,128)(2,1)S(1)}, u32[]{:S(2)}, u32[]{:S(2)}) collective-permute-start(bf16[272,128]{1,0:T(8,128)(2,1)S(1)} %get-tuple-element.44), channel_id=1, source_target_pairs={{0,8},{8,16},{16,24},{24,0},{1,9},{9,17},{17,25},{25,1},{2,10},{10... | collective-permute-start | bytes 208904 | tf_op jit(solution)/shard_map/ppermute | solution.py:416
  11.0 4.5 %collective-permute-start.5 = (bf16[272,128]{1,0:T(8,128)(2,1)S(1)}, bf16[272,128]{1,0:T(8,128)(2,1)S(1)}, u32[]{:S(2)}, u32[]{:S(2)}) collective-permute-start(bf16[272,128]{1,0:T(8,128)(2,1)S(1)} %get-tuple-element.45), channel_id=1, source_target_pairs={{0,24},{8,0},{16,8},{24,16},{1,25},{9,1},{17,9},{25,17},{2,26},{10... | collective-permute-start | bytes 208904 | tf_op jit(solution)/shard_map/ppermute | solution.py:416
  13.1 2.4 %copy-start.6 = (s32[1,96,2]{1,2,0:T(2,128)S(1)}, s32[1,96,2]{1,2,0:T(2,128)}, u32[]{:S(2)}) copy-start(s32[1,96,2]{1,2,0:T(2,128)} %param.20) | copy-start | bytes 2308
  13.9 4.6 %collective-permute-start.1 = (bf16[368,128]{1,0:T(8,128)(2,1)S(1)}, bf16[368,128]{1,0:T(8,128)(2,1)S(1)}, u32[]{:S(2)}, u32[]{:S(2)}) collective-permute-start(bf16[368,128]{1,0:T(8,128)(2,1)S(1)} %fusion.after_ref), channel_id=1, source_target_pairs={{0,2},{1,3},{2,0},{3,1},{4,6},{5,7},{6,4},{7,5},{8,10},{9,11},{10,... | collective-permute-start | bytes 282632 | tf_op jit(solution)/shard_map/ppermute | solution.py:416
  18.6 6.0 %collective-permute-start.2 = (bf16[368,128]{1,0:T(8,128)(2,1)S(1)}, bf16[368,128]{1,0:T(8,128)(2,1)S(1)}, u32[]{:S(2)}, u32[]{:S(2)}) collective-permute-start(bf16[368,128]{1,0:T(8,128)(2,1)S(1)} %fusion.1.after_ref), channel_id=1, source_target_pairs={{0,4},{1,5},{2,6},{3,7},{4,0},{5,1},{6,2},{7,3},{8,12},{9,13},{10,... | collective-permute-start | bytes 282632 | tf_op jit(solution)/shard_map/ppermute | solution.py:416
  18.8 9.5 %copy-start = (bf16[128,256]{1,0:T(8,128)(2,1)S(1)}, bf16[128,256]{1,0:T(8,128)(2,1)}, u32[]{:S(2)}) copy-start(bf16[128,256]{1,0:T(8,128)(2,1)} %w_in_ref.1) | copy-start | bytes 196612
  18.8 9.5 %copy-start.1 = (bf16[256,128]{1,0:T(8,128)(2,1)S(1)}, bf16[256,128]{1,0:T(8,128)(2,1)}, u32[]{:S(2)}) copy-start(bf16[256,128]{1,0:T(8,128)(2,1)} %w_out_ref.1) | copy-start | bytes 196612
  18.8 9.5 %copy-start.4 = (bf16[128,128]{1,0:T(8,128)(2,1)S(1)}, bf16[128,128]{1,0:T(8,128)(2,1)}, u32[]{:S(2)}) copy-start(bf16[128,128]{1,0:T(8,128)(2,1)} %w_long_ref.1) | copy-start | bytes 98308
  18.8 9.5 %copy-start.5 = (s32[512,3]{0,1:T(4,128)S(1)}, s32[512,3]{0,1:T(4,128)}, u32[]{:S(2)}) copy-start(s32[512,3]{0,1:T(4,128)} %param.22) | copy-start | bytes 18436
  18.8 9.5 %copy-start.8 = (f32[128]{0:T(128)S(1)}, f32[128]{0:T(128)}, u32[]{:S(2)}) copy-start(f32[128]{0:T(128)} %param.27) | copy-start | bytes 1540
  18.8 9.5 %copy-start.9 = (f32[368,1]{1,0:T(8,128)S(1)}, f32[368,1]{1,0:T(8,128)}, u32[]{:S(2)}) copy-start(f32[368,1]{1,0:T(8,128)} %constant.22.clone.norm2_ref) | copy-start | bytes 4420
  24.7 4.1 %collective-permute-start.6 = (bf16[624,128]{1,0:T(8,128)(2,1)S(1)}, bf16[624,128]{1,0:T(8,128)(2,1)S(1)}, u32[]{:S(2)}, u32[]{:S(2)}) collective-permute-start(bf16[624,128]{1,0:T(8,128)(2,1)S(1)} %pad_maximum_fusion.after_ref), channel_id=1, source_target_pairs={{0,1},{1,0},{2,3},{3,2},{4,5},{5,4},{6,7},{7,6},{8,9},{9,8},{10,11... | collective-permute-start | bytes 479240 | tf_op jit(solution)/shard_map/ppermute | solution.py:416
  24.8 7.5 %collective-permute-start.7 = (bf16[256,128]{1,0:T(8,128)(2,1)S(1)}, bf16[256,128]{1,0:T(8,128)(2,1)S(1)}, u32[]{:S(2)}, u32[]{:S(2)}) collective-permute-start(bf16[256,128]{1,0:T(8,128)(2,1)S(1)} %get-tuple-element.66), channel_id=1, source_target_pairs={{0,7},{1,2},{2,1},{3,4},{4,3},{5,6},{6,5},{7,0},{8,15},{9,10},{10,... | collective-permute-start | bytes 196616 | tf_op jit(solution)/shard_map/ppermute | solution.py:416
  26.3 6.0 %collective-permute-start.8 = (bf16[256,128]{1,0:T(8,128)(2,1)S(1)}, bf16[256,128]{1,0:T(8,128)(2,1)S(1)}, u32[]{:S(2)}, u32[]{:S(2)}) collective-permute-start(bf16[256,128]{1,0:T(8,128)(2,1)S(1)} %get-tuple-element.67), channel_id=1, source_target_pairs={{0,24},{8,0},{16,8},{24,16},{1,25},{9,1},{17,9},{25,17},{2,26},{10... | collective-permute-start | bytes 196616 | tf_op jit(solution)/shard_map/ppermute | solution.py:416
  27.9 5.2 %collective-permute-start.9 = (bf16[256,128]{1,0:T(8,128)(2,1)S(1)}, bf16[256,128]{1,0:T(8,128)(2,1)S(1)}, u32[]{:S(2)}, u32[]{:S(2)}) collective-permute-start(bf16[256,128]{1,0:T(8,128)(2,1)S(1)} %get-tuple-element.68), channel_id=1, source_target_pairs={{0,8},{8,16},{16,24},{24,0},{1,9},{9,17},{17,25},{25,1},{2,10},{10... | collective-permute-start | bytes 196616 | tf_op jit(solution)/shard_map/ppermute | solution.py:416
  28.8 4.3 %copy-start.7 = (s32[1,4,2]{1,2,0:T(2,128)S(1)}, s32[1,4,2]{1,2,0:T(2,128)}, u32[]{:S(2)}) copy-start(s32[1,4,2]{1,2,0:T(2,128)} %param.19) | copy-start | bytes 100

commit v2 on v1

--- a/solution.py
+++ b/solution.py
@@ -124,6 +124,16 @@
 
 def block(ref, b):
     return ref[b * BLK : (b + 1) * BLK, :]
+
+
+def send_block(lists_ref, direction, feats_ref, coords_ref, out_ref):
+    pieces = []
+    for h in range(HB):
+        start = pl.multiple_of(lists_ref[0, h, direction] * BLK, BLK)
+        out_ref[pl.ds(h * BLK, BLK), :] = feats_ref[pl.ds(start, BLK), :]
+        pieces.append(coords_ref[:, pl.ds(start, BLK)].astype(F32))
+        pieces.append(jnp.zeros((COORD_ROWS // HB - 3, BLK), F32))
+    out_ref[pl.ds(HB * BLK, COORD_ROWS), :] = jnp.concatenate(pieces, axis=0).astype(BF16)
 
 
 def load_kernel(n_load, flip_ref, lists_hbm, *refs):
@@ -137,17 +147,9 @@
         copy.start()
     for copy in copies[:3]:
         copy.wait()
-    feats_ref, coords_ref = loaded[0], loaded[1]
     odd = flip_ref[0]
-    for slot, direction in enumerate((odd, 1 - odd, 2, 3)):
-        pieces = []
-        for h in range(HB):
-            b = lists_ref[0, h, direction]
-            start = pl.multiple_of(b * BLK, BLK)
-            outs[slot][pl.ds(h * BLK, BLK), :] = feats_ref[pl.ds(start, BLK), :]
-            pieces.append(coords_ref[:, pl.ds(start, BLK)].astype(F32))
-            pieces.append(jnp.zeros((COORD_ROWS // HB - 3, BLK), F32))
-        outs[slot][pl.ds(HB * BLK, COORD_ROWS), :] = jnp.concatenate(pieces, axis=0).astype(BF16)
+    for out_ref, direction in zip(outs, (odd, 1 - odd, 2, 3)):
+        send_block(lists_ref, direction, loaded[0], loaded[1], out_ref)
     for copy in copies[3:]:
         copy.wait()
 
@@ -159,9 +161,10 @@
     table = table_ref[...].astype(BF16)
     w = w_ref[...]
     for first in range(0, atoms, chunk):
-        charges = dot(feats_ref[pl.ds(first, chunk), :], w).astype(BF16)
-        trig = trig_chunk(table, coords16(coords_ref[:, pl.ds(first, chunk)]))
-        trig_ref[:, pl.ds(first, chunk)] = trig
+        at = slice(first, first + chunk)
+        charges = dot(feats_ref[at, :], w).astype(BF16)
+        trig = trig_chunk(table, coords16(coords_ref[:, at]))
+        trig_ref[:, at] = trig
         part = dot(trig, charges)
         if first == 0:
             total_ref[...] = part
@@ -176,7 +179,7 @@
 
 
 def source_block(j, w_cat, feats, far, proj_ref, far_ref):
-    both = dot(w_cat, feats, NT).astype(BF16)
+    both = (dot(w_cat, feats, NT) * MSG_SCALE).astype(BF16)
     proj_ref[j, :, 0:BLK] = both[:BLK]
     proj_ref[j, :, BLK:] = both[BLK:]
     far_ref[j] = far.T.astype(BF16)
@@ -186,10 +189,56 @@
     return jnp.concatenate([wa_ref[...].astype(F32).T, wb_ref[...].astype(F32).T], axis=0).astype(BF16)
 
 
+def halo_blocks(got, first_block, w_cat, proj_ref, far_ref):
+    tail = got[HB * BLK : HB * BLK + COORD_ROWS, :].astype(F32)
+    for h in range(HB):
+        at = h * (COORD_ROWS // HB)
+        far = dist_rows(tail[at : at + 3], False)
+        source_block(first_block + h, w_cat, block(got, h), far, proj_ref, far_ref)
+
+
+def tile_plan(tiles_ref, count_ref, nblk):
+    slots = tiles_ref.shape[2]
+    tiles = tiles_ref[0].astype(F32)
+    iota = lambda axis: lax.broadcasted_iota(jnp.int32, (slots, slots), axis)
+    before = (iota(1) < iota(0)).astype(F32).astype(BF16)
+    same = (iota(1) == iota(0)).astype(F32).astype(BF16)
+    number = lax.broadcasted_iota(jnp.int32, (1, slots), 1)
+    live = (number < count_ref[...]).astype(F32)
+    own = live * (tiles[1:2] < float(nblk)).astype(F32)
+    parts = []
+    for chosen in (own, live - own):
+        row = jnp.broadcast_to(chosen, (8, slots)).astype(BF16)
+        place = dot(before, row, NT)[:, 0:1].astype(jnp.int32)
+        here = dot(same, row, NT)[:, 0:1] > 0.5
+        move = ((iota(1) == place) & here).astype(F32).astype(BF16)
+        moved = dot(jnp.concatenate([tiles, tiles, tiles, tiles], axis=0).astype(BF16), move)
+        parts += [moved[0:2], jnp.broadcast_to(jnp.sum(chosen, axis=1, keepdims=True), (1, slots))]
+    parts.append(jnp.zeros((2, slots), F32))
+    return jnp.concatenate(parts, axis=0).astype(jnp.int32)
+
+
 def local_kernel(
-    feats_ref, coords_ref, cot_ref, wa_ref, wb_ref, after_ref, proj_ref, far_ref, near_ref, cotp_ref
+    tiles_ref,
+    count_ref,
+    feats_ref,
+    coords_ref,
+    cot_ref,
+    wa_ref,
+    wb_ref,
+    flip_ref,
+    got1,
+    got2,
+    got3,
+    after_ref,
+    proj_ref,
+    far_ref,
+    near_ref,
+    cotp_ref,
+    plan_ref,
 ):
     nblk = feats_ref.shape[0] // BLK
+    plan_ref[...] = tile_plan(tiles_ref, count_ref, nblk)
     w_cat = both_transposed(wa_ref, wb_ref)
     w_side = jnp.concatenate([wa_ref[...], wb_ref[...]], axis=0)
     near = dist_rows(coords_ref[...], True).astype(BF16)
@@ -198,24 +247,25 @@
         at = slice(b * BLK, (b + 1) * BLK)
         source_block(b, w_cat, block(feats_ref, b), far[:, at], proj_ref, far_ref)
         near_ref[b] = near[:, at]
-        both = dot(block(cot_ref, b), w_side, NT).astype(BF16)
+        both = (dot(block(cot_ref, b), w_side, NT) * MSG_SCALE).astype(BF16)
         cotp_ref[b, 0:BLK, :] = both[:, :BLK]
         cotp_ref[b, BLK:, :] = both[:, BLK:]
-
-
-def tile_range(
-    unroll, first, last, count, tiles_ref, proj_ref, far_ref, near_ref, cotp_ref, msg_ref, grad_ref
-):
+    for got, place in zip((got1, got2, got3), (flip_ref[0], 2, 3)):
+        halo_blocks(got, nblk + place * HB, w_cat, proj_ref, far_ref)
+
+
+def tile_part(unroll, row, plan_ref, proj_ref, far_ref, near_ref, cotp_ref, msg_ref, grad_ref):
     spare_i, spare_j = msg_ref.shape[0] - 1, grad_ref.shape[0] - 1
-    slots = tiles_ref.shape[2]
-
-    @pl.loop(first, last)
+    slots = plan_ref.shape[1]
+    count = plan_ref[row + 2, 0]
+
+    @pl.loop(0, (count + unroll - 1) // unroll)
     def _(step):
         idx = []
         for u in range(unroll):
             t = step * unroll + u
             at = jnp.minimum(t, slots - 1)
-            i, j, live = tiles_ref[0, 0, at], tiles_ref[0, 1, at], t < count
+            i, j, live = plan_ref[row, at], plan_ref[row + 1, at], t < count
             idx.append((i, j, jnp.where(live, i, spare_i), jnp.where(live, j, spare_j)))
         kers = []
         for i, j, _, _ in idx:
@@ -229,19 +279,11 @@
             grad_ref[to_j] += dot(jnp.concatenate([ka, kb], axis=1), cotp_ref[i])
 
 
-def groups(count, unroll):
-    return (count + unroll - 1) // unroll
-
-
-def tiles_first_kernel(
+def tiles_received_kernel(
     unroll,
     flip_ref,
-    tiles_ref,
-    count_ref,
+    plan_ref,
     got0,
-    got1,
-    got2,
-    got3,
     wa_ref,
     wb_ref,
     near_ref,
@@ -253,54 +295,31 @@
     far_ref,
     msg_ref,
     grad_ref,
-):
-    nblk = near_ref.shape[0]
-    w_cat = both_transposed(wa_ref, wb_ref)
-    odd = flip_ref[0]
-    for got, place in zip((got0, got1, got2, got3), (1 - odd, odd, 2, 3)):
-        tail = got[HB * BLK : HB * BLK + COORD_ROWS, :].astype(F32)
-        for h in range(HB):
-            at = h * (COORD_ROWS // HB)
-            far = dist_rows(tail[at : at + 3], False)
-            source_block(nblk + place * HB + h, w_cat, block(got, h), far, proj_ref, far_ref)
-    msg_ref[...] = jnp.zeros_like(msg_ref)
-    grad_ref[...] = jnp.zeros_like(grad_ref)
-    count = count_ref[0]
-    last = groups(count, unroll) // 2
-    tile_range(unroll, 0, last, count, tiles_ref, proj_ref, far_ref, near_ref, cotp_ref, msg_ref, grad_ref)
-
-
-def tiles_second_kernel(
-    unroll,
-    flip_ref,
-    tiles_ref,
-    count_ref,
-    proj_ref,
-    far_ref,
-    near_ref,
-    cotp_ref,
-    msg_in,
-    grad_in,
-    after_ref,
-    msg_ref,
-    grad_ref,
     held0,
     held1,
     held2,
     held3,
 ):
     nblk = near_ref.shape[0]
-    count = count_ref[0]
-    last = groups(count, unroll)
-    tile_range(unroll, last // 2, last, count, tiles_ref, proj_ref, far_ref, near_ref, cotp_ref, msg_ref, grad_ref)
     odd = flip_ref[0]
+    halo_blocks(got0, nblk + (1 - odd) * HB, both_transposed(wa_ref, wb_ref), proj_ref, far_ref)
+    msg_ref[...] = jnp.zeros_like(msg_ref)
+    grad_ref[...] = jnp.zeros_like(grad_ref)
+    tile_part(unroll, 3, plan_ref, proj_ref, far_ref, near_ref, cotp_ref, msg_ref, grad_ref)
     for held, place in zip((held0, held1, held2, held3), (1 - odd, odd, 2, 3)):
         for h in range(HB):
-            held[h * BLK : (h + 1) * BLK, :] = (grad_ref[nblk + place * HB + h] * MSG_SCALE).astype(BF16)
+            held[h * BLK : (h + 1) * BLK, :] = grad_ref[nblk + place * HB + h].astype(BF16)
+
+
+def tiles_own_kernel(
+    unroll, plan_ref, proj_ref, far_ref, near_ref, cotp_ref, msg_in, grad_in, after_ref, msg_ref, grad_ref
+):
+    tile_part(unroll, 0, plan_ref, proj_ref, far_ref, near_ref, cotp_ref, msg_ref, grad_ref)
 
 
 def prepare_kernel(
     group_atoms,
+    flip_ref,
     wave_ref,
     norm2_ref,
     w_long_ref,
@@ -308,14 +327,19 @@
     w_in_ref,
     w_out_ref,
     feats_ref,
-    after_ref,
+    after1,
+    after2,
+    after3,
+    after4,
     strength_ref,
     w_long_t_ref,
     w_in_t_ref,
     w_out_t_ref,
     gain_t_ref,
     feats_t_ref,
-):
+    parity_ref,
+):
+    parity_ref[...] = jnp.full(parity_ref.shape, flip_ref[0].astype(F32))
     n = wave_ref[...].astype(F32)
     n0, n1, n2 = n[0:1], n[1:2], n[2:3]
     lead = jnp.where(n0 != 0.0, n0, jnp.where(n1 != 0.0, n1, n2))
@@ -345,7 +369,6 @@
 
 def update_kernel(
     chunk,
-    flip_ref,
     mine_ref,
     other_ref,
     strength_ref,
@@ -356,52 +379,64 @@
     gain_t_ref,
     w_in_t_ref,
     w_out_t_ref,
+    parity_ref,
     out_ref,
-    done_ref,
-):
-    done_ref[...] = jnp.zeros_like(done_ref)
+):
     atoms = feats_t_ref.shape[1]
-    mine = flip_ref[0] == 0
-    a = (strength_ref[...] * mine_ref[...].astype(F32)).astype(BF16)
-    b = (strength_ref[...] * other_ref[HB * BLK :, :].astype(F32)).astype(BF16)
-    weighted = jnp.concatenate([jnp.where(mine, a, b), jnp.where(mine, b, a)], axis=0)
+    a = strength_ref[...] * mine_ref[...].astype(F32)
+    b = strength_ref[...] * other_ref[HB * BLK :, :].astype(F32)
+    even = parity_ref[0:1, :] == 0.0
+    weighted = jnp.concatenate([jnp.where(even, a, b), jnp.where(even, b, a)], axis=0).astype(BF16)
     mix_w = dot(w_long_t_ref[...], weighted, NT).astype(BF16)
     gain = jnp.concatenate([gain_t_ref[...]] * (chunk // BLK), axis=1)
     w_in_t = w_in_t_ref[...]
     w_out_t = w_out_t_ref[...]
-    for first in range(0, atoms, chunk):
-        at = slice(first, first + chunk)
-        msg = jnp.concatenate([msg_ref[(first // BLK) + i] for i in range(chunk // BLK)], axis=1)
-        mixed = dot(mix_w, trig_ref[:, at]) + msg * MSG_SCALE + feats_t_ref[:, at].astype(F32)
+    for step in range(atoms // chunk):
+        at = slice(step * chunk, (step + 1) * chunk)
+        msg = jnp.concatenate([msg_ref[step * (chunk // BLK) + i] for i in range(chunk // BLK)], axis=1)
+        mixed = dot(mix_w, trig_ref[:, at]) + msg + feats_t_ref[:, at].astype(F32)
         scale = lax.rsqrt(jnp.mean(mixed * mixed, axis=0, keepdims=True) + 1e-06)
         normed = (mixed * scale * gain).astype(BF16)
         pre = dot(w_in_t, normed)
-        hidden = (pre / (1.0 + jnp.exp(-pre))).astype(BF16)
+        half = 0.5 * pre
+        hidden = (half * jnp.tanh(half) + half).astype(BF16)
         out = mixed + dot(w_out_t, hidden)
         out_ref[at, :] = out.T.astype(BF16)
 
 
-def adjoint_kernel(lists_ref, flip_ref, grad_ref, r0, r1, r2, r3, after_ref, out_ref):
-    nblk = out_ref.shape[0] // BLK
+def finish_kernel(
+    lists_ref,
+    flip_ref,
+    new_ref,
+    back0,
+    back1,
+    back2,
+    back3,
+    grad_in,
+    out_hbm,
+    adjoint_hbm,
+    grad_ref,
+    sems,
+):
+    nblk = adjoint_hbm.shape[0]
+    first = pltpu.make_async_copy(new_ref, out_hbm, sems.at[0])
+    first.start()
     odd = flip_ref[0]
-    for b in range(nblk):
-        out_ref[b * BLK : (b + 1) * BLK, :] = grad_ref[b] * MSG_SCALE
-    for ref, direction in zip((r0, r1, r2, r3), (odd, 1 - odd, 2, 3)):
+    for ref, direction in zip((back0, back1, back2, back3), (odd, 1 - odd, 2, 3)):
         for h in range(HB):
-            b = lists_ref[0, h, direction]
-            at = pl.ds(pl.multiple_of(b * BLK, BLK), BLK)
-            out_ref[at, :] += ref[h * BLK : (h + 1) * BLK, :].astype(F32)
-
-
-def call(kernel, outs, args, specs, scratch=(), us=1.0, aliases=None):
-    single = not isinstance(outs, (list, tuple))
+            grad_ref[lists_ref[0, h, direction]] += block(ref, h).astype(F32)
+    second = pltpu.make_async_copy(grad_ref.at[pl.ds(0, nblk)], adjoint_hbm, sems.at[1])
+    second.start()
+    first.wait()
+    second.wait()
+
+
+def call(kernel, outs, args, specs, scratch=(), us=1.0, aliases=None, out_specs=None):
     return pl.pallas_call(
         kernel,
         out_shape=outs,
         in_specs=[pl.BlockSpec(memory_space=s) for s in specs],
-        out_specs=pl.BlockSpec(memory_space=VMEM)
-        if single
-        else [pl.BlockSpec(memory_space=VMEM) for _ in outs],
+        out_specs=[pl.BlockSpec(memory_space=s) for s in (out_specs or (VMEM,) * len(outs))],
         scratch_shapes=list(scratch),
         input_output_aliases=aliases or {},
         compiler_params=pltpu.CompilerParams(vmem_limit_bytes=24 * 1024 * 1024),
@@ -448,17 +483,16 @@
     down = lambda i: i - 1
     lists = jnp.swapaxes(send_list, 1, 2)
     tile_rows = jnp.swapaxes(tiles, 1, 2)
+    tile_count = tile_count.reshape(1, 1)
     table = jnp.asarray(base_table())
     norm2 = jnp.asarray(grid_norm2())
 
-    loads = tuple(
-        pltpu.with_memory_space_constraint(x, pltpu.HBM)
-        for x in (feats, coords, msg_cot, table, w_charge)
-    )
+    in_hbm = lambda x: pltpu.with_memory_space_constraint(x, pltpu.HBM)
+    loads = tuple(in_hbm(x) for x in (feats, coords, msg_cot, table, w_charge))
     loaded = call(
         functools.partial(load_kernel, len(loads)),
         [like(x) for x in loads] + [sds((HB * BLK + COORD_ROWS, width), BF16)] * 4,
-        (flip, pltpu.with_memory_space_constraint(lists, pltpu.HBM), *loads),
+        (flip, in_hbm(lists), *loads),
         (SMEM,) + (pltpu.HBM,) * (1 + len(loads)),
         scratch=[SMEM(lists.shape, lists.dtype), pltpu.SemaphoreType.DMA((1 + len(loads),))],
         us=1.2,
@@ -482,18 +516,6 @@
         us=2.3,
     )
     got0 = exchange(send, "dom", near_pair)
-    proj, far, near, cotp = call(
-        local_kernel,
-        [
-            sds((extent, width, 2 * BLK), BF16),
-            sds((extent, BLK, COORD_ROWS), BF16),
-            sds((nblk, COORD_ROWS, BLK), BF16),
-            sds((nblk, 2 * BLK, width), BF16),
-        ],
-        (feats, coords, msg_cot, w_rad_a, w_rad_b, send),
-        (VMEM,) * 5 + (pl.ANY,),
-        us=1.0,
-    )
     total = keep + got0[HB * BLK + COORD_ROWS :].astype(F32)
     sums = [total.astype(BF16)]
     step = 2
@@ -502,30 +524,43 @@
         sums.append(total.astype(BF16))
         step *= 2
 
-    proj, far, msg, grad = call(
-        functools.partial(tiles_first_kernel, unroll),
-        [like(proj), like(far), sds((nblk + 1, width, BLK), F32), sds((extent + 1, BLK, width), F32)],
-        (flip, tile_rows, tile_count, got0, got1, got2, got3, w_rad_a, w_rad_b, near, cotp, proj, far, sums[0]),
-        (SMEM,) * 3 + (VMEM,) * 10 + (pl.ANY,),
-        aliases={11: 0, 12: 1},
-        us=3.5,
-    )
-    msg, grad, *held = call(
-        functools.partial(tiles_second_kernel, unroll),
-        [like(msg), like(grad)] + [sds((HB * BLK, width), BF16)] * 4,
-        (flip, tile_rows, tile_count, proj, far, near, cotp, msg, grad, sums[min(1, len(sums) - 1)]),
-        (SMEM,) * 3 + (VMEM,) * 6 + (pl.ANY,),
+    proj, far, near, cotp, plan = call(
+        local_kernel,
+        [
+            sds((extent, width, 2 * BLK), BF16),
+            sds((extent, BLK, COORD_ROWS), BF16),
+            sds((nblk, COORD_ROWS, BLK), BF16),
+            sds((nblk, 2 * BLK, width), BF16),
+            sds((8, tiles.shape[1]), jnp.int32),
+        ],
+        (tile_rows, tile_count, feats, coords, msg_cot, w_rad_a, w_rad_b, flip, got1, got2, got3, send),
+        (VMEM,) * 7 + (SMEM,) + (VMEM,) * 3 + (pl.ANY,),
+        us=1.0,
+    )
+    proj, far, msg, grad, *held = call(
+        functools.partial(tiles_received_kernel, unroll),
+        [like(proj), like(far), sds((nblk + 1, width, BLK), F32), sds((extent + 1, BLK, width), F32)]
+        + [sds((HB * BLK, width), BF16)] * 4,
+        (flip, plan, got0, w_rad_a, w_rad_b, near, cotp, proj, far, sums[0]),
+        (SMEM,) * 2 + (VMEM,) * 7 + (pl.ANY,),
+        us=3.0,
         aliases={7: 0, 8: 1},
-        us=3.5,
+    )
+    msg, grad = call(
+        functools.partial(tiles_own_kernel, unroll),
+        [like(msg), like(grad)],
+        (plan, proj, far, near, cotp, msg, grad, sums[min(1, len(sums) - 1)]),
+        (SMEM,) + (VMEM,) * 6 + (pl.ANY,),
+        us=5.0,
+        aliases={5: 0, 6: 1},
     )
     back1 = exchange(held[1], "dom", far_pair)
     back2 = exchange(held[2], "group", down)
     back3 = exchange(held[3], "group", up)
     total = sums[-1]
-    last = jnp.concatenate([held[0], total], axis=0)
-    back0 = exchange(last, "dom", near_pair)
-
-    strength, w_long_t, w_in_t, w_out_t, gain_t, feats_t = call(
+    back0 = exchange(jnp.concatenate([held[0], total], axis=0), "dom", near_pair)
+
+    strength, w_long_t, w_in_t, w_out_t, gain_t, feats_t, parity = call(
         functools.partial(prepare_kernel, atoms * domains),
         [
             sds((HALF, width), F32),
@@ -534,26 +569,30 @@
             sds((width, hidden), BF16),
             sds((width, BLK), F32),
             sds((width, atoms), BF16),
+            sds((8, width), F32),
         ],
-        (wavevec.T, norm2, w_long, norm_gain.reshape(1, width), w_in, w_out, feats, last),
-        (VMEM,) * 7 + (pl.ANY,),
+        (flip, wavevec.T, norm2, w_long, norm_gain.reshape(1, width), w_in, w_out, feats, back1, back2, back3, msg),
+        (SMEM,) + (VMEM,) * 7 + (pl.ANY,) * 4,
         us=0.5,
     )
-    new_feats, done = call(
-        functools.partial(update_kernel, 256),
-        [sds((atoms, width), BF16), sds((8, BLK), F32)],
-        (flip, total, back0, strength, trig, feats_t, msg, w_long_t, gain_t, w_in_t, w_out_t),
-        (SMEM,) + (VMEM,) * 10,
-        us=3.4,
-    )
-    adjoint = call(
-        adjoint_kernel,
-        sds((atoms, width), F32),
-        (lists, flip, grad, back0, back1, back2, back3, done),
-        (SMEM, SMEM) + (VMEM,) * 5 + (pl.ANY,),
-        us=1.6,
-    )
-    return (new_feats, adjoint)
+    (new_feats,) = call(
+        functools.partial(update_kernel, atoms // 2),
+        [sds((atoms, width), BF16)],
+        (total, back0, strength, trig, feats_t, msg, w_long_t, gain_t, w_in_t, w_out_t, parity),
+        (VMEM,) * 11,
+        us=2.5,
+    )
+    new_feats, adjoint, _ = call(
+        finish_kernel,
+        [sds((atoms, width), BF16), sds((nblk, BLK, width), F32), like(grad)],
+        (lists, flip, new_feats, back0, back1, back2, back3, grad),
+        (SMEM, SMEM) + (VMEM,) * 6,
+        scratch=[pltpu.SemaphoreType.DMA((2,))],
+        us=1.5,
+        aliases={7: 2},
+        out_specs=(pltpu.HBM, pltpu.HBM, VMEM),
+    )
+    return (new_feats, adjoint.reshape(atoms, width))
 
 
 def solution(mesh):

time: 34.9 us -> 32.6 us (0.934)
  waiting for transfers between devices: 7.6 us -> 4 us
  Pallas kernels: 13.4 us -> 16.1 us
  starting transfers between devices: 12 us -> 10.6 us
    ppermute x10, waiting for transfers between devices: 7.6 us -> 4 us  [exchange(): lax.ppermute(value, axis, [(i, partner(i) % length) for i in range(length)])]
    pallas_call x8, Pallas kernels: 13.4 us -> 16.1 us  [call(): pl.pallas_call(kernel, out_shape=outs, in_specs=[pl.BlockSpec(memory_spac...]
    ppermute x10, starting transfers between devices: 12 us -> 10.6 us  [exchange(): lax.ppermute(value, axis, [(i, partner(i) % length) for i in range(length)])]
  transfers between devices with their start and end apart: 10 -> 10, of which waited for: 5 -> 4; matrix products, arithmetic and copies ran while one was open for 0% -> 0% of each run, Pallas kernels for 23% -> 27%
where the time goes in v2:
time: 32.6 us; the launch traced here: 32.4 us
  Pallas kernels  16.1 us (49%)
  starting transfers between devices  10.6 us (33%)
  waiting for transfers between devices  4 us (12%)
  between operations  1.55 us (5%)
    pallas_call x8, Pallas kernels, call(): pl.pallas_call(kernel, out_shape=outs, in_specs=[pl.BlockSpec(memory_spac...  16.1 us
    ppermute x10, starting transfers between devices, exchange(): lax.ppermute(value, axis, [(i, partner(i) % length) for i in range(length)])  10.6 us
    ppermute x10, waiting for transfers between devices, exchange(): lax.ppermute(value, axis, [(i, partner(i) % length) for i in range(length)])  4 us
  transfers between devices with their start and end apart: 10, of which 4 were waited for; matrix products, arithmetic and copies ran while one was open for 0% of the time, Pallas kernels for 27%

profile of v2, /device:TPU:0, one launch (start us, length us, event | category | flops | bytes accessed | tf_op | source)
XLA Modules:
  0.0 32.4 jit_solution(302193741109494738)
XLA Ops:
  0.6 1.3 %shard_map.167 = (bf16[2048,128]{1,0:T(8,128)(2,1)S(1)}, bf16[3,2048]{1,0:T(4,128)(2,1)S(1)}, bf16[2048,128]{1,0:T(8,128)(2,1)S(1)}, f32[48,16]{1,0:T(8,128)S(1)...) custom-call(s32[1]{0:T(128)} %bitcast.1.flip_ref, ...), custom_call_target="tpu_custom_call" | custom-call | flops 1320000000 | bytes 4080000 | tf_op jit(solution)/shard_map/pallas_call | solution.py:435
  1.9 0.0 copy-start.6
  1.9 0.0 copy-start.7
  1.9 0.0 copy-start.8
  2.0 2.3 %shard_map.168 = (f32[368,128]{1,0:T(8,128)S(1)}, bf16[640,128]{1,0:T(8,128)(2,1)S(1)}, bf16[736,2048]{1,0:T(8,128)(2,1)S(1)}) custom-call(s32[1]{0:T(128)} %bitcast.1.flip_ref, bf16[2048,128]{1,0:T(8,128)(2,1)S(1)} %get-tuple-element.38.feats_ref, bf16[3,2048]{1,0:T(4,128)(2,1)S(1)} %get-tuple-element.39.coords_ref, ...), custom_call_target="tpu_custom_call" | custom-call | flops 2529999872 | bytes 7819999 | tf_op jit(solution)/shard_map/pallas_call | solution.py:435
  4.3 0.5 %collective-permute-start = (bf16[640,128]{1,0:T(8,128)(2,1)S(1)}, bf16[640,128]{1,0:T(8,128)(2,1)S(1)}, u32[]{:S(2)}, u32[]{:S(2)}) collective-permute-start(bf16[640,128]{1,0:T(8,128)(2,1)S(1)} %get-tuple-element.44.after_ref), channel_id=1, source_target_pairs={{0,1},{1,0},{2,3},{3,2},{4,5},{5,4},{6,7},{7,6},{8,9},{9,8},{10,11... | collective-permute-start | bytes 491528 | tf_op jit(solution)/shard_map/ppermute | solution.py:451
  4.8 4.7 %collective-permute-start.3 = (bf16[272,128]{1,0:T(8,128)(2,1)S(1)}, bf16[272,128]{1,0:T(8,128)(2,1)S(1)}, u32[]{:S(2)}, u32[]{:S(2)}) collective-permute-start(bf16[272,128]{1,0:T(8,128)(2,1)S(1)} %get-tuple-element.46), channel_id=1, source_target_pairs={{0,7},{1,2},{2,1},{3,4},{4,3},{5,6},{6,5},{7,0},{8,15},{9,10},{10,... | collective-permute-start | bytes 208904 | tf_op jit(solution)/shard_map/ppermute | solution.py:451
  9.5 1.5 %collective-permute-start.4 = (bf16[272,128]{1,0:T(8,128)(2,1)S(1)}, bf16[272,128]{1,0:T(8,128)(2,1)S(1)}, u32[]{:S(2)}, u32[]{:S(2)}) collective-permute-start(bf16[272,128]{1,0:T(8,128)(2,1)S(1)} %get-tuple-element.47), channel_id=1, source_target_pairs={{0,8},{8,16},{16,24},{24,0},{1,9},{9,17},{17,25},{25,1},{2,10},{10... | collective-permute-start | bytes 208904 | tf_op jit(solution)/shard_map/ppermute | solution.py:451
  11.0 1.4 %collective-permute-start.5 = (bf16[272,128]{1,0:T(8,128)(2,1)S(1)}, bf16[272,128]{1,0:T(8,128)(2,1)S(1)}, u32[]{:S(2)}, u32[]{:S(2)}) collective-permute-start(bf16[272,128]{1,0:T(8,128)(2,1)S(1)} %get-tuple-element.48), channel_id=1, source_target_pairs={{0,24},{8,0},{16,8},{24,16},{1,25},{9,1},{17,9},{25,17},{2,26},{10... | collective-permute-start | bytes 208904 | tf_op jit(solution)/shard_map/ppermute | solution.py:451
  13.2 0.1 collective-permute-start.1
  13.3 1.5 %collective-permute-done.4.got2 = bf16[272,128]{1,0:T(8,128)(2,1)S(1)} collective-permute-done((bf16[272,128]{1,0:T(8,128)(2,1)S(1)}, bf16[272,128]{1,0:T(8,128)(2,1)S(1)}, u32[]{:S(2)}, u32[]{:S(2)}) %collective-permute-start.4) | collective-permute-done | bytes 69664 | tf_op jit(solution)/shard_map/ppermute | solution.py:451
  14.8 0.8 %collective-permute-done.5.got3 = bf16[272,128]{1,0:T(8,128)(2,1)S(1)} collective-permute-done((bf16[272,128]{1,0:T(8,128)(2,1)S(1)}, bf16[272,128]{1,0:T(8,128)(2,1)S(1)}, u32[]{:S(2)}, u32[]{:S(2)}) %collective-permute-start.5) | collective-permute-done | bytes 69664 | tf_op jit(solution)/shard_map/ppermute | solution.py:451
  15.6 1.4 %shard_map.169 = (bf16[24,128,256]{2,1,0:T(8,128)(2,1)S(1)}, bf16[24,128,16]{2,1,0:T(8,128)(2,1)S(1)}, bf16[16,16,128]{2,1,0:T(8,128)(2,1)S(1)}, bf16[16,256,128]{2,1,0:T(8,128)(2,1)S(1)}, s32[8,96]{1,0:T(8,128)S(1)}) custom-call(s32[1,2,96]{2,1,0:T(2,128)S(1)} %bitcast.10, s32[1,1]{1,0:T(1,128)} %bitcast.7.count_ref, ...), custom_call_target="tpu_custom_call" | custom-call | flops 1100000000 | bytes 3400000 | tf_op jit(solution)/shard_map/pallas_call | solution.py:435
  16.9 0.9 %collective-permute-done.1 = bf16[368,128]{1,0:T(8,128)(2,1)S(1)} collective-permute-done((bf16[368,128]{1,0:T(8,128)(2,1)S(1)}, bf16[368,128]{1,0:T(8,128)(2,1)S(1)}, u32[]{:S(2)}, u32[]{:S(2)}) %collective-permute-start.1) | collective-permute-done | bytes 94240 | tf_op jit(solution)/shard_map/ppermute | solution.py:451
  17.9 0.2 collective-permute-start.2
  18.0 3.7 %shard_map.170 = (bf16[24,128,256]{2,1,0:T(8,128)(2,1)S(1)}, bf16[24,128,16]{2,1,0:T(8,128)(2,1)S(1)}, f32[17,128,128]{2,1,0:T(8,128)S(1)}, f32[25,128,128]{2,1,...) custom-call(s32[1]{0:T(128)} %bitcast.1.flip_ref, ...), custom_call_target="tpu_custom_call", output_to_operand_aliasing={{0}: (7, {}), {1}: (8, {})} | custom-call | flops 3300000000 | bytes 10200000 | tf_op jit(solution)/shard_map/pallas_call | solution.py:435
  21.8 0.1 collective-permute-start.7
  21.8 1.0 %collective-permute-start.8 = (bf16[256,128]{1,0:T(8,128)(2,1)S(1)}, bf16[256,128]{1,0:T(8,128)(2,1)S(1)}, u32[]{:S(2)}, u32[]{:S(2)}) collective-permute-start(bf16[256,128]{1,0:T(8,128)(2,1)S(1)} %get-tuple-element.56), channel_id=1, source_target_pairs={{0,24},{8,0},{16,8},{24,16},{1,25},{9,1},{17,9},{25,17},{2,26},{10... | collective-permute-start | bytes 196616 | tf_op jit(solution)/shard_map/ppermute | solution.py:451
  22.8 1.1 %collective-permute-start.9 = (bf16[256,128]{1,0:T(8,128)(2,1)S(1)}, bf16[256,128]{1,0:T(8,128)(2,1)S(1)}, u32[]{:S(2)}, u32[]{:S(2)}) collective-permute-start(bf16[256,128]{1,0:T(8,128)(2,1)S(1)} %get-tuple-element.57), channel_id=1, source_target_pairs={{0,8},{8,16},{16,24},{24,0},{1,9},{9,17},{17,25},{25,1},{2,10},{10... | collective-permute-start | bytes 196616 | tf_op jit(solution)/shard_map/ppermute | solution.py:451
  23.9 0.0 collective-permute-done.2
  23.9 0.1 add_convert_fusion.mine_ref
  24.0 0.1 collective-permute-start.6
  24.1 0.0 copy-start
  24.1 0.0 copy-start.1
  24.1 0.0 copy-start.3
  24.1 0.0 copy-start.4
  24.2 3.3 %shard_map.171 = (f32[17,128,128]{2,1,0:T(8,128)S(1)}, f32[25,128,128]{2,1,0:T(8,128)S(1)}) custom-call(s32[8,96]{1,0:T(8,128)S(1)} %get-tuple-element.49.plan_ref, bf16[24,128,256]{2,1,0:T(8,128)(2,1)S(1)} %get-tuple-element.58.proj_ref, bf16[24,128,16]{2,1,0:T(8,128)(2,1)S(1)} %get-tuple-element.59.far_ref, ...), custom_call_target="tpu_custom_call", output_to_operand_aliasing={{0}: (5, {}), {1}: (6, {})} | custom-call | flops 5500000256 | bytes 17000000 | tf_op jit(solution)/shard_map/pallas_call | solution.py:435
  27.5 0.8 %collective-permute-done.9.after3.back3 = bf16[256,128]{1,0:T(8,128)(2,1)S(1)} collective-permute-done((bf16[256,128]{1,0:T(8,128)(2,1)S(1)}, bf16[256,128]{1,0:T(8,128)(2,1)S(1)}, u32[]{:S(2)}, u32[]{:S(2)}) %collective-permute-start.9) | collective-permute-done | bytes 65568 | tf_op jit(solution)/shard_map/ppermute | solution.py:451
  28.3 0.5 %shard_map.172 = (f32[368,128]{1,0:T(8,128)S(1)}, bf16[128,128]{1,0:T(8,128)(2,1)S(1)}, bf16[256,128]{1,0:T(8,128)(2,1)S(1)}, bf16[128,256]{1,0:T(8,128)(2,1)S(1...) custom-call(s32[1]{0:T(128)} %bitcast.1.flip_ref, s32[3,512]{1,0:T(4,128)S(1)} %bitcast.8, ...), custom_call_target="tpu_custom_call" | custom-call | flops 550000000 | bytes 1700000 | tf_op jit(solution)/shard_map/pallas_call | solution.py:435
  28.8 0.0 copy-start.9
  28.8 1.9 %shard_map.173.new_ref = bf16[2048,128]{1,0:T(8,128)(2,1)S(1)} custom-call(bf16[368,128]{1,0:T(8,128)(2,1)S(1)} %add_convert_fusion.mine_ref, bf16[624,128]{1,0:T(8,128)(2,1)S(1)} %collective-permute-done.6.other_ref.back0, f32[368,128]{1,0:T(8,128)S(1)} %get-tuple-element.63.strength_ref, bf16[736,2048]{1,0:T(8,128)(2,1)S(1)} %get-tuple-element.64.trig_ref, ...), custom_call_target="tpu_custom_call" | custom-call | flops 2750000128 | bytes 8500000 | tf_op jit(solution)/shard_map/pallas_call | solution.py:435
  30.7 1.7 %shard_map.174 = (bf16[2048,128]{1,0:T(8,128)(2,1)}, f32[16,128,128]{2,1,0:T(8,128)}, f32[25,128,128]{2,1,0:T(8,128)S(1)}) custom-call(s32[1,2,4]{2,1,0:T(2,128)S(1)} %bitcast.12, s32[1]{0:T(128)} %bitcast.1.flip_ref, bf16[2048,128]{1,0:T(8,128)(2,1)S(1)} %shard_map.173.new_ref, ...), custom_call_target="tpu_custom_call", output_to_operand_aliasing={{2}: (7, {})} | custom-call | flops 1650000000 | bytes 5100000 | tf_op jit(solution)/shard_map/pallas_call | solution.py:435
  (20 shorter events, 0.1 us)
Async XLA Ops:
  1.9 13.6 %copy-start.6 = (bf16[128,128]{1,0:T(8,128)(2,1)S(1)}, bf16[128,128]{1,0:T(8,128)(2,1)}, u32[]{:S(2)}) copy-start(bf16[128,128]{1,0:T(8,128)(2,1)} %wa_ref.3) | copy-start | bytes 98308
  1.9 13.6 %copy-start.7 = (bf16[128,128]{1,0:T(8,128)(2,1)S(1)}, bf16[128,128]{1,0:T(8,128)(2,1)}, u32[]{:S(2)}) copy-start(bf16[128,128]{1,0:T(8,128)(2,1)} %wb_ref.3) | copy-start | bytes 98308
  1.9 13.6 %copy-start.8 = (s32[1,96,2]{1,2,0:T(2,128)S(1)}, s32[1,96,2]{1,2,0:T(2,128)}, u32[]{:S(2)}) copy-start(s32[1,96,2]{1,2,0:T(2,128)} %param.20) | copy-start | bytes 2308
  4.3 8.8 %collective-permute-start = (bf16[640,128]{1,0:T(8,128)(2,1)S(1)}, bf16[640,128]{1,0:T(8,128)(2,1)S(1)}, u32[]{:S(2)}, u32[]{:S(2)}) collective-permute-start(bf16[640,128]{1,0:T(8,128)(2,1)S(1)} %get-tuple-element.44.after_ref), channel_id=1, source_target_pairs={{0,1},{1,0},{2,3},{3,2},{4,5},{5,4},{6,7},{7,6},{8,9},{9,8},{10,11... | collective-permute-start | bytes 491528 | tf_op jit(solution)/shard_map/ppermute | solution.py:451
  4.8 8.4 %collective-permute-start.3 = (bf16[272,128]{1,0:T(8,128)(2,1)S(1)}, bf16[272,128]{1,0:T(8,128)(2,1)S(1)}, u32[]{:S(2)}, u32[]{:S(2)}) collective-permute-start(bf16[272,128]{1,0:T(8,128)(2,1)S(1)} %get-tuple-element.46), channel_id=1, source_target_pairs={{0,7},{1,2},{2,1},{3,4},{4,3},{5,6},{6,5},{7,0},{8,15},{9,10},{10,... | collective-permute-start | bytes 208904 | tf_op jit(solution)/shard_map/ppermute | solution.py:451
  9.5 5.2 %collective-permute-start.4 = (bf16[272,128]{1,0:T(8,128)(2,1)S(1)}, bf16[272,128]{1,0:T(8,128)(2,1)S(1)}, u32[]{:S(2)}, u32[]{:S(2)}) collective-permute-start(bf16[272,128]{1,0:T(8,128)(2,1)S(1)} %get-tuple-element.47), channel_id=1, source_target_pairs={{0,8},{8,16},{16,24},{24,0},{1,9},{9,17},{17,25},{25,1},{2,10},{10... | collective-permute-start | bytes 208904 | tf_op jit(solution)/shard_map/ppermute | solution.py:451
  11.0 4.5 %collective-permute-start.5 = (bf16[272,128]{1,0:T(8,128)(2,1)S(1)}, bf16[272,128]{1,0:T(8,128)(2,1)S(1)}, u32[]{:S(2)}, u32[]{:S(2)}) collective-permute-start(bf16[272,128]{1,0:T(8,128)(2,1)S(1)} %get-tuple-element.48), channel_id=1, source_target_pairs={{0,24},{8,0},{16,8},{24,16},{1,25},{9,1},{17,9},{25,17},{2,26},{10... | collective-permute-start | bytes 208904 | tf_op jit(solution)/shard_map/ppermute | solution.py:451
  13.2 4.6 %collective-permute-start.1 = (bf16[368,128]{1,0:T(8,128)(2,1)S(1)}, bf16[368,128]{1,0:T(8,128)(2,1)S(1)}, u32[]{:S(2)}, u32[]{:S(2)}) collective-permute-start(bf16[368,128]{1,0:T(8,128)(2,1)S(1)} %fusion.after_ref), channel_id=1, source_target_pairs={{0,2},{1,3},{2,0},{3,1},{4,6},{5,7},{6,4},{7,5},{8,10},{9,11},{10,... | collective-permute-start | bytes 282632 | tf_op jit(solution)/shard_map/ppermute | solution.py:451
  17.9 6.1 %collective-permute-start.2 = (bf16[368,128]{1,0:T(8,128)(2,1)S(1)}, bf16[368,128]{1,0:T(8,128)(2,1)S(1)}, u32[]{:S(2)}, u32[]{:S(2)}) collective-permute-start(bf16[368,128]{1,0:T(8,128)(2,1)S(1)} %fusion.1.after_ref), channel_id=1, source_target_pairs={{0,4},{1,5},{2,6},{3,7},{4,0},{5,1},{6,2},{7,3},{8,12},{9,13},{10,... | collective-permute-start | bytes 282632 | tf_op jit(solution)/shard_map/ppermute | solution.py:451
  21.8 5.7 %collective-permute-start.7 = (bf16[256,128]{1,0:T(8,128)(2,1)S(1)}, bf16[256,128]{1,0:T(8,128)(2,1)S(1)}, u32[]{:S(2)}, u32[]{:S(2)}) collective-permute-start(bf16[256,128]{1,0:T(8,128)(2,1)S(1)} %get-tuple-element.55), channel_id=1, source_target_pairs={{0,7},{1,2},{2,1},{3,4},{4,3},{5,6},{6,5},{7,0},{8,15},{9,10},{10,... | collective-permute-start | bytes 196616 | tf_op jit(solution)/shard_map/ppermute | solution.py:451
  21.8 5.7 %collective-permute-start.8 = (bf16[256,128]{1,0:T(8,128)(2,1)S(1)}, bf16[256,128]{1,0:T(8,128)(2,1)S(1)}, u32[]{:S(2)}, u32[]{:S(2)}) collective-permute-start(bf16[256,128]{1,0:T(8,128)(2,1)S(1)} %get-tuple-element.56), channel_id=1, source_target_pairs={{0,24},{8,0},{16,8},{24,16},{1,25},{9,1},{17,9},{25,17},{2,26},{10... | collective-permute-start | bytes 196616 | tf_op jit(solution)/shard_map/ppermute | solution.py:451
  22.8 5.5 %collective-permute-start.9 = (bf16[256,128]{1,0:T(8,128)(2,1)S(1)}, bf16[256,128]{1,0:T(8,128)(2,1)S(1)}, u32[]{:S(2)}, u32[]{:S(2)}) collective-permute-start(bf16[256,128]{1,0:T(8,128)(2,1)S(1)} %get-tuple-element.57), channel_id=1, source_target_pairs={{0,8},{8,16},{16,24},{24,0},{1,9},{9,17},{17,25},{25,1},{2,10},{10... | collective-permute-start | bytes 196616 | tf_op jit(solution)/shard_map/ppermute | solution.py:451
  24.0 4.8 %collective-permute-start.6 = (bf16[624,128]{1,0:T(8,128)(2,1)S(1)}, bf16[624,128]{1,0:T(8,128)(2,1)S(1)}, u32[]{:S(2)}, u32[]{:S(2)}) collective-permute-start(bf16[624,128]{1,0:T(8,128)(2,1)S(1)} %pad_maximum_fusion), channel_id=1, source_target_pairs={{0,1},{1,0},{2,3},{3,2},{4,5},{5,4},{6,7},{7,6},{8,9},{9,8},{10,11... | collective-permute-start | bytes 479240 | tf_op jit(solution)/shard_map/ppermute | solution.py:451
  24.1 4.2 %copy-start = (f32[368,1]{1,0:T(8,128)S(1)}, f32[368,1]{1,0:T(8,128)}, u32[]{:S(2)}) copy-start(f32[368,1]{1,0:T(8,128)} %constant.22.clone.norm2_ref) | copy-start | bytes 4420
  24.1 4.2 %copy-start.1 = (bf16[128,256]{1,0:T(8,128)(2,1)S(1)}, bf16[128,256]{1,0:T(8,128)(2,1)}, u32[]{:S(2)}) copy-start(bf16[128,256]{1,0:T(8,128)(2,1)} %w_in_ref.1) | copy-start | bytes 196612
  24.1 4.2 %copy-start.2 = (bf16[256,128]{1,0:T(8,128)(2,1)S(1)}, bf16[256,128]{1,0:T(8,128)(2,1)}, u32[]{:S(2)}) copy-start(bf16[256,128]{1,0:T(8,128)(2,1)} %w_out_ref.1) | copy-start | bytes 196612
  24.1 4.2 %copy-start.3 = (bf16[128,128]{1,0:T(8,128)(2,1)S(1)}, bf16[128,128]{1,0:T(8,128)(2,1)}, u32[]{:S(2)}) copy-start(bf16[128,128]{1,0:T(8,128)(2,1)} %w_long_ref.1) | copy-start | bytes 98308
  24.1 4.2 %copy-start.4 = (s32[512,3]{0,1:T(4,128)S(1)}, s32[512,3]{0,1:T(4,128)}, u32[]{:S(2)}) copy-start(s32[512,3]{0,1:T(4,128)} %param.22) | copy-start | bytes 18436
  24.2 4.2 %copy-start.5 = (f32[128]{0:T(128)S(1)}, f32[128]{0:T(128)}, u32[]{:S(2)}) copy-start(f32[128]{0:T(128)} %param.27) | copy-start | bytes 1540
  28.8 1.9 %copy-start.9 = (s32[1,4,2]{1,2,0:T(2,128)S(1)}, s32[1,4,2]{1,2,0:T(2,128)}, u32[]{:S(2)}) copy-start(s32[1,4,2]{1,2,0:T(2,128)} %param.19) | copy-start | bytes 100

commit v3 on v2

--- a/solution.py
+++ b/solution.py
@@ -214,31 +214,22 @@
         move = ((iota(1) == place) & here).astype(F32).astype(BF16)
         moved = dot(jnp.concatenate([tiles, tiles, tiles, tiles], axis=0).astype(BF16), move)
         parts += [moved[0:2], jnp.broadcast_to(jnp.sum(chosen, axis=1, keepdims=True), (1, slots))]
-    parts.append(jnp.zeros((2, slots), F32))
-    return jnp.concatenate(parts, axis=0).astype(jnp.int32)
+    return parts
 
 
 def local_kernel(
-    tiles_ref,
-    count_ref,
     feats_ref,
     coords_ref,
     cot_ref,
     wa_ref,
     wb_ref,
-    flip_ref,
-    got1,
-    got2,
-    got3,
     after_ref,
     proj_ref,
     far_ref,
     near_ref,
     cotp_ref,
-    plan_ref,
 ):
     nblk = feats_ref.shape[0] // BLK
-    plan_ref[...] = tile_plan(tiles_ref, count_ref, nblk)
     w_cat = both_transposed(wa_ref, wb_ref)
     w_side = jnp.concatenate([wa_ref[...], wb_ref[...]], axis=0)
     near = dist_rows(coords_ref[...], True).astype(BF16)
@@ -250,8 +241,6 @@
         both = (dot(block(cot_ref, b), w_side, NT) * MSG_SCALE).astype(BF16)
         cotp_ref[b, 0:BLK, :] = both[:, :BLK]
         cotp_ref[b, BLK:, :] = both[:, BLK:]
-    for got, place in zip((got1, got2, got3), (flip_ref[0], 2, 3)):
-        halo_blocks(got, nblk + place * HB, w_cat, proj_ref, far_ref)
 
 
 def tile_part(unroll, row, plan_ref, proj_ref, far_ref, near_ref, cotp_ref, msg_ref, grad_ref):
@@ -259,11 +248,10 @@
     slots = plan_ref.shape[1]
     count = plan_ref[row + 2, 0]
 
-    @pl.loop(0, (count + unroll - 1) // unroll)
-    def _(step):
+    def group(first, width):
         idx = []
-        for u in range(unroll):
-            t = step * unroll + u
+        for u in range(width):
+            t = first + u
             at = jnp.minimum(t, slots - 1)
             i, j, live = plan_ref[row, at], plan_ref[row + 1, at], t < count
             idx.append((i, j, jnp.where(live, i, spare_i), jnp.where(live, j, spare_j)))
@@ -278,11 +266,24 @@
             msg_ref[to_i] += dot(proj_ref[j], jnp.concatenate([ka, kb], axis=0))
             grad_ref[to_j] += dot(jnp.concatenate([ka, kb], axis=1), cotp_ref[i])
 
+    half = unroll // 2
+    whole = (count + half - 1) // unroll
+
+    @pl.loop(0, whole)
+    def _(step):
+        group(step * unroll, unroll)
+
+    @pl.when(count > whole * unroll)
+    def _():
+        group(whole * unroll, half)
+
 
 def tiles_received_kernel(
     unroll,
-    flip_ref,
-    plan_ref,
+    plan_vmem,
+    got2,
+    got3,
+    got1,
     got0,
     wa_ref,
     wb_ref,
@@ -299,14 +300,24 @@
     held1,
     held2,
     held3,
+    plan_ref,
+    sem,
 ):
+    copy = pltpu.make_async_copy(plan_vmem, plan_ref, sem)
+    copy.start()
     nblk = near_ref.shape[0]
-    odd = flip_ref[0]
-    halo_blocks(got0, nblk + (1 - odd) * HB, both_transposed(wa_ref, wb_ref), proj_ref, far_ref)
+    w_cat = both_transposed(wa_ref, wb_ref)
+    for got, place in ((got2, 2), (got3, 3)):
+        halo_blocks(got, nblk + place * HB, w_cat, proj_ref, far_ref)
     msg_ref[...] = jnp.zeros_like(msg_ref)
     grad_ref[...] = jnp.zeros_like(grad_ref)
+    copy.wait()
+    odd = plan_ref[6, 0]
+    places = (1 - odd, odd, 2, 3)
+    for got, place in ((got0, 1 - odd), (got1, odd)):
+        halo_blocks(got, nblk + place * HB, w_cat, proj_ref, far_ref)
     tile_part(unroll, 3, plan_ref, proj_ref, far_ref, near_ref, cotp_ref, msg_ref, grad_ref)
-    for held, place in zip((held0, held1, held2, held3), (1 - odd, odd, 2, 3)):
+    for held, place in zip((held0, held1, held2, held3), places):
         for h in range(HB):
             held[h * BLK : (h + 1) * BLK, :] = grad_ref[nblk + place * HB + h].astype(BF16)
 
@@ -319,7 +330,10 @@
 
 def prepare_kernel(
     group_atoms,
+    lists_ref,
     flip_ref,
+    tiles_ref,
+    count_ref,
     wave_ref,
     norm2_ref,
     w_long_ref,
@@ -327,10 +341,8 @@
     w_in_ref,
     w_out_ref,
     feats_ref,
-    after1,
-    after2,
-    after3,
-    after4,
+    keep_in,
+    after_ref,
     strength_ref,
     w_long_t_ref,
     w_in_t_ref,
@@ -338,7 +350,17 @@
     gain_t_ref,
     feats_t_ref,
     parity_ref,
+    plan_ref,
+    keep_ref,
 ):
+    parts = tile_plan(tiles_ref, count_ref, feats_ref.shape[0] // BLK)
+    lane = lax.broadcasted_iota(jnp.int32, (1, plan_ref.shape[1]), 1)
+    blocks = jnp.zeros(lane.shape, jnp.int32)
+    for direction in range(4):
+        for h in range(HB):
+            blocks = jnp.where(lane == direction * HB + h, lists_ref[0, h, direction], blocks)
+    parts += [jnp.full(lane.shape, flip_ref[0].astype(F32)), blocks.astype(F32)]
+    plan_ref[...] = jnp.concatenate(parts, axis=0).astype(jnp.int32)
     parity_ref[...] = jnp.full(parity_ref.shape, flip_ref[0].astype(F32))
     n = wave_ref[...].astype(F32)
     n0, n1, n2 = n[0:1], n[1:2], n[2:3]
@@ -367,10 +389,14 @@
         feats_t_ref[:, b * BLK : (b + 1) * BLK] = block(feats_ref, b).astype(F32).T.astype(BF16)
 
 
-def update_kernel(
+def finish_kernel(
     chunk,
+    plan_vmem,
     mine_ref,
-    other_ref,
+    back2,
+    back3,
+    back1,
+    back0,
     strength_ref,
     trig_ref,
     feats_t_ref,
@@ -380,11 +406,20 @@
     w_in_t_ref,
     w_out_t_ref,
     parity_ref,
+    grad_in,
+    out_hbm,
+    adjoint_hbm,
+    grad_ref,
     out_ref,
+    plan_ref,
+    sems,
 ):
+    plan_copy = pltpu.make_async_copy(plan_vmem, plan_ref, sems.at[1])
+    plan_copy.start()
+    copies = []
     atoms = feats_t_ref.shape[1]
     a = strength_ref[...] * mine_ref[...].astype(F32)
-    b = strength_ref[...] * other_ref[HB * BLK :, :].astype(F32)
+    b = strength_ref[...] * back0[HB * BLK :, :].astype(F32)
     even = parity_ref[0:1, :] == 0.0
     weighted = jnp.concatenate([jnp.where(even, a, b), jnp.where(even, b, a)], axis=0).astype(BF16)
     mix_w = dot(w_long_t_ref[...], weighted, NT).astype(BF16)
@@ -395,6 +430,16 @@
         at = slice(step * chunk, (step + 1) * chunk)
         msg = jnp.concatenate([msg_ref[step * (chunk // BLK) + i] for i in range(chunk // BLK)], axis=1)
         mixed = dot(mix_w, trig_ref[:, at]) + msg + feats_t_ref[:, at].astype(F32)
+        if step == 0:
+            nblk = adjoint_hbm.shape[0]
+            plan_copy.wait()
+            odd = plan_ref[6, 0]
+            for ref, direction in zip((back0, back1, back2, back3), (odd, 1 - odd, 2, 3)):
+                for h in range(HB):
+                    grad_ref[plan_ref[7, direction * HB + h]] += block(ref, h).astype(F32)
+            copy = pltpu.make_async_copy(grad_ref.at[pl.ds(0, nblk)], adjoint_hbm, sems.at[0])
+            copy.start()
+            copies.append(copy)
         scale = lax.rsqrt(jnp.mean(mixed * mixed, axis=0, keepdims=True) + 1e-06)
         normed = (mixed * scale * gain).astype(BF16)
         pre = dot(w_in_t, normed)
@@ -402,33 +447,12 @@
         hidden = (half * jnp.tanh(half) + half).astype(BF16)
         out = mixed + dot(w_out_t, hidden)
         out_ref[at, :] = out.T.astype(BF16)
-
-
-def finish_kernel(
-    lists_ref,
-    flip_ref,
-    new_ref,
-    back0,
-    back1,
-    back2,
-    back3,
-    grad_in,
-    out_hbm,
-    adjoint_hbm,
-    grad_ref,
-    sems,
-):
-    nblk = adjoint_hbm.shape[0]
-    first = pltpu.make_async_copy(new_ref, out_hbm, sems.at[0])
-    first.start()
-    odd = flip_ref[0]
-    for ref, direction in zip((back0, back1, back2, back3), (odd, 1 - odd, 2, 3)):
-        for h in range(HB):
-            grad_ref[lists_ref[0, h, direction]] += block(ref, h).astype(F32)
-    second = pltpu.make_async_copy(grad_ref.at[pl.ds(0, nblk)], adjoint_hbm, sems.at[1])
-    second.start()
-    first.wait()
-    second.wait()
+        rows = pl.ds(step * chunk, chunk)
+        copy = pltpu.make_async_copy(out_ref.at[rows], out_hbm.at[rows], sems.at[2 + step])
+        copy.start()
+        copies.append(copy)
+    for copy in copies:
+        copy.wait()
 
 
 def call(kernel, outs, args, specs, scratch=(), us=1.0, aliases=None, out_specs=None):
@@ -499,9 +523,9 @@
     )
     feats, coords, msg_cot, table, w_charge = loaded[: len(loads)]
     sent = loaded[len(loads) :]
-    got1 = exchange(sent[1], "dom", far_pair)
     got2 = exchange(sent[2], "group", up)
     got3 = exchange(sent[3], "group", down)
+    got1 = exchange(sent[1], "dom", far_pair)
 
     keep, send, trig = call(
         functools.partial(struct_kernel, 256),
@@ -513,54 +537,10 @@
         (flip, feats, coords, w_charge, table, sent[0]),
         (SMEM,) + (VMEM,) * 5,
         scratch=[VMEM((2 * HALF, width), F32)],
-        us=2.3,
+        us=0.1,
     )
     got0 = exchange(send, "dom", near_pair)
-    total = keep + got0[HB * BLK + COORD_ROWS :].astype(F32)
-    sums = [total.astype(BF16)]
-    step = 2
-    while step < domains:
-        total = total + exchange(sums[-1], "dom", lambda i: i ^ step).astype(F32)
-        sums.append(total.astype(BF16))
-        step *= 2
-
-    proj, far, near, cotp, plan = call(
-        local_kernel,
-        [
-            sds((extent, width, 2 * BLK), BF16),
-            sds((extent, BLK, COORD_ROWS), BF16),
-            sds((nblk, COORD_ROWS, BLK), BF16),
-            sds((nblk, 2 * BLK, width), BF16),
-            sds((8, tiles.shape[1]), jnp.int32),
-        ],
-        (tile_rows, tile_count, feats, coords, msg_cot, w_rad_a, w_rad_b, flip, got1, got2, got3, send),
-        (VMEM,) * 7 + (SMEM,) + (VMEM,) * 3 + (pl.ANY,),
-        us=1.0,
-    )
-    proj, far, msg, grad, *held = call(
-        functools.partial(tiles_received_kernel, unroll),
-        [like(proj), like(far), sds((nblk + 1, width, BLK), F32), sds((extent + 1, BLK, width), F32)]
-        + [sds((HB * BLK, width), BF16)] * 4,
-        (flip, plan, got0, w_rad_a, w_rad_b, near, cotp, proj, far, sums[0]),
-        (SMEM,) * 2 + (VMEM,) * 7 + (pl.ANY,),
-        us=3.0,
-        aliases={7: 0, 8: 1},
-    )
-    msg, grad = call(
-        functools.partial(tiles_own_kernel, unroll),
-        [like(msg), like(grad)],
-        (plan, proj, far, near, cotp, msg, grad, sums[min(1, len(sums) - 1)]),
-        (SMEM,) + (VMEM,) * 6 + (pl.ANY,),
-        us=5.0,
-        aliases={5: 0, 6: 1},
-    )
-    back1 = exchange(held[1], "dom", far_pair)
-    back2 = exchange(held[2], "group", down)
-    back3 = exchange(held[3], "group", up)
-    total = sums[-1]
-    back0 = exchange(jnp.concatenate([held[0], total], axis=0), "dom", near_pair)
-
-    strength, w_long_t, w_in_t, w_out_t, gain_t, feats_t, parity = call(
+    strength, w_long_t, w_in_t, w_out_t, gain_t, feats_t, parity, plan, keep = call(
         functools.partial(prepare_kernel, atoms * domains),
         [
             sds((HALF, width), F32),
@@ -570,26 +550,77 @@
             sds((width, BLK), F32),
             sds((width, atoms), BF16),
             sds((8, width), F32),
+            sds((8, tiles.shape[1]), jnp.int32),
+            like(keep),
         ],
-        (flip, wavevec.T, norm2, w_long, norm_gain.reshape(1, width), w_in, w_out, feats, back1, back2, back3, msg),
-        (SMEM,) + (VMEM,) * 7 + (pl.ANY,) * 4,
-        us=0.5,
-    )
-    (new_feats,) = call(
-        functools.partial(update_kernel, atoms // 2),
-        [sds((atoms, width), BF16)],
-        (total, back0, strength, trig, feats_t, msg, w_long_t, gain_t, w_in_t, w_out_t, parity),
-        (VMEM,) * 11,
-        us=2.5,
-    )
+        (
+            lists, flip, tile_rows, tile_count, wavevec.T, norm2, w_long, norm_gain.reshape(1, width), w_in, w_out,
+            feats, keep, send,
+        ),
+        (SMEM, SMEM) + (VMEM,) * 10 + (pl.ANY,),
+        aliases={11: 8},
+        us=0.1,
+    )
+    total = keep + got0[HB * BLK + COORD_ROWS :].astype(F32)
+    sums = [total.astype(BF16)]
+    step = 2
+    while step < domains:
+        total = total + exchange(sums[-1], "dom", lambda i: i ^ step).astype(F32)
+        sums.append(total.astype(BF16))
+        step *= 2
+
+    proj, far, near, cotp = call(
+        local_kernel,
+        [
+            sds((extent, width, 2 * BLK), BF16),
+            sds((extent, BLK, COORD_ROWS), BF16),
+            sds((nblk, COORD_ROWS, BLK), BF16),
+            sds((nblk, 2 * BLK, width), BF16),
+        ],
+        (feats, coords, msg_cot, w_rad_a, w_rad_b, send),
+        (VMEM,) * 5 + (pl.ANY,),
+        us=0.1,
+    )
+    proj, far, msg, grad, *held = call(
+        functools.partial(tiles_received_kernel, unroll),
+        [like(proj), like(far), sds((nblk + 1, width, BLK), F32), sds((extent + 1, BLK, width), F32)]
+        + [sds((HB * BLK, width), BF16)] * 4,
+        (plan, got2, got3, got1, got0, w_rad_a, w_rad_b, near, cotp, proj, far, sums[0]),
+        (VMEM,) * 11 + (pl.ANY,),
+        scratch=[SMEM(plan.shape, plan.dtype), pltpu.SemaphoreType.DMA],
+        us=3.0,
+        aliases={9: 0, 10: 1},
+    )
+    msg, grad = call(
+        functools.partial(tiles_own_kernel, unroll),
+        [like(msg), like(grad)],
+        (plan, proj, far, near, cotp, msg, grad, sums[min(1, len(sums) - 1)]),
+        (SMEM,) + (VMEM,) * 6 + (pl.ANY,),
+        us=5.0,
+        aliases={5: 0, 6: 1},
+    )
+    back2 = exchange(held[2], "group", down)
+    back3 = exchange(held[3], "group", up)
+    back1 = exchange(held[1], "dom", far_pair)
+    total = sums[-1]
+    back0 = exchange(jnp.concatenate([held[0], total], axis=0), "dom", near_pair)
+
+    chunk = atoms
     new_feats, adjoint, _ = call(
-        finish_kernel,
+        functools.partial(finish_kernel, chunk),
         [sds((atoms, width), BF16), sds((nblk, BLK, width), F32), like(grad)],
-        (lists, flip, new_feats, back0, back1, back2, back3, grad),
-        (SMEM, SMEM) + (VMEM,) * 6,
-        scratch=[pltpu.SemaphoreType.DMA((2,))],
-        us=1.5,
-        aliases={7: 2},
+        (
+            plan, total, back2, back3, back1, back0, strength, trig, feats_t, msg, w_long_t, gain_t,
+            w_in_t, w_out_t, parity, grad,
+        ),
+        (VMEM,) * 16,
+        scratch=[
+            VMEM((atoms, width), BF16),
+            SMEM(plan.shape, plan.dtype),
+            pltpu.SemaphoreType.DMA((2 + atoms // chunk,)),
+        ],
+        us=3.0,
+        aliases={15: 2},
         out_specs=(pltpu.HBM, pltpu.HBM, VMEM),
     )
     return (new_feats, adjoint.reshape(atoms, width))

time: 32.6 us -> 31.5 us (0.966)
  Pallas kernels: 16.1 us -> 13.3 us
  waiting for transfers between devices: 4 us -> 5.25 us
  starting transfers between devices: 10.6 us -> 11.3 us
    pallas_call x8 -> x7, Pallas kernels: 16.1 us -> 13.3 us  [call(): pl.pallas_call(kernel, out_shape=outs, in_specs=[pl.BlockSpec(memory_spac...]
    ppermute x10, waiting for transfers between devices: 4 us -> 5.25 us  [exchange(): lax.ppermute(value, axis, [(i, partner(i) % length) for i in range(length)])]
    ppermute x10, starting transfers between devices: 10.6 us -> 11.3 us  [exchange(): lax.ppermute(value, axis, [(i, partner(i) % length) for i in range(length)])]
  transfers between devices with their start and end apart: 10 -> 10, of which waited for: 4 -> 4; matrix products, arithmetic and copies ran while one was open for 0% -> 0% of each run, Pallas kernels for 27% -> 21%
where the time goes in v3:
time: 31.5 us; the launch traced here: 31.6 us
  Pallas kernels  13.3 us (42%)
  starting transfers between devices  11.3 us (36%)
  waiting for transfers between devices  5.25 us (17%)
  between operations  1.54 us (5%)
    pallas_call x7, Pallas kernels, call(): pl.pallas_call(kernel, out_shape=outs, in_specs=[pl.BlockSpec(memory_spac...  13.3 us
    ppermute x10, starting transfers between devices, exchange(): lax.ppermute(value, axis, [(i, partner(i) % length) for i in range(length)])  11.3 us
    ppermute x10, waiting for transfers between devices, exchange(): lax.ppermute(value, axis, [(i, partner(i) % length) for i in range(length)])  5.25 us
  transfers between devices with their start and end apart: 10, of which 4 were waited for; matrix products, arithmetic and copies ran while one was open for 0% of the time, Pallas kernels for 21%

profile of v3, /device:TPU:0, one launch (start us, length us, event | category | flops | bytes accessed | tf_op | source)
XLA Modules:
  0.0 31.6 jit_solution(9955899997823586860)
XLA Ops:
  0.6 0.0 copy-start
  0.7 1.4 %shard_map.167 = (bf16[2048,128]{1,0:T(8,128)(2,1)S(1)}, bf16[3,2048]{1,0:T(4,128)(2,1)S(1)}, bf16[2048,128]{1,0:T(8,128)(2,1)S(1)}, f32[48,16]{1,0:T(8,128)S(1)...) custom-call(s32[1]{0:T(128)} %bitcast.1.flip_ref, ...), custom_call_target="tpu_custom_call" | custom-call | flops 1320000000 | bytes 4080000 | tf_op jit(solution)/shard_map/pallas_call | solution.py:459
  2.1 0.0 copy-start.3
  2.2 0.0 copy-start.4
  2.2 2.3 %shard_map.168 = (f32[368,128]{1,0:T(8,128)S(1)}, bf16[640,128]{1,0:T(8,128)(2,1)S(1)}, bf16[736,2048]{1,0:T(8,128)(2,1)S(1)}) custom-call(s32[1]{0:T(128)} %bitcast.1.flip_ref, bf16[2048,128]{1,0:T(8,128)(2,1)S(1)} %get-tuple-element.39.feats_ref, bf16[3,2048]{1,0:T(4,128)(2,1)S(1)} %get-tuple-element.40.coords_ref, ...), custom_call_target="tpu_custom_call" | custom-call | flops 110000000 | bytes 340000 | tf_op jit(solution)/shard_map/pallas_call | solution.py:459
  4.5 0.5 %collective-permute-start = (bf16[640,128]{1,0:T(8,128)(2,1)S(1)}, bf16[640,128]{1,0:T(8,128)(2,1)S(1)}, u32[]{:S(2)}, u32[]{:S(2)}) collective-permute-start(bf16[640,128]{1,0:T(8,128)(2,1)S(1)} %get-tuple-element.45.after_ref), channel_id=1, source_target_pairs={{0,1},{1,0},{2,3},{3,2},{4,5},{5,4},{6,7},{7,6},{8,9},{9,8},{10,11... | collective-permute-start | bytes 491528 | tf_op jit(solution)/shard_map/ppermute | solution.py:475
  5.8 1.2 %shard_map.169 = (f32[368,128]{1,0:T(8,128)S(1)}, bf16[128,128]{1,0:T(8,128)(2,1)S(1)}, bf16[256,128]{1,0:T(8,128)(2,1)S(1)}, bf16[128,256]{1,0:T(8,128)(2,1)S(1...) custom-call(s32[1,2,4]{2,1,0:T(2,128)S(1)} %bitcast.10, ...), custom_call_target="tpu_custom_call", output_to_operand_aliasing={{8}: (11, {})} | custom-call | flops 110000000 | bytes 340000 | tf_op jit(solution)/shard_map/pallas_call | solution.py:459
  7.0 0.0 collective-permute-done.got0
  7.0 2.6 %collective-permute-start.1 = (bf16[368,128]{1,0:T(8,128)(2,1)S(1)}, bf16[368,128]{1,0:T(8,128)(2,1)S(1)}, u32[]{:S(2)}, u32[]{:S(2)}) collective-permute-start(bf16[368,128]{1,0:T(8,128)(2,1)S(1)} %fusion.after_ref), channel_id=1, source_target_pairs={{0,2},{1,3},{2,0},{3,1},{4,6},{5,7},{6,4},{7,5},{8,10},{9,11},{10,... | collective-permute-start | bytes 282632 | tf_op jit(solution)/shard_map/ppermute | solution.py:475
  9.7 1.5 %collective-permute-start.3 = (bf16[272,128]{1,0:T(8,128)(2,1)S(1)}, bf16[272,128]{1,0:T(8,128)(2,1)S(1)}, u32[]{:S(2)}, u32[]{:S(2)}) collective-permute-start(bf16[272,128]{1,0:T(8,128)(2,1)S(1)} %get-tuple-element.48), channel_id=1, source_target_pairs={{0,8},{8,16},{16,24},{24,0},{1,9},{9,17},{17,25},{25,1},{2,10},{10... | collective-permute-start | bytes 208904 | tf_op jit(solution)/shard_map/ppermute | solution.py:475
  11.2 1.4 %collective-permute-start.4 = (bf16[272,128]{1,0:T(8,128)(2,1)S(1)}, bf16[272,128]{1,0:T(8,128)(2,1)S(1)}, u32[]{:S(2)}, u32[]{:S(2)}) collective-permute-start(bf16[272,128]{1,0:T(8,128)(2,1)S(1)} %get-tuple-element.49), channel_id=1, source_target_pairs={{0,24},{8,0},{16,8},{24,16},{1,25},{9,1},{17,9},{25,17},{2,26},{10... | collective-permute-start | bytes 208904 | tf_op jit(solution)/shard_map/ppermute | solution.py:475
  12.6 1.7 %collective-permute-start.5 = (bf16[272,128]{1,0:T(8,128)(2,1)S(1)}, bf16[272,128]{1,0:T(8,128)(2,1)S(1)}, u32[]{:S(2)}, u32[]{:S(2)}) collective-permute-start(bf16[272,128]{1,0:T(8,128)(2,1)S(1)} %get-tuple-element.50), channel_id=1, source_target_pairs={{0,7},{1,2},{2,1},{3,4},{4,3},{5,6},{6,5},{7,0},{8,15},{9,10},{10,... | collective-permute-start | bytes 208904 | tf_op jit(solution)/shard_map/ppermute | solution.py:475
  14.3 0.0 copy-done.3
  14.4 0.8 %shard_map.170 = (bf16[24,128,256]{2,1,0:T(8,128)(2,1)S(1)}, bf16[24,128,16]{2,1,0:T(8,128)(2,1)S(1)}, bf16[16,16,128]{2,1,0:T(8,128)(2,1)S(1)}, bf16[16,256,128]{2,1,0:T(8,128)(2,1)S(1)}) custom-call(bf16[2048,128]{1,0:T(8,128)(2,1)S(1)} %get-tuple-element.39.feats_ref, bf16[3,2048]{1,0:T(4,128)(2,1)S(1)} %get-tuple-element.40.coords_ref, ...), custom_call_target="tpu_custom_call" | custom-call | flops 110000000 | bytes 340000 | tf_op jit(solution)/shard_map/pallas_call | solution.py:459
  15.1 0.0 collective-permute-done.1
  15.2 0.9 %collective-permute-start.2 = (bf16[368,128]{1,0:T(8,128)(2,1)S(1)}, bf16[368,128]{1,0:T(8,128)(2,1)S(1)}, u32[]{:S(2)}, u32[]{:S(2)}) collective-permute-start(bf16[368,128]{1,0:T(8,128)(2,1)S(1)} %fusion.1.after_ref), channel_id=1, source_target_pairs={{0,4},{1,5},{2,6},{3,7},{4,0},{5,1},{6,2},{7,3},{8,12},{9,13},{10,... | collective-permute-start | bytes 282632 | tf_op jit(solution)/shard_map/ppermute | solution.py:475
  16.1 0.0 collective-permute-done.3.got2
  16.1 0.3 %collective-permute-done.4.got3 = bf16[272,128]{1,0:T(8,128)(2,1)S(1)} collective-permute-done((bf16[272,128]{1,0:T(8,128)(2,1)S(1)}, bf16[272,128]{1,0:T(8,128)(2,1)S(1)}, u32[]{:S(2)}, u32[]{:S(2)}) %collective-permute-start.4) | collective-permute-done | bytes 69664 | tf_op jit(solution)/shard_map/ppermute | solution.py:475
  16.4 2.4 %collective-permute-done.5.got1 = bf16[272,128]{1,0:T(8,128)(2,1)S(1)} collective-permute-done((bf16[272,128]{1,0:T(8,128)(2,1)S(1)}, bf16[272,128]{1,0:T(8,128)(2,1)S(1)}, u32[]{:S(2)}, u32[]{:S(2)}) %collective-permute-start.5) | collective-permute-done | bytes 69664 | tf_op jit(solution)/shard_map/ppermute | solution.py:475
  18.8 2.3 %shard_map.171 = (bf16[24,128,256]{2,1,0:T(8,128)(2,1)S(1)}, bf16[24,128,16]{2,1,0:T(8,128)(2,1)S(1)}, f32[17,128,128]{2,1,0:T(8,128)S(1)}, f32[25,128,128]{2,1,...) custom-call(s32[8,96]{1,0:T(8,128)S(1)} %get-tuple-element.46.plan_v, ...), custom_call_target="tpu_custom_call", output_to_operand_aliasing={{0}: (9, {}), {1}: (10, {})} | custom-call | flops 3300000000 | bytes 10200000 | tf_op jit(solution)/shard_map/pallas_call | solution.py:459
  21.2 1.6 %collective-permute-start.6 = (bf16[256,128]{1,0:T(8,128)(2,1)S(1)}, bf16[256,128]{1,0:T(8,128)(2,1)S(1)}, u32[]{:S(2)}, u32[]{:S(2)}) collective-permute-start(bf16[256,128]{1,0:T(8,128)(2,1)S(1)} %get-tuple-element.56), channel_id=1, source_target_pairs={{0,24},{8,0},{16,8},{24,16},{1,25},{9,1},{17,9},{25,17},{2,26},{10... | collective-permute-start | bytes 196616 | tf_op jit(solution)/shard_map/ppermute | solution.py:475
  22.8 0.5 %collective-permute-start.7 = (bf16[256,128]{1,0:T(8,128)(2,1)S(1)}, bf16[256,128]{1,0:T(8,128)(2,1)S(1)}, u32[]{:S(2)}, u32[]{:S(2)}) collective-permute-start(bf16[256,128]{1,0:T(8,128)(2,1)S(1)} %get-tuple-element.57), channel_id=1, source_target_pairs={{0,8},{8,16},{16,24},{24,0},{1,9},{9,17},{17,25},{25,1},{2,10},{10... | collective-permute-start | bytes 196616 | tf_op jit(solution)/shard_map/ppermute | solution.py:475
  23.3 0.4 %collective-permute-start.8 = (bf16[256,128]{1,0:T(8,128)(2,1)S(1)}, bf16[256,128]{1,0:T(8,128)(2,1)S(1)}, u32[]{:S(2)}, u32[]{:S(2)}) collective-permute-start(bf16[256,128]{1,0:T(8,128)(2,1)S(1)} %get-tuple-element.58), channel_id=1, source_target_pairs={{0,7},{1,2},{2,1},{3,4},{4,3},{5,6},{6,5},{7,0},{8,15},{9,10},{10,... | collective-permute-start | bytes 196616 | tf_op jit(solution)/shard_map/ppermute | solution.py:475
  23.7 0.0 collective-permute-done.2
  23.7 0.1 add_convert_fusion.mine_ref
  23.7 0.1 collective-permute-start.9
  23.8 2.4 %shard_map.172 = (f32[17,128,128]{2,1,0:T(8,128)S(1)}, f32[25,128,128]{2,1,0:T(8,128)S(1)}) custom-call(s32[8,96]{1,0:T(8,128)S(1)} %get-tuple-element.46.plan_vmem.plan_ref, bf16[24,128,256]{2,1,0:T(8,128)(2,1)S(1)} %get-tuple-element.63.proj_ref, bf16[24,128,16]{2,1,0:T(8,128)(2,1)S(1)} %get-tuple-element.64.far_ref, ...), custom_call_target="tpu_custom_call", output_to_operand_aliasing={{0}: (5, {}), {1}: (6, {})} | custom-call | flops 5500000256 | bytes 17000000 | tf_op jit(solution)/shard_map/pallas_call | solution.py:459
  26.2 0.0 collective-permute-done.6.back2
  26.2 1.7 %collective-permute-done.7.back3 = bf16[256,128]{1,0:T(8,128)(2,1)S(1)} collective-permute-done((bf16[256,128]{1,0:T(8,128)(2,1)S(1)}, bf16[256,128]{1,0:T(8,128)(2,1)S(1)}, u32[]{:S(2)}, u32[]{:S(2)}) %collective-permute-start.7) | collective-permute-done | bytes 65568 | tf_op jit(solution)/shard_map/ppermute | solution.py:475
  27.9 0.8 %collective-permute-done.8.back1 = bf16[256,128]{1,0:T(8,128)(2,1)S(1)} collective-permute-done((bf16[256,128]{1,0:T(8,128)(2,1)S(1)}, bf16[256,128]{1,0:T(8,128)(2,1)S(1)}, u32[]{:S(2)}, u32[]{:S(2)}) %collective-permute-start.8) | collective-permute-done | bytes 65568 | tf_op jit(solution)/shard_map/ppermute | solution.py:475
  28.7 0.0 collective-permute-done.9.back0
  28.7 2.9 %shard_map.173 = (bf16[2048,128]{1,0:T(8,128)(2,1)}, f32[16,128,128]{2,1,0:T(8,128)}, f32[25,128,128]{2,1,0:T(8,128)S(1)}) custom-call(s32[8,96]{1,0:T(8,128)S(1)} %get-tuple-element.46.plan_vmem.plan_ref, bf16[368,128]{1,0:T(8,128)(2,1)S(1)} %add_convert_fusion.mine_ref, ...), custom_call_target="tpu_custom_call", output_to_operand_aliasing={{2}: (15, {})} | custom-call | flops 3300000000 | bytes 10200000 | tf_op jit(solution)/shard_map/pallas_call | solution.py:459
  (19 shorter events, 0.1 us)
Async XLA Ops:
  0.6 5.0 %copy-start = (f32[368,1]{1,0:T(8,128)S(1)}, f32[368,1]{1,0:T(8,128)}, u32[]{:S(2)}) copy-start(f32[368,1]{1,0:T(8,128)} %constant.22.clone.norm2_ref) | copy-start | bytes 4420
  0.7 5.0 %copy-start.1 = (bf16[128,256]{1,0:T(8,128)(2,1)S(1)}, bf16[128,256]{1,0:T(8,128)(2,1)}, u32[]{:S(2)}) copy-start(bf16[128,256]{1,0:T(8,128)(2,1)} %w_in_ref.1) | copy-start | bytes 196612
  0.7 5.0 %copy-start.2 = (bf16[256,128]{1,0:T(8,128)(2,1)S(1)}, bf16[256,128]{1,0:T(8,128)(2,1)}, u32[]{:S(2)}) copy-start(bf16[256,128]{1,0:T(8,128)(2,1)} %w_out_ref.1) | copy-start | bytes 196612
  0.7 5.0 %copy-start.5 = (bf16[128,128]{1,0:T(8,128)(2,1)S(1)}, bf16[128,128]{1,0:T(8,128)(2,1)}, u32[]{:S(2)}) copy-start(bf16[128,128]{1,0:T(8,128)(2,1)} %w_long_ref.1) | copy-start | bytes 98308
  0.7 5.0 %copy-start.6 = (s32[512,3]{0,1:T(4,128)S(1)}, s32[512,3]{0,1:T(4,128)}, u32[]{:S(2)}) copy-start(s32[512,3]{0,1:T(4,128)} %param.22) | copy-start | bytes 18436
  0.7 5.0 %copy-start.7 = (s32[1,4,2]{1,2,0:T(2,128)S(1)}, s32[1,4,2]{1,2,0:T(2,128)}, u32[]{:S(2)}) copy-start(s32[1,4,2]{1,2,0:T(2,128)} %param.19) | copy-start | bytes 100
  0.7 5.0 %copy-start.8 = (s32[1,96,2]{1,2,0:T(2,128)S(1)}, s32[1,96,2]{1,2,0:T(2,128)}, u32[]{:S(2)}) copy-start(s32[1,96,2]{1,2,0:T(2,128)} %param.20) | copy-start | bytes 2308
  0.7 5.0 %copy-start.9 = (f32[128]{0:T(128)S(1)}, f32[128]{0:T(128)}, u32[]{:S(2)}) copy-start(f32[128]{0:T(128)} %param.27) | copy-start | bytes 1540
  2.1 12.2 %copy-start.3 = (bf16[128,128]{1,0:T(8,128)(2,1)S(1)}, bf16[128,128]{1,0:T(8,128)(2,1)}, u32[]{:S(2)}) copy-start(bf16[128,128]{1,0:T(8,128)(2,1)} %wa_ref.3) | copy-start | bytes 98308
  2.2 12.2 %copy-start.4 = (bf16[128,128]{1,0:T(8,128)(2,1)S(1)}, bf16[128,128]{1,0:T(8,128)(2,1)}, u32[]{:S(2)}) copy-start(bf16[128,128]{1,0:T(8,128)(2,1)} %wb_ref.3) | copy-start | bytes 98308
  4.5 2.5 %collective-permute-start = (bf16[640,128]{1,0:T(8,128)(2,1)S(1)}, bf16[640,128]{1,0:T(8,128)(2,1)S(1)}, u32[]{:S(2)}, u32[]{:S(2)}) collective-permute-start(bf16[640,128]{1,0:T(8,128)(2,1)S(1)} %get-tuple-element.45.after_ref), channel_id=1, source_target_pairs={{0,1},{1,0},{2,3},{3,2},{4,5},{5,4},{6,7},{7,6},{8,9},{9,8},{10,11... | collective-permute-start | bytes 491528 | tf_op jit(solution)/shard_map/ppermute | solution.py:475
  7.0 8.1 %collective-permute-start.1 = (bf16[368,128]{1,0:T(8,128)(2,1)S(1)}, bf16[368,128]{1,0:T(8,128)(2,1)S(1)}, u32[]{:S(2)}, u32[]{:S(2)}) collective-permute-start(bf16[368,128]{1,0:T(8,128)(2,1)S(1)} %fusion.after_ref), channel_id=1, source_target_pairs={{0,2},{1,3},{2,0},{3,1},{4,6},{5,7},{6,4},{7,5},{8,10},{9,11},{10,... | collective-permute-start | bytes 282632 | tf_op jit(solution)/shard_map/ppermute | solution.py:475
  9.7 6.4 %collective-permute-start.3 = (bf16[272,128]{1,0:T(8,128)(2,1)S(1)}, bf16[272,128]{1,0:T(8,128)(2,1)S(1)}, u32[]{:S(2)}, u32[]{:S(2)}) collective-permute-start(bf16[272,128]{1,0:T(8,128)(2,1)S(1)} %get-tuple-element.48), channel_id=1, source_target_pairs={{0,8},{8,16},{16,24},{24,0},{1,9},{9,17},{17,25},{25,1},{2,10},{10... | collective-permute-start | bytes 208904 | tf_op jit(solution)/shard_map/ppermute | solution.py:475
  11.2 5.3 %collective-permute-start.4 = (bf16[272,128]{1,0:T(8,128)(2,1)S(1)}, bf16[272,128]{1,0:T(8,128)(2,1)S(1)}, u32[]{:S(2)}, u32[]{:S(2)}) collective-permute-start(bf16[272,128]{1,0:T(8,128)(2,1)S(1)} %get-tuple-element.49), channel_id=1, source_target_pairs={{0,24},{8,0},{16,8},{24,16},{1,25},{9,1},{17,9},{25,17},{2,26},{10... | collective-permute-start | bytes 208904 | tf_op jit(solution)/shard_map/ppermute | solution.py:475
  12.6 6.2 %collective-permute-start.5 = (bf16[272,128]{1,0:T(8,128)(2,1)S(1)}, bf16[272,128]{1,0:T(8,128)(2,1)S(1)}, u32[]{:S(2)}, u32[]{:S(2)}) collective-permute-start(bf16[272,128]{1,0:T(8,128)(2,1)S(1)} %get-tuple-element.50), channel_id=1, source_target_pairs={{0,7},{1,2},{2,1},{3,4},{4,3},{5,6},{6,5},{7,0},{8,15},{9,10},{10,... | collective-permute-start | bytes 208904 | tf_op jit(solution)/shard_map/ppermute | solution.py:475
  15.2 8.5 %collective-permute-start.2 = (bf16[368,128]{1,0:T(8,128)(2,1)S(1)}, bf16[368,128]{1,0:T(8,128)(2,1)S(1)}, u32[]{:S(2)}, u32[]{:S(2)}) collective-permute-start(bf16[368,128]{1,0:T(8,128)(2,1)S(1)} %fusion.1.after_ref), channel_id=1, source_target_pairs={{0,4},{1,5},{2,6},{3,7},{4,0},{5,1},{6,2},{7,3},{8,12},{9,13},{10,... | collective-permute-start | bytes 282632 | tf_op jit(solution)/shard_map/ppermute | solution.py:475
  21.2 5.0 %collective-permute-start.6 = (bf16[256,128]{1,0:T(8,128)(2,1)S(1)}, bf16[256,128]{1,0:T(8,128)(2,1)S(1)}, u32[]{:S(2)}, u32[]{:S(2)}) collective-permute-start(bf16[256,128]{1,0:T(8,128)(2,1)S(1)} %get-tuple-element.56), channel_id=1, source_target_pairs={{0,24},{8,0},{16,8},{24,16},{1,25},{9,1},{17,9},{25,17},{2,26},{10... | collective-permute-start | bytes 196616 | tf_op jit(solution)/shard_map/ppermute | solution.py:475
  22.8 5.2 %collective-permute-start.7 = (bf16[256,128]{1,0:T(8,128)(2,1)S(1)}, bf16[256,128]{1,0:T(8,128)(2,1)S(1)}, u32[]{:S(2)}, u32[]{:S(2)}) collective-permute-start(bf16[256,128]{1,0:T(8,128)(2,1)S(1)} %get-tuple-element.57), channel_id=1, source_target_pairs={{0,8},{8,16},{16,24},{24,0},{1,9},{9,17},{17,25},{25,1},{2,10},{10... | collective-permute-start | bytes 196616 | tf_op jit(solution)/shard_map/ppermute | solution.py:475
  23.3 5.5 %collective-permute-start.8 = (bf16[256,128]{1,0:T(8,128)(2,1)S(1)}, bf16[256,128]{1,0:T(8,128)(2,1)S(1)}, u32[]{:S(2)}, u32[]{:S(2)}) collective-permute-start(bf16[256,128]{1,0:T(8,128)(2,1)S(1)} %get-tuple-element.58), channel_id=1, source_target_pairs={{0,7},{1,2},{2,1},{3,4},{4,3},{5,6},{6,5},{7,0},{8,15},{9,10},{10,... | collective-permute-start | bytes 196616 | tf_op jit(solution)/shard_map/ppermute | solution.py:475
  23.7 5.0 %collective-permute-start.9 = (bf16[624,128]{1,0:T(8,128)(2,1)S(1)}, bf16[624,128]{1,0:T(8,128)(2,1)S(1)}, u32[]{:S(2)}, u32[]{:S(2)}) collective-permute-start(bf16[624,128]{1,0:T(8,128)(2,1)S(1)} %pad_maximum_fusion), channel_id=1, source_target_pairs={{0,1},{1,0},{2,3},{3,2},{4,5},{5,4},{6,7},{7,6},{8,9},{9,8},{10,11... | collective-permute-start | bytes 479240 | tf_op jit(solution)/shard_map/ppermute | solution.py:475

commit v4 on v3

--- a/solution.py
+++ b/solution.py
@@ -206,14 +206,17 @@
     number = lax.broadcasted_iota(jnp.int32, (1, slots), 1)
     live = (number < count_ref[...]).astype(F32)
     own = live * (tiles[1:2] < float(nblk)).astype(F32)
+    sub = lax.broadcasted_iota(jnp.int32, (8, slots), 0)
+    rows = jnp.where(sub == 0, own, jnp.where(sub == 1, live - own, 0.0)).astype(BF16)
+    columns = dot(jnp.concatenate([before, same], axis=0), rows, NT)
+    counts = dot(rows, jnp.ones((slots, slots), BF16))
+    both = jnp.where(sub % 2 == 0, tiles[0:1], tiles[1:2]).astype(BF16)
     parts = []
-    for chosen in (own, live - own):
-        row = jnp.broadcast_to(chosen, (8, slots)).astype(BF16)
-        place = dot(before, row, NT)[:, 0:1].astype(jnp.int32)
-        here = dot(same, row, NT)[:, 0:1] > 0.5
-        move = ((iota(1) == place) & here).astype(F32).astype(BF16)
-        moved = dot(jnp.concatenate([tiles, tiles, tiles, tiles], axis=0).astype(BF16), move)
-        parts += [moved[0:2], jnp.broadcast_to(jnp.sum(chosen, axis=1, keepdims=True), (1, slots))]
+    for k in range(2):
+        place = columns[:slots, k : k + 1].astype(jnp.int32)
+        here = columns[slots:, k : k + 1] > 0.5
+        moved = dot(both, ((iota(1) == place) & here).astype(F32).astype(BF16))
+        parts += [moved[0:2], counts[k : k + 1]]
     return parts
 
 
@@ -330,7 +333,6 @@
 
 def prepare_kernel(
     group_atoms,
-    lists_ref,
     flip_ref,
     tiles_ref,
     count_ref,
@@ -354,12 +356,7 @@
     keep_ref,
 ):
     parts = tile_plan(tiles_ref, count_ref, feats_ref.shape[0] // BLK)
-    lane = lax.broadcasted_iota(jnp.int32, (1, plan_ref.shape[1]), 1)
-    blocks = jnp.zeros(lane.shape, jnp.int32)
-    for direction in range(4):
-        for h in range(HB):
-            blocks = jnp.where(lane == direction * HB + h, lists_ref[0, h, direction], blocks)
-    parts += [jnp.full(lane.shape, flip_ref[0].astype(F32)), blocks.astype(F32)]
+    parts.append(jnp.full((2, plan_ref.shape[1]), flip_ref[0].astype(F32)))
     plan_ref[...] = jnp.concatenate(parts, axis=0).astype(jnp.int32)
     parity_ref[...] = jnp.full(parity_ref.shape, flip_ref[0].astype(F32))
     n = wave_ref[...].astype(F32)
@@ -391,6 +388,7 @@
 
 def finish_kernel(
     chunk,
+    lists_vmem,
     plan_vmem,
     mine_ref,
     back2,
@@ -411,11 +409,16 @@
     adjoint_hbm,
     grad_ref,
     out_ref,
+    lists_ref,
     plan_ref,
     sems,
 ):
-    plan_copy = pltpu.make_async_copy(plan_vmem, plan_ref, sems.at[1])
-    plan_copy.start()
+    scalars = [
+        pltpu.make_async_copy(lists_vmem, lists_ref, sems.at[1]),
+        pltpu.make_async_copy(plan_vmem, plan_ref, sems.at[2]),
+    ]
+    for copy in scalars:
+        copy.start()
     copies = []
     atoms = feats_t_ref.shape[1]
     a = strength_ref[...] * mine_ref[...].astype(F32)
@@ -432,11 +435,12 @@
         mixed = dot(mix_w, trig_ref[:, at]) + msg + feats_t_ref[:, at].astype(F32)
         if step == 0:
             nblk = adjoint_hbm.shape[0]
-            plan_copy.wait()
+            for copy in scalars:
+                copy.wait()
             odd = plan_ref[6, 0]
             for ref, direction in zip((back0, back1, back2, back3), (odd, 1 - odd, 2, 3)):
                 for h in range(HB):
-                    grad_ref[plan_ref[7, direction * HB + h]] += block(ref, h).astype(F32)
+                    grad_ref[lists_ref[0, h, direction]] += block(ref, h).astype(F32)
             copy = pltpu.make_async_copy(grad_ref.at[pl.ds(0, nblk)], adjoint_hbm, sems.at[0])
             copy.start()
             copies.append(copy)
@@ -448,7 +452,7 @@
         out = mixed + dot(w_out_t, hidden)
         out_ref[at, :] = out.T.astype(BF16)
         rows = pl.ds(step * chunk, chunk)
-        copy = pltpu.make_async_copy(out_ref.at[rows], out_hbm.at[rows], sems.at[2 + step])
+        copy = pltpu.make_async_copy(out_ref.at[rows], out_hbm.at[rows], sems.at[3 + step])
         copy.start()
         copies.append(copy)
     for copy in copies:
@@ -554,11 +558,11 @@
             like(keep),
         ],
         (
-            lists, flip, tile_rows, tile_count, wavevec.T, norm2, w_long, norm_gain.reshape(1, width), w_in, w_out,
+            flip, tile_rows, tile_count, wavevec.T, norm2, w_long, norm_gain.reshape(1, width), w_in, w_out,
             feats, keep, send,
         ),
-        (SMEM, SMEM) + (VMEM,) * 10 + (pl.ANY,),
-        aliases={11: 8},
+        (SMEM,) + (VMEM,) * 10 + (pl.ANY,),
+        aliases={10: 8},
         us=0.1,
     )
     total = keep + got0[HB * BLK + COORD_ROWS :].astype(F32)
@@ -610,17 +614,18 @@
         functools.partial(finish_kernel, chunk),
         [sds((atoms, width), BF16), sds((nblk, BLK, width), F32), like(grad)],
         (
-            plan, total, back2, back3, back1, back0, strength, trig, feats_t, msg, w_long_t, gain_t,
+            lists, plan, total, back2, back3, back1, back0, strength, trig, feats_t, msg, w_long_t, gain_t,
             w_in_t, w_out_t, parity, grad,
         ),
-        (VMEM,) * 16,
+        (VMEM,) * 17,
         scratch=[
             VMEM((atoms, width), BF16),
+            SMEM(lists.shape, lists.dtype),
             SMEM(plan.shape, plan.dtype),
-            pltpu.SemaphoreType.DMA((2 + atoms // chunk,)),
+            pltpu.SemaphoreType.DMA((3 + atoms // chunk,)),
         ],
         us=3.0,
-        aliases={15: 2},
+        aliases={16: 2},
         out_specs=(pltpu.HBM, pltpu.HBM, VMEM),
     )
     return (new_feats, adjoint.reshape(atoms, width))

time: 31.5 us -> 31 us (0.984); the launches traced: 31.6 us -> 30.5 us
  Pallas kernels: 13.3 us -> 11 us
  starting transfers between devices: 11.3 us -> 12.2 us
    pallas_call x7, Pallas kernels: 13.3 us -> 11 us  [call(): pl.pallas_call(kernel, out_shape=outs, in_specs=[pl.BlockSpec(memory_spac...]
    ppermute x10, starting transfers between devices: 11.3 us -> 12.2 us  [exchange(): lax.ppermute(value, axis, [(i, partner(i) % length) for i in range(length)])]
  transfers between devices with their start and end apart: 10 -> 10, of which waited for: 4 -> 4; matrix products, arithmetic and copies ran while one was open for 0% -> 0% of each run, Pallas kernels for 21% -> 14%
where the time goes in v4:
time: 31 us; the launch traced here: 30.5 us
  starting transfers between devices  12.2 us (39%)
  Pallas kernels  11 us (35%)
  waiting for transfers between devices  5.51 us (18%)
  between operations  1.53 us (5%)
    ppermute x10, starting transfers between devices, exchange(): lax.ppermute(value, axis, [(i, partner(i) % length) for i in range(length)])  12.2 us
    pallas_call x7, Pallas kernels, call(): pl.pallas_call(kernel, out_shape=outs, in_specs=[pl.BlockSpec(memory_spac...  11 us
    ppermute x10, waiting for transfers between devices, exchange(): lax.ppermute(value, axis, [(i, partner(i) % length) for i in range(length)])  5.51 us
  transfers between devices with their start and end apart: 10, of which 4 were waited for; matrix products, arithmetic and copies ran while one was open for 0% of the time, Pallas kernels for 14%

profile of v4, /device:TPU:0, one launch (start us, length us, event | category | flops | bytes accessed | tf_op | source)
XLA Modules:
  0.0 30.5 jit_solution(10392465253099511544)
XLA Ops:
  0.6 0.0 copy-start
  0.7 1.4 %shard_map.167 = (bf16[2048,128]{1,0:T(8,128)(2,1)S(1)}, bf16[3,2048]{1,0:T(4,128)(2,1)S(1)}, bf16[2048,128]{1,0:T(8,128)(2,1)S(1)}, f32[48,16]{1,0:T(8,128)S(1)...) custom-call(s32[1]{0:T(128)} %bitcast.1.flip_ref, ...), custom_call_target="tpu_custom_call" | custom-call | flops 1320000000 | bytes 4080000 | tf_op jit(solution)/shard_map/pallas_call | solution.py:463
  2.1 0.0 copy-start.4
  2.1 0.0 copy-start.5
  2.2 2.3 %shard_map.168 = (f32[368,128]{1,0:T(8,128)S(1)}, bf16[640,128]{1,0:T(8,128)(2,1)S(1)}, bf16[736,2048]{1,0:T(8,128)(2,1)S(1)}) custom-call(s32[1]{0:T(128)} %bitcast.1.flip_ref, bf16[2048,128]{1,0:T(8,128)(2,1)S(1)} %get-tuple-element.39.feats_ref, bf16[3,2048]{1,0:T(4,128)(2,1)S(1)} %get-tuple-element.40.coords_ref, ...), custom_call_target="tpu_custom_call" | custom-call | flops 110000000 | bytes 340000 | tf_op jit(solution)/shard_map/pallas_call | solution.py:463
  4.5 0.5 %collective-permute-start = (bf16[640,128]{1,0:T(8,128)(2,1)S(1)}, bf16[640,128]{1,0:T(8,128)(2,1)S(1)}, u32[]{:S(2)}, u32[]{:S(2)}) collective-permute-start(bf16[640,128]{1,0:T(8,128)(2,1)S(1)} %get-tuple-element.45.after_ref), channel_id=1, source_target_pairs={{0,1},{1,0},{2,3},{3,2},{4,5},{5,4},{6,7},{7,6},{8,9},{9,8},{10,11... | collective-permute-start | bytes 491528 | tf_op jit(solution)/shard_map/ppermute | solution.py:479
  5.7 0.7 %shard_map.169 = (f32[368,128]{1,0:T(8,128)S(1)}, bf16[128,128]{1,0:T(8,128)(2,1)S(1)}, bf16[256,128]{1,0:T(8,128)(2,1)S(1)}, bf16[128,256]{1,0:T(8,128)(2,1)S(1...) custom-call(s32[1]{0:T(128)} %bitcast.1.flip_ref, ...), custom_call_target="tpu_custom_call", output_to_operand_aliasing={{8}: (10, {})} | custom-call | flops 110000000 | bytes 340000 | tf_op jit(solution)/shard_map/pallas_call | solution.py:463
  6.4 0.0 collective-permute-done.got0
  6.4 2.6 %collective-permute-start.1 = (bf16[368,128]{1,0:T(8,128)(2,1)S(1)}, bf16[368,128]{1,0:T(8,128)(2,1)S(1)}, u32[]{:S(2)}, u32[]{:S(2)}) collective-permute-start(bf16[368,128]{1,0:T(8,128)(2,1)S(1)} %fusion.after_ref), channel_id=1, source_target_pairs={{0,2},{1,3},{2,0},{3,1},{4,6},{5,7},{6,4},{7,5},{8,10},{9,11},{10,... | collective-permute-start | bytes 282632 | tf_op jit(solution)/shard_map/ppermute | solution.py:479
  9.1 1.5 %collective-permute-start.3 = (bf16[272,128]{1,0:T(8,128)(2,1)S(1)}, bf16[272,128]{1,0:T(8,128)(2,1)S(1)}, u32[]{:S(2)}, u32[]{:S(2)}) collective-permute-start(bf16[272,128]{1,0:T(8,128)(2,1)S(1)} %get-tuple-element.48), channel_id=1, source_target_pairs={{0,8},{8,16},{16,24},{24,0},{1,9},{9,17},{17,25},{25,1},{2,10},{10... | collective-permute-start | bytes 208904 | tf_op jit(solution)/shard_map/ppermute | solution.py:479
  10.6 1.4 %collective-permute-start.4 = (bf16[272,128]{1,0:T(8,128)(2,1)S(1)}, bf16[272,128]{1,0:T(8,128)(2,1)S(1)}, u32[]{:S(2)}, u32[]{:S(2)}) collective-permute-start(bf16[272,128]{1,0:T(8,128)(2,1)S(1)} %get-tuple-element.49), channel_id=1, source_target_pairs={{0,24},{8,0},{16,8},{24,16},{1,25},{9,1},{17,9},{25,17},{2,26},{10... | collective-permute-start | bytes 208904 | tf_op jit(solution)/shard_map/ppermute | solution.py:479
  12.0 1.7 %collective-permute-start.5 = (bf16[272,128]{1,0:T(8,128)(2,1)S(1)}, bf16[272,128]{1,0:T(8,128)(2,1)S(1)}, u32[]{:S(2)}, u32[]{:S(2)}) collective-permute-start(bf16[272,128]{1,0:T(8,128)(2,1)S(1)} %get-tuple-element.50), channel_id=1, source_target_pairs={{0,7},{1,2},{2,1},{3,4},{4,3},{5,6},{6,5},{7,0},{8,15},{9,10},{10,... | collective-permute-start | bytes 208904 | tf_op jit(solution)/shard_map/ppermute | solution.py:479
  13.8 0.8 %shard_map.170 = (bf16[24,128,256]{2,1,0:T(8,128)(2,1)S(1)}, bf16[24,128,16]{2,1,0:T(8,128)(2,1)S(1)}, bf16[16,16,128]{2,1,0:T(8,128)(2,1)S(1)}, bf16[16,256,128]{2,1,0:T(8,128)(2,1)S(1)}) custom-call(bf16[2048,128]{1,0:T(8,128)(2,1)S(1)} %get-tuple-element.39.feats_ref, bf16[3,2048]{1,0:T(4,128)(2,1)S(1)} %get-tuple-element.40.coords_ref, ...), custom_call_target="tpu_custom_call" | custom-call | flops 110000000 | bytes 340000 | tf_op jit(solution)/shard_map/pallas_call | solution.py:463
  14.5 0.0 collective-permute-done.1
  14.6 0.9 %collective-permute-start.2 = (bf16[368,128]{1,0:T(8,128)(2,1)S(1)}, bf16[368,128]{1,0:T(8,128)(2,1)S(1)}, u32[]{:S(2)}, u32[]{:S(2)}) collective-permute-start(bf16[368,128]{1,0:T(8,128)(2,1)S(1)} %fusion.1.after_ref), channel_id=1, source_target_pairs={{0,4},{1,5},{2,6},{3,7},{4,0},{5,1},{6,2},{7,3},{8,12},{9,13},{10,... | collective-permute-start | bytes 282632 | tf_op jit(solution)/shard_map/ppermute | solution.py:479
  15.5 0.0 collective-permute-done.3.got2
  15.5 0.3 %collective-permute-done.4.got3 = bf16[272,128]{1,0:T(8,128)(2,1)S(1)} collective-permute-done((bf16[272,128]{1,0:T(8,128)(2,1)S(1)}, bf16[272,128]{1,0:T(8,128)(2,1)S(1)}, u32[]{:S(2)}, u32[]{:S(2)}) %collective-permute-start.4) | collective-permute-done | bytes 69664 | tf_op jit(solution)/shard_map/ppermute | solution.py:479
  15.9 2.4 %collective-permute-done.5.got1 = bf16[272,128]{1,0:T(8,128)(2,1)S(1)} collective-permute-done((bf16[272,128]{1,0:T(8,128)(2,1)S(1)}, bf16[272,128]{1,0:T(8,128)(2,1)S(1)}, u32[]{:S(2)}, u32[]{:S(2)}) %collective-permute-start.5) | collective-permute-done | bytes 69664 | tf_op jit(solution)/shard_map/ppermute | solution.py:479
  18.2 1.8 %shard_map.171 = (bf16[24,128,256]{2,1,0:T(8,128)(2,1)S(1)}, bf16[24,128,16]{2,1,0:T(8,128)(2,1)S(1)}, f32[17,128,128]{2,1,0:T(8,128)S(1)}, f32[25,128,128]{2,1,...) custom-call(s32[8,96]{1,0:T(8,128)S(1)} %get-tuple-element.46.plan_v, ...), custom_call_target="tpu_custom_call", output_to_operand_aliasing={{0}: (9, {}), {1}: (10, {})} | custom-call | flops 3300000000 | bytes 10200000 | tf_op jit(solution)/shard_map/pallas_call | solution.py:463
  20.0 1.6 %collective-permute-start.6 = (bf16[256,128]{1,0:T(8,128)(2,1)S(1)}, bf16[256,128]{1,0:T(8,128)(2,1)S(1)}, u32[]{:S(2)}, u32[]{:S(2)}) collective-permute-start(bf16[256,128]{1,0:T(8,128)(2,1)S(1)} %get-tuple-element.56), channel_id=1, source_target_pairs={{0,24},{8,0},{16,8},{24,16},{1,25},{9,1},{17,9},{25,17},{2,26},{10... | collective-permute-start | bytes 196616 | tf_op jit(solution)/shard_map/ppermute | solution.py:479
  21.6 0.5 %collective-permute-start.7 = (bf16[256,128]{1,0:T(8,128)(2,1)S(1)}, bf16[256,128]{1,0:T(8,128)(2,1)S(1)}, u32[]{:S(2)}, u32[]{:S(2)}) collective-permute-start(bf16[256,128]{1,0:T(8,128)(2,1)S(1)} %get-tuple-element.57), channel_id=1, source_target_pairs={{0,8},{8,16},{16,24},{24,0},{1,9},{9,17},{17,25},{25,1},{2,10},{10... | collective-permute-start | bytes 196616 | tf_op jit(solution)/shard_map/ppermute | solution.py:479
  22.1 1.3 %collective-permute-start.8 = (bf16[256,128]{1,0:T(8,128)(2,1)S(1)}, bf16[256,128]{1,0:T(8,128)(2,1)S(1)}, u32[]{:S(2)}, u32[]{:S(2)}) collective-permute-start(bf16[256,128]{1,0:T(8,128)(2,1)S(1)} %get-tuple-element.58), channel_id=1, source_target_pairs={{0,7},{1,2},{2,1},{3,4},{4,3},{5,6},{6,5},{7,0},{8,15},{9,10},{10,... | collective-permute-start | bytes 196616 | tf_op jit(solution)/shard_map/ppermute | solution.py:479
  23.4 0.0 collective-permute-done.2
  23.4 0.1 add_convert_fusion.mine_ref
  23.5 0.1 collective-permute-start.9
  23.6 0.0 copy-start.9
  23.6 1.2 %shard_map.172 = (f32[17,128,128]{2,1,0:T(8,128)S(1)}, f32[25,128,128]{2,1,0:T(8,128)S(1)}) custom-call(s32[8,96]{1,0:T(8,128)S(1)} %get-tuple-element.46.plan_vmem.plan_ref, bf16[24,128,256]{2,1,0:T(8,128)(2,1)S(1)} %get-tuple-element.63.proj_ref, bf16[24,128,16]{2,1,0:T(8,128)(2,1)S(1)} %get-tuple-element.64.far_ref, ...), custom_call_target="tpu_custom_call", output_to_operand_aliasing={{0}: (5, {}), {1}: (6, {})} | custom-call | flops 5500000256 | bytes 17000000 | tf_op jit(solution)/shard_map/pallas_call | solution.py:463
  24.8 0.0 collective-permute-done.6.back2
  24.8 2.0 %collective-permute-done.7.back3 = bf16[256,128]{1,0:T(8,128)(2,1)S(1)} collective-permute-done((bf16[256,128]{1,0:T(8,128)(2,1)S(1)}, bf16[256,128]{1,0:T(8,128)(2,1)S(1)}, u32[]{:S(2)}, u32[]{:S(2)}) %collective-permute-start.7) | collective-permute-done | bytes 65568 | tf_op jit(solution)/shard_map/ppermute | solution.py:479
  26.8 0.8 %collective-permute-done.8.back1 = bf16[256,128]{1,0:T(8,128)(2,1)S(1)} collective-permute-done((bf16[256,128]{1,0:T(8,128)(2,1)S(1)}, bf16[256,128]{1,0:T(8,128)(2,1)S(1)}, u32[]{:S(2)}, u32[]{:S(2)}) %collective-permute-start.8) | collective-permute-done | bytes 65568 | tf_op jit(solution)/shard_map/ppermute | solution.py:479
  27.6 0.0 collective-permute-done.9.back0
  27.6 2.9 %shard_map.173 = (bf16[2048,128]{1,0:T(8,128)(2,1)}, f32[16,128,128]{2,1,0:T(8,128)}, f32[25,128,128]{2,1,0:T(8,128)S(1)}) custom-call(s32[1,2,4]{2,1,0:T(2,128)S(1)} %bitcast.12, s32[8,96]{1,0:T(8,128)S(1)} %get-tuple-element.46.plan_vmem.plan_ref, bf16[368,128]{1,0:T(8,128)(2,1)S(1)} %add_convert_fusion.mine_ref, ...), custom_call_target="tpu_custom_call", output_to_operand_aliasing={{2}: (16, {})} | custom-call | flops 3300000000 | bytes 10200000 | tf_op jit(solution)/shard_map/pallas_call | solution.py:463
  (19 shorter events, 0.1 us)
Async XLA Ops:
  0.6 5.0 %copy-start = (f32[368,1]{1,0:T(8,128)S(1)}, f32[368,1]{1,0:T(8,128)}, u32[]{:S(2)}) copy-start(f32[368,1]{1,0:T(8,128)} %constant.22.clone.norm2_ref) | copy-start | bytes 4420
  0.7 5.0 %copy-start.1 = (bf16[128,256]{1,0:T(8,128)(2,1)S(1)}, bf16[128,256]{1,0:T(8,128)(2,1)}, u32[]{:S(2)}) copy-start(bf16[128,256]{1,0:T(8,128)(2,1)} %w_in_ref.1) | copy-start | bytes 196612
  0.7 5.0 %copy-start.2 = (bf16[256,128]{1,0:T(8,128)(2,1)S(1)}, bf16[256,128]{1,0:T(8,128)(2,1)}, u32[]{:S(2)}) copy-start(bf16[256,128]{1,0:T(8,128)(2,1)} %w_out_ref.1) | copy-start | bytes 196612
  0.7 5.0 %copy-start.3 = (bf16[128,128]{1,0:T(8,128)(2,1)S(1)}, bf16[128,128]{1,0:T(8,128)(2,1)}, u32[]{:S(2)}) copy-start(bf16[128,128]{1,0:T(8,128)(2,1)} %w_long_ref.1) | copy-start | bytes 98308
  0.7 5.0 %copy-start.6 = (s32[512,3]{0,1:T(4,128)S(1)}, s32[512,3]{0,1:T(4,128)}, u32[]{:S(2)}) copy-start(s32[512,3]{0,1:T(4,128)} %param.22) | copy-start | bytes 18436
  0.7 5.0 %copy-start.7 = (s32[1,96,2]{1,2,0:T(2,128)S(1)}, s32[1,96,2]{1,2,0:T(2,128)}, u32[]{:S(2)}) copy-start(s32[1,96,2]{1,2,0:T(2,128)} %param.20) | copy-start | bytes 2308
  0.7 5.0 %copy-start.8 = (f32[128]{0:T(128)S(1)}, f32[128]{0:T(128)}, u32[]{:S(2)}) copy-start(f32[128]{0:T(128)} %param.27) | copy-start | bytes 1540
  2.1 11.6 %copy-start.4 = (bf16[128,128]{1,0:T(8,128)(2,1)S(1)}, bf16[128,128]{1,0:T(8,128)(2,1)}, u32[]{:S(2)}) copy-start(bf16[128,128]{1,0:T(8,128)(2,1)} %wa_ref.3) | copy-start | bytes 98308
  2.1 11.6 %copy-start.5 = (bf16[128,128]{1,0:T(8,128)(2,1)S(1)}, bf16[128,128]{1,0:T(8,128)(2,1)}, u32[]{:S(2)}) copy-start(bf16[128,128]{1,0:T(8,128)(2,1)} %wb_ref.3) | copy-start | bytes 98308
  4.5 1.9 %collective-permute-start = (bf16[640,128]{1,0:T(8,128)(2,1)S(1)}, bf16[640,128]{1,0:T(8,128)(2,1)S(1)}, u32[]{:S(2)}, u32[]{:S(2)}) collective-permute-start(bf16[640,128]{1,0:T(8,128)(2,1)S(1)} %get-tuple-element.45.after_ref), channel_id=1, source_target_pairs={{0,1},{1,0},{2,3},{3,2},{4,5},{5,4},{6,7},{7,6},{8,9},{9,8},{10,11... | collective-permute-start | bytes 491528 | tf_op jit(solution)/shard_map/ppermute | solution.py:479
  6.4 8.1 %collective-permute-start.1 = (bf16[368,128]{1,0:T(8,128)(2,1)S(1)}, bf16[368,128]{1,0:T(8,128)(2,1)S(1)}, u32[]{:S(2)}, u32[]{:S(2)}) collective-permute-start(bf16[368,128]{1,0:T(8,128)(2,1)S(1)} %fusion.after_ref), channel_id=1, source_target_pairs={{0,2},{1,3},{2,0},{3,1},{4,6},{5,7},{6,4},{7,5},{8,10},{9,11},{10,... | collective-permute-start | bytes 282632 | tf_op jit(solution)/shard_map/ppermute | solution.py:479
  9.1 6.4 %collective-permute-start.3 = (bf16[272,128]{1,0:T(8,128)(2,1)S(1)}, bf16[272,128]{1,0:T(8,128)(2,1)S(1)}, u32[]{:S(2)}, u32[]{:S(2)}) collective-permute-start(bf16[272,128]{1,0:T(8,128)(2,1)S(1)} %get-tuple-element.48), channel_id=1, source_target_pairs={{0,8},{8,16},{16,24},{24,0},{1,9},{9,17},{17,25},{25,1},{2,10},{10... | collective-permute-start | bytes 208904 | tf_op jit(solution)/shard_map/ppermute | solution.py:479
  10.6 5.3 %collective-permute-start.4 = (bf16[272,128]{1,0:T(8,128)(2,1)S(1)}, bf16[272,128]{1,0:T(8,128)(2,1)S(1)}, u32[]{:S(2)}, u32[]{:S(2)}) collective-permute-start(bf16[272,128]{1,0:T(8,128)(2,1)S(1)} %get-tuple-element.49), channel_id=1, source_target_pairs={{0,24},{8,0},{16,8},{24,16},{1,25},{9,1},{17,9},{25,17},{2,26},{10... | collective-permute-start | bytes 208904 | tf_op jit(solution)/shard_map/ppermute | solution.py:479
  12.0 6.2 %collective-permute-start.5 = (bf16[272,128]{1,0:T(8,128)(2,1)S(1)}, bf16[272,128]{1,0:T(8,128)(2,1)S(1)}, u32[]{:S(2)}, u32[]{:S(2)}) collective-permute-start(bf16[272,128]{1,0:T(8,128)(2,1)S(1)} %get-tuple-element.50), channel_id=1, source_target_pairs={{0,7},{1,2},{2,1},{3,4},{4,3},{5,6},{6,5},{7,0},{8,15},{9,10},{10,... | collective-permute-start | bytes 208904 | tf_op jit(solution)/shard_map/ppermute | solution.py:479
  14.6 8.8 %collective-permute-start.2 = (bf16[368,128]{1,0:T(8,128)(2,1)S(1)}, bf16[368,128]{1,0:T(8,128)(2,1)S(1)}, u32[]{:S(2)}, u32[]{:S(2)}) collective-permute-start(bf16[368,128]{1,0:T(8,128)(2,1)S(1)} %fusion.1.after_ref), channel_id=1, source_target_pairs={{0,4},{1,5},{2,6},{3,7},{4,0},{5,1},{6,2},{7,3},{8,12},{9,13},{10,... | collective-permute-start | bytes 282632 | tf_op jit(solution)/shard_map/ppermute | solution.py:479
  20.0 4.8 %collective-permute-start.6 = (bf16[256,128]{1,0:T(8,128)(2,1)S(1)}, bf16[256,128]{1,0:T(8,128)(2,1)S(1)}, u32[]{:S(2)}, u32[]{:S(2)}) collective-permute-start(bf16[256,128]{1,0:T(8,128)(2,1)S(1)} %get-tuple-element.56), channel_id=1, source_target_pairs={{0,24},{8,0},{16,8},{24,16},{1,25},{9,1},{17,9},{25,17},{2,26},{10... | collective-permute-start | bytes 196616 | tf_op jit(solution)/shard_map/ppermute | solution.py:479
  21.6 5.2 %collective-permute-start.7 = (bf16[256,128]{1,0:T(8,128)(2,1)S(1)}, bf16[256,128]{1,0:T(8,128)(2,1)S(1)}, u32[]{:S(2)}, u32[]{:S(2)}) collective-permute-start(bf16[256,128]{1,0:T(8,128)(2,1)S(1)} %get-tuple-element.57), channel_id=1, source_target_pairs={{0,8},{8,16},{16,24},{24,0},{1,9},{9,17},{17,25},{25,1},{2,10},{10... | collective-permute-start | bytes 196616 | tf_op jit(solution)/shard_map/ppermute | solution.py:479
  22.1 5.5 %collective-permute-start.8 = (bf16[256,128]{1,0:T(8,128)(2,1)S(1)}, bf16[256,128]{1,0:T(8,128)(2,1)S(1)}, u32[]{:S(2)}, u32[]{:S(2)}) collective-permute-start(bf16[256,128]{1,0:T(8,128)(2,1)S(1)} %get-tuple-element.58), channel_id=1, source_target_pairs={{0,7},{1,2},{2,1},{3,4},{4,3},{5,6},{6,5},{7,0},{8,15},{9,10},{10,... | collective-permute-start | bytes 196616 | tf_op jit(solution)/shard_map/ppermute | solution.py:479
  23.5 4.1 %collective-permute-start.9 = (bf16[624,128]{1,0:T(8,128)(2,1)S(1)}, bf16[624,128]{1,0:T(8,128)(2,1)S(1)}, u32[]{:S(2)}, u32[]{:S(2)}) collective-permute-start(bf16[624,128]{1,0:T(8,128)(2,1)S(1)} %pad_maximum_fusion), channel_id=1, source_target_pairs={{0,1},{1,0},{2,3},{3,2},{4,5},{5,4},{6,7},{7,6},{8,9},{9,8},{10,11... | collective-permute-start | bytes 479240 | tf_op jit(solution)/shard_map/ppermute | solution.py:479
  23.6 4.0 %copy-start.9 = (s32[1,4,2]{1,2,0:T(2,128)S(1)}, s32[1,4,2]{1,2,0:T(2,128)}, u32[]{:S(2)}) copy-start(s32[1,4,2]{1,2,0:T(2,128)} %param.19) | copy-start | bytes 100

commit v5 on v4

--- a/solution.py
+++ b/solution.py
@@ -284,9 +284,9 @@
 def tiles_received_kernel(
     unroll,
     plan_vmem,
+    got1,
     got2,
     got3,
-    got1,
     got0,
     wa_ref,
     wb_ref,
@@ -589,7 +589,7 @@
         functools.partial(tiles_received_kernel, unroll),
         [like(proj), like(far), sds((nblk + 1, width, BLK), F32), sds((extent + 1, BLK, width), F32)]
         + [sds((HB * BLK, width), BF16)] * 4,
-        (plan, got2, got3, got1, got0, w_rad_a, w_rad_b, near, cotp, proj, far, sums[0]),
+        (plan, got1, got2, got3, got0, w_rad_a, w_rad_b, near, cotp, proj, far, sums[0]),
         (VMEM,) * 11 + (pl.ANY,),
         scratch=[SMEM(plan.shape, plan.dtype), pltpu.SemaphoreType.DMA],
         us=3.0,

time: 31 us -> 30.4 us (0.981); the launches traced: 30.5 us -> 30.5 us
  waiting for transfers between devices: 5.51 us -> 3.45 us
  starting transfers between devices: 12.2 us -> 13.4 us
  Pallas kernels: 11 us -> 11.9 us
    ppermute x10, waiting for transfers between devices: 5.51 us -> 3.45 us  [exchange(): lax.ppermute(value, axis, [(i, partner(i) % length) for i in range(length)])]
    ppermute x10, starting transfers between devices: 12.2 us -> 13.4 us  [exchange(): lax.ppermute(value, axis, [(i, partner(i) % length) for i in range(length)])]
    pallas_call x7, Pallas kernels: 11 us -> 11.9 us  [call(): pl.pallas_call(kernel, out_shape=outs, in_specs=[pl.BlockSpec(memory_spac...]
  transfers between devices with their start and end apart: 10 -> 10, of which waited for: 4 -> 4; matrix products, arithmetic and copies ran while one was open for 0% -> 0% of each run, Pallas kernels for 14% -> 17%
where the time goes in v5:
time: 30.4 us; the launch traced here: 30.5 us
  starting transfers between devices  13.4 us (44%)
  Pallas kernels  11.9 us (39%)
  waiting for transfers between devices  3.45 us (11%)
  between operations  1.52 us (5%)
    ppermute x10, starting transfers between devices, exchange(): lax.ppermute(value, axis, [(i, partner(i) % length) for i in range(length)])  13.4 us
    pallas_call x7, Pallas kernels, call(): pl.pallas_call(kernel, out_shape=outs, in_specs=[pl.BlockSpec(memory_spac...  11.9 us
    ppermute x10, waiting for transfers between devices, exchange(): lax.ppermute(value, axis, [(i, partner(i) % length) for i in range(length)])  3.45 us
  transfers between devices with their start and end apart: 10, of which 4 were waited for; matrix products, arithmetic and copies ran while one was open for 0% of the time, Pallas kernels for 17%

profile of v5, /device:TPU:0, one launch (start us, length us, event | category | flops | bytes accessed | tf_op | source)
XLA Modules:
  0.0 30.5 jit_solution(15814762683954177212)
XLA Ops:
  0.6 0.0 copy-start
  0.7 0.0 copy-start.1
  0.7 1.4 %shard_map.167 = (bf16[2048,128]{1,0:T(8,128)(2,1)S(1)}, bf16[3,2048]{1,0:T(4,128)(2,1)S(1)}, bf16[2048,128]{1,0:T(8,128)(2,1)S(1)}, f32[48,16]{1,0:T(8,128)S(1)...) custom-call(s32[1]{0:T(128)} %bitcast.1.flip_ref, ...), custom_call_target="tpu_custom_call" | custom-call | flops 1320000000 | bytes 4080000 | tf_op jit(solution)/shard_map/pallas_call | solution.py:463
  2.1 0.0 copy-start.4
  2.1 0.0 copy-start.5
  2.2 2.3 %shard_map.168 = (f32[368,128]{1,0:T(8,128)S(1)}, bf16[640,128]{1,0:T(8,128)(2,1)S(1)}, bf16[736,2048]{1,0:T(8,128)(2,1)S(1)}) custom-call(s32[1]{0:T(128)} %bitcast.1.flip_ref, bf16[2048,128]{1,0:T(8,128)(2,1)S(1)} %get-tuple-element.39.feats_ref, bf16[3,2048]{1,0:T(4,128)(2,1)S(1)} %get-tuple-element.40.coords_ref, ...), custom_call_target="tpu_custom_call" | custom-call | flops 110000000 | bytes 340000 | tf_op jit(solution)/shard_map/pallas_call | solution.py:463
  4.5 0.5 %collective-permute-start = (bf16[640,128]{1,0:T(8,128)(2,1)S(1)}, bf16[640,128]{1,0:T(8,128)(2,1)S(1)}, u32[]{:S(2)}, u32[]{:S(2)}) collective-permute-start(bf16[640,128]{1,0:T(8,128)(2,1)S(1)} %get-tuple-element.45.after_ref), channel_id=1, source_target_pairs={{0,1},{1,0},{2,3},{3,2},{4,5},{5,4},{6,7},{7,6},{8,9},{9,8},{10,11... | collective-permute-start | bytes 491528 | tf_op jit(solution)/shard_map/ppermute | solution.py:479
  5.7 0.7 %shard_map.169 = (f32[368,128]{1,0:T(8,128)S(1)}, bf16[128,128]{1,0:T(8,128)(2,1)S(1)}, bf16[256,128]{1,0:T(8,128)(2,1)S(1)}, bf16[128,256]{1,0:T(8,128)(2,1)S(1...) custom-call(s32[1]{0:T(128)} %bitcast.1.flip_ref, ...), custom_call_target="tpu_custom_call", output_to_operand_aliasing={{8}: (10, {})} | custom-call | flops 110000000 | bytes 340000 | tf_op jit(solution)/shard_map/pallas_call | solution.py:463
  6.4 0.0 collective-permute-done.got0
  6.4 2.6 %collective-permute-start.1 = (bf16[368,128]{1,0:T(8,128)(2,1)S(1)}, bf16[368,128]{1,0:T(8,128)(2,1)S(1)}, u32[]{:S(2)}, u32[]{:S(2)}) collective-permute-start(bf16[368,128]{1,0:T(8,128)(2,1)S(1)} %fusion.after_ref), channel_id=1, source_target_pairs={{0,2},{1,3},{2,0},{3,1},{4,6},{5,7},{6,4},{7,5},{8,10},{9,11},{10,... | collective-permute-start | bytes 282632 | tf_op jit(solution)/shard_map/ppermute | solution.py:479
  9.1 2.3 %collective-permute-start.3 = (bf16[272,128]{1,0:T(8,128)(2,1)S(1)}, bf16[272,128]{1,0:T(8,128)(2,1)S(1)}, u32[]{:S(2)}, u32[]{:S(2)}) collective-permute-start(bf16[272,128]{1,0:T(8,128)(2,1)S(1)} %get-tuple-element.48), channel_id=1, source_target_pairs={{0,7},{1,2},{2,1},{3,4},{4,3},{5,6},{6,5},{7,0},{8,15},{9,10},{10,... | collective-permute-start | bytes 208904 | tf_op jit(solution)/shard_map/ppermute | solution.py:479
  11.4 1.5 %collective-permute-start.4 = (bf16[272,128]{1,0:T(8,128)(2,1)S(1)}, bf16[272,128]{1,0:T(8,128)(2,1)S(1)}, u32[]{:S(2)}, u32[]{:S(2)}) collective-permute-start(bf16[272,128]{1,0:T(8,128)(2,1)S(1)} %get-tuple-element.49), channel_id=1, source_target_pairs={{0,8},{8,16},{16,24},{24,0},{1,9},{9,17},{17,25},{25,1},{2,10},{10... | collective-permute-start | bytes 208904 | tf_op jit(solution)/shard_map/ppermute | solution.py:479
  12.9 1.4 %collective-permute-start.5 = (bf16[272,128]{1,0:T(8,128)(2,1)S(1)}, bf16[272,128]{1,0:T(8,128)(2,1)S(1)}, u32[]{:S(2)}, u32[]{:S(2)}) collective-permute-start(bf16[272,128]{1,0:T(8,128)(2,1)S(1)} %get-tuple-element.50), channel_id=1, source_target_pairs={{0,24},{8,0},{16,8},{24,16},{1,25},{9,1},{17,9},{25,17},{2,26},{10... | collective-permute-start | bytes 208904 | tf_op jit(solution)/shard_map/ppermute | solution.py:479
  14.3 0.8 %shard_map.170 = (bf16[24,128,256]{2,1,0:T(8,128)(2,1)S(1)}, bf16[24,128,16]{2,1,0:T(8,128)(2,1)S(1)}, bf16[16,16,128]{2,1,0:T(8,128)(2,1)S(1)}, bf16[16,256,128]{2,1,0:T(8,128)(2,1)S(1)}) custom-call(bf16[2048,128]{1,0:T(8,128)(2,1)S(1)} %get-tuple-element.39.feats_ref, bf16[3,2048]{1,0:T(4,128)(2,1)S(1)} %get-tuple-element.40.coords_ref, ...), custom_call_target="tpu_custom_call" | custom-call | flops 110000000 | bytes 340000 | tf_op jit(solution)/shard_map/pallas_call | solution.py:463
  15.1 0.0 collective-permute-done.1
  15.1 0.6 %collective-permute-start.2 = (bf16[368,128]{1,0:T(8,128)(2,1)S(1)}, bf16[368,128]{1,0:T(8,128)(2,1)S(1)}, u32[]{:S(2)}, u32[]{:S(2)}) collective-permute-start(bf16[368,128]{1,0:T(8,128)(2,1)S(1)} %fusion.1.after_ref), channel_id=1, source_target_pairs={{0,4},{1,5},{2,6},{3,7},{4,0},{5,1},{6,2},{7,3},{8,12},{9,13},{10,... | collective-permute-start | bytes 282632 | tf_op jit(solution)/shard_map/ppermute | solution.py:479
  15.7 0.0 collective-permute-done.3.got1
  15.8 0.8 %collective-permute-done.4.got2 = bf16[272,128]{1,0:T(8,128)(2,1)S(1)} collective-permute-done((bf16[272,128]{1,0:T(8,128)(2,1)S(1)}, bf16[272,128]{1,0:T(8,128)(2,1)S(1)}, u32[]{:S(2)}, u32[]{:S(2)}) %collective-permute-start.4) | collective-permute-done | bytes 69664 | tf_op jit(solution)/shard_map/ppermute | solution.py:479
  16.6 0.8 %collective-permute-done.5.got3 = bf16[272,128]{1,0:T(8,128)(2,1)S(1)} collective-permute-done((bf16[272,128]{1,0:T(8,128)(2,1)S(1)}, bf16[272,128]{1,0:T(8,128)(2,1)S(1)}, u32[]{:S(2)}, u32[]{:S(2)}) %collective-permute-start.5) | collective-permute-done | bytes 69664 | tf_op jit(solution)/shard_map/ppermute | solution.py:479
  17.4 1.8 %shard_map.171 = (bf16[24,128,256]{2,1,0:T(8,128)(2,1)S(1)}, bf16[24,128,16]{2,1,0:T(8,128)(2,1)S(1)}, f32[17,128,128]{2,1,0:T(8,128)S(1)}, f32[25,128,128]{2,1,...) custom-call(s32[8,96]{1,0:T(8,128)S(1)} %get-tuple-element.46.plan_v, ...), custom_call_target="tpu_custom_call", output_to_operand_aliasing={{0}: (9, {}), {1}: (10, {})} | custom-call | flops 3300000000 | bytes 10200000 | tf_op jit(solution)/shard_map/pallas_call | solution.py:463
  19.2 2.2 %collective-permute-start.6 = (bf16[256,128]{1,0:T(8,128)(2,1)S(1)}, bf16[256,128]{1,0:T(8,128)(2,1)S(1)}, u32[]{:S(2)}, u32[]{:S(2)}) collective-permute-start(bf16[256,128]{1,0:T(8,128)(2,1)S(1)} %get-tuple-element.56), channel_id=1, source_target_pairs={{0,24},{8,0},{16,8},{24,16},{1,25},{9,1},{17,9},{25,17},{2,26},{10... | collective-permute-start | bytes 196616 | tf_op jit(solution)/shard_map/ppermute | solution.py:479
  21.4 0.7 %collective-permute-start.7 = (bf16[256,128]{1,0:T(8,128)(2,1)S(1)}, bf16[256,128]{1,0:T(8,128)(2,1)S(1)}, u32[]{:S(2)}, u32[]{:S(2)}) collective-permute-start(bf16[256,128]{1,0:T(8,128)(2,1)S(1)} %get-tuple-element.57), channel_id=1, source_target_pairs={{0,8},{8,16},{16,24},{24,0},{1,9},{9,17},{17,25},{25,1},{2,10},{10... | collective-permute-start | bytes 196616 | tf_op jit(solution)/shard_map/ppermute | solution.py:479
  22.1 0.6 %collective-permute-start.8 = (bf16[256,128]{1,0:T(8,128)(2,1)S(1)}, bf16[256,128]{1,0:T(8,128)(2,1)S(1)}, u32[]{:S(2)}, u32[]{:S(2)}) collective-permute-start(bf16[256,128]{1,0:T(8,128)(2,1)S(1)} %get-tuple-element.58), channel_id=1, source_target_pairs={{0,7},{1,2},{2,1},{3,4},{4,3},{5,6},{6,5},{7,0},{8,15},{9,10},{10,... | collective-permute-start | bytes 196616 | tf_op jit(solution)/shard_map/ppermute | solution.py:479
  22.7 0.0 collective-permute-done.2
  22.7 0.1 add_convert_fusion.mine_ref
  22.7 1.0 %collective-permute-start.9 = (bf16[624,128]{1,0:T(8,128)(2,1)S(1)}, bf16[624,128]{1,0:T(8,128)(2,1)S(1)}, u32[]{:S(2)}, u32[]{:S(2)}) collective-permute-start(bf16[624,128]{1,0:T(8,128)(2,1)S(1)} %pad_maximum_fusion), channel_id=1, source_target_pairs={{0,1},{1,0},{2,3},{3,2},{4,5},{5,4},{6,7},{7,6},{8,9},{9,8},{10,11... | collective-permute-start | bytes 479240 | tf_op jit(solution)/shard_map/ppermute | solution.py:479
  23.7 2.1 %shard_map.172 = (f32[17,128,128]{2,1,0:T(8,128)S(1)}, f32[25,128,128]{2,1,0:T(8,128)S(1)}) custom-call(s32[8,96]{1,0:T(8,128)S(1)} %get-tuple-element.46.plan_vmem.plan_ref, bf16[24,128,256]{2,1,0:T(8,128)(2,1)S(1)} %get-tuple-element.63.proj_ref, bf16[24,128,16]{2,1,0:T(8,128)(2,1)S(1)} %get-tuple-element.64.far_ref, ...), custom_call_target="tpu_custom_call", output_to_operand_aliasing={{0}: (5, {}), {1}: (6, {})} | custom-call | flops 5500000256 | bytes 17000000 | tf_op jit(solution)/shard_map/pallas_call | solution.py:463
  25.8 0.0 collective-permute-done.6.back2
  25.8 0.7 %collective-permute-done.7.back3 = bf16[256,128]{1,0:T(8,128)(2,1)S(1)} collective-permute-done((bf16[256,128]{1,0:T(8,128)(2,1)S(1)}, bf16[256,128]{1,0:T(8,128)(2,1)S(1)}, u32[]{:S(2)}, u32[]{:S(2)}) %collective-permute-start.7) | collective-permute-done | bytes 65568 | tf_op jit(solution)/shard_map/ppermute | solution.py:479
  26.5 1.0 %collective-permute-done.8.back1 = bf16[256,128]{1,0:T(8,128)(2,1)S(1)} collective-permute-done((bf16[256,128]{1,0:T(8,128)(2,1)S(1)}, bf16[256,128]{1,0:T(8,128)(2,1)S(1)}, u32[]{:S(2)}, u32[]{:S(2)}) %collective-permute-start.8) | collective-permute-done | bytes 65568 | tf_op jit(solution)/shard_map/ppermute | solution.py:479
  27.6 0.0 collective-permute-done.9.back0
  27.6 2.9 %shard_map.173 = (bf16[2048,128]{1,0:T(8,128)(2,1)}, f32[16,128,128]{2,1,0:T(8,128)}, f32[25,128,128]{2,1,0:T(8,128)S(1)}) custom-call(s32[1,2,4]{2,1,0:T(2,128)S(1)} %bitcast.12, s32[8,96]{1,0:T(8,128)S(1)} %get-tuple-element.46.plan_vmem.plan_ref, bf16[368,128]{1,0:T(8,128)(2,1)S(1)} %add_convert_fusion.mine_ref, ...), custom_call_target="tpu_custom_call", output_to_operand_aliasing={{2}: (16, {})} | custom-call | flops 3300000000 | bytes 10200000 | tf_op jit(solution)/shard_map/pallas_call | solution.py:463
  (19 shorter events, 0.1 us)
Async XLA Ops:
  0.6 5.0 %copy-start = (f32[368,1]{1,0:T(8,128)S(1)}, f32[368,1]{1,0:T(8,128)}, u32[]{:S(2)}) copy-start(f32[368,1]{1,0:T(8,128)} %constant.22.clone.norm2_ref) | copy-start | bytes 4420
  0.7 5.0 %copy-start.1 = (bf16[128,256]{1,0:T(8,128)(2,1)S(1)}, bf16[128,256]{1,0:T(8,128)(2,1)}, u32[]{:S(2)}) copy-start(bf16[128,256]{1,0:T(8,128)(2,1)} %w_in_ref.1) | copy-start | bytes 196612
  0.7 5.0 %copy-start.2 = (bf16[256,128]{1,0:T(8,128)(2,1)S(1)}, bf16[256,128]{1,0:T(8,128)(2,1)}, u32[]{:S(2)}) copy-start(bf16[256,128]{1,0:T(8,128)(2,1)} %w_out_ref.1) | copy-start | bytes 196612
  0.7 5.0 %copy-start.3 = (bf16[128,128]{1,0:T(8,128)(2,1)S(1)}, bf16[128,128]{1,0:T(8,128)(2,1)}, u32[]{:S(2)}) copy-start(bf16[128,128]{1,0:T(8,128)(2,1)} %w_long_ref.1) | copy-start | bytes 98308
  0.7 5.0 %copy-start.6 = (s32[512,3]{0,1:T(4,128)S(1)}, s32[512,3]{0,1:T(4,128)}, u32[]{:S(2)}) copy-start(s32[512,3]{0,1:T(4,128)} %param.22) | copy-start | bytes 18436
  0.7 5.0 %copy-start.7 = (s32[1,96,2]{1,2,0:T(2,128)S(1)}, s32[1,96,2]{1,2,0:T(2,128)}, u32[]{:S(2)}) copy-start(s32[1,96,2]{1,2,0:T(2,128)} %param.20) | copy-start | bytes 2308
  0.7 5.0 %copy-start.8 = (f32[128]{0:T(128)S(1)}, f32[128]{0:T(128)}, u32[]{:S(2)}) copy-start(f32[128]{0:T(128)} %param.27) | copy-start | bytes 1540
  2.1 12.2 %copy-start.4 = (bf16[128,128]{1,0:T(8,128)(2,1)S(1)}, bf16[128,128]{1,0:T(8,128)(2,1)}, u32[]{:S(2)}) copy-start(bf16[128,128]{1,0:T(8,128)(2,1)} %wa_ref.3) | copy-start | bytes 98308
  2.1 12.2 %copy-start.5 = (bf16[128,128]{1,0:T(8,128)(2,1)S(1)}, bf16[128,128]{1,0:T(8,128)(2,1)}, u32[]{:S(2)}) copy-start(bf16[128,128]{1,0:T(8,128)(2,1)} %wb_ref.3) | copy-start | bytes 98308
  4.5 1.9 %collective-permute-start = (bf16[640,128]{1,0:T(8,128)(2,1)S(1)}, bf16[640,128]{1,0:T(8,128)(2,1)S(1)}, u32[]{:S(2)}, u32[]{:S(2)}) collective-permute-start(bf16[640,128]{1,0:T(8,128)(2,1)S(1)} %get-tuple-element.45.after_ref), channel_id=1, source_target_pairs={{0,1},{1,0},{2,3},{3,2},{4,5},{5,4},{6,7},{7,6},{8,9},{9,8},{10,11... | collective-permute-start | bytes 491528 | tf_op jit(solution)/shard_map/ppermute | solution.py:479
  6.4 8.6 %collective-permute-start.1 = (bf16[368,128]{1,0:T(8,128)(2,1)S(1)}, bf16[368,128]{1,0:T(8,128)(2,1)S(1)}, u32[]{:S(2)}, u32[]{:S(2)}) collective-permute-start(bf16[368,128]{1,0:T(8,128)(2,1)S(1)} %fusion.after_ref), channel_id=1, source_target_pairs={{0,2},{1,3},{2,0},{3,1},{4,6},{5,7},{6,4},{7,5},{8,10},{9,11},{10,... | collective-permute-start | bytes 282632 | tf_op jit(solution)/shard_map/ppermute | solution.py:479
  9.1 6.7 %collective-permute-start.3 = (bf16[272,128]{1,0:T(8,128)(2,1)S(1)}, bf16[272,128]{1,0:T(8,128)(2,1)S(1)}, u32[]{:S(2)}, u32[]{:S(2)}) collective-permute-start(bf16[272,128]{1,0:T(8,128)(2,1)S(1)} %get-tuple-element.48), channel_id=1, source_target_pairs={{0,7},{1,2},{2,1},{3,4},{4,3},{5,6},{6,5},{7,0},{8,15},{9,10},{10,... | collective-permute-start | bytes 208904 | tf_op jit(solution)/shard_map/ppermute | solution.py:479
  11.4 5.2 %collective-permute-start.4 = (bf16[272,128]{1,0:T(8,128)(2,1)S(1)}, bf16[272,128]{1,0:T(8,128)(2,1)S(1)}, u32[]{:S(2)}, u32[]{:S(2)}) collective-permute-start(bf16[272,128]{1,0:T(8,128)(2,1)S(1)} %get-tuple-element.49), channel_id=1, source_target_pairs={{0,8},{8,16},{16,24},{24,0},{1,9},{9,17},{17,25},{25,1},{2,10},{10... | collective-permute-start | bytes 208904 | tf_op jit(solution)/shard_map/ppermute | solution.py:479
  12.9 4.5 %collective-permute-start.5 = (bf16[272,128]{1,0:T(8,128)(2,1)S(1)}, bf16[272,128]{1,0:T(8,128)(2,1)S(1)}, u32[]{:S(2)}, u32[]{:S(2)}) collective-permute-start(bf16[272,128]{1,0:T(8,128)(2,1)S(1)} %get-tuple-element.50), channel_id=1, source_target_pairs={{0,24},{8,0},{16,8},{24,16},{1,25},{9,1},{17,9},{25,17},{2,26},{10... | collective-permute-start | bytes 208904 | tf_op jit(solution)/shard_map/ppermute | solution.py:479
  15.1 7.5 %collective-permute-start.2 = (bf16[368,128]{1,0:T(8,128)(2,1)S(1)}, bf16[368,128]{1,0:T(8,128)(2,1)S(1)}, u32[]{:S(2)}, u32[]{:S(2)}) collective-permute-start(bf16[368,128]{1,0:T(8,128)(2,1)S(1)} %fusion.1.after_ref), channel_id=1, source_target_pairs={{0,4},{1,5},{2,6},{3,7},{4,0},{5,1},{6,2},{7,3},{8,12},{9,13},{10,... | collective-permute-start | bytes 282632 | tf_op jit(solution)/shard_map/ppermute | solution.py:479
  19.2 6.6 %collective-permute-start.6 = (bf16[256,128]{1,0:T(8,128)(2,1)S(1)}, bf16[256,128]{1,0:T(8,128)(2,1)S(1)}, u32[]{:S(2)}, u32[]{:S(2)}) collective-permute-start(bf16[256,128]{1,0:T(8,128)(2,1)S(1)} %get-tuple-element.56), channel_id=1, source_target_pairs={{0,24},{8,0},{16,8},{24,16},{1,25},{9,1},{17,9},{25,17},{2,26},{10... | collective-permute-start | bytes 196616 | tf_op jit(solution)/shard_map/ppermute | solution.py:479
  21.4 5.2 %collective-permute-start.7 = (bf16[256,128]{1,0:T(8,128)(2,1)S(1)}, bf16[256,128]{1,0:T(8,128)(2,1)S(1)}, u32[]{:S(2)}, u32[]{:S(2)}) collective-permute-start(bf16[256,128]{1,0:T(8,128)(2,1)S(1)} %get-tuple-element.57), channel_id=1, source_target_pairs={{0,8},{8,16},{16,24},{24,0},{1,9},{9,17},{17,25},{25,1},{2,10},{10... | collective-permute-start | bytes 196616 | tf_op jit(solution)/shard_map/ppermute | solution.py:479
  22.1 5.5 %collective-permute-start.8 = (bf16[256,128]{1,0:T(8,128)(2,1)S(1)}, bf16[256,128]{1,0:T(8,128)(2,1)S(1)}, u32[]{:S(2)}, u32[]{:S(2)}) collective-permute-start(bf16[256,128]{1,0:T(8,128)(2,1)S(1)} %get-tuple-element.58), channel_id=1, source_target_pairs={{0,7},{1,2},{2,1},{3,4},{4,3},{5,6},{6,5},{7,0},{8,15},{9,10},{10,... | collective-permute-start | bytes 196616 | tf_op jit(solution)/shard_map/ppermute | solution.py:479
  22.7 4.8 %collective-permute-start.9 = (bf16[624,128]{1,0:T(8,128)(2,1)S(1)}, bf16[624,128]{1,0:T(8,128)(2,1)S(1)}, u32[]{:S(2)}, u32[]{:S(2)}) collective-permute-start(bf16[624,128]{1,0:T(8,128)(2,1)S(1)} %pad_maximum_fusion), channel_id=1, source_target_pairs={{0,1},{1,0},{2,3},{3,2},{4,5},{5,4},{6,7},{7,6},{8,9},{9,8},{10,11... | collective-permute-start | bytes 479240 | tf_op jit(solution)/shard_map/ppermute | solution.py:479
  23.7 3.9 %copy-start.9 = (s32[1,4,2]{1,2,0:T(2,128)S(1)}, s32[1,4,2]{1,2,0:T(2,128)}, u32[]{:S(2)}) copy-start(s32[1,4,2]{1,2,0:T(2,128)} %param.19) | copy-start | bytes 100

commit v6 on v5

--- a/solution.py
+++ b/solution.py
@@ -532,7 +532,7 @@
     got1 = exchange(sent[1], "dom", far_pair)
 
     keep, send, trig = call(
-        functools.partial(struct_kernel, 256),
+        functools.partial(struct_kernel, min(atoms, 1024)),
         [
             sds((HALF, width), F32),
             sds((HB * BLK + COORD_ROWS + HALF, width), BF16),

time: 30.4 us -> 30.6 us (level)
  waiting for transfers between devices: 3.45 us -> 4.92 us
  Pallas kernels: 11.9 us -> 11.3 us
  starting transfers between devices: 13.4 us -> 12.8 us
    ppermute x10, waiting for transfers between devices: 3.45 us -> 4.92 us  [exchange(): lax.ppermute(value, axis, [(i, partner(i) % length) for i in range(length)])]
    pallas_call x7, Pallas kernels: 11.9 us -> 11.3 us  [call(): pl.pallas_call(kernel, out_shape=outs, in_specs=[pl.BlockSpec(memory_spac...]
    ppermute x10, starting transfers between devices: 13.4 us -> 12.8 us  [exchange(): lax.ppermute(value, axis, [(i, partner(i) % length) for i in range(length)])]
  transfers between devices with their start and end apart: 10 -> 10, of which waited for: 4 -> 4; matrix products, arithmetic and copies ran while one was open for 0% -> 0% of each run, Pallas kernels for 17% -> 15%
where the time goes in v6:
time: 30.6 us; the launch traced here: 30.7 us
  starting transfers between devices  12.8 us (42%)
  Pallas kernels  11.3 us (37%)
  waiting for transfers between devices  4.92 us (16%)
  between operations  1.52 us (5%)
    ppermute x10, starting transfers between devices, exchange(): lax.ppermute(value, axis, [(i, partner(i) % length) for i in range(length)])  12.8 us
    pallas_call x7, Pallas kernels, call(): pl.pallas_call(kernel, out_shape=outs, in_specs=[pl.BlockSpec(memory_spac...  11.3 us
    ppermute x10, waiting for transfers between devices, exchange(): lax.ppermute(value, axis, [(i, partner(i) % length) for i in range(length)])  4.92 us
  transfers between devices with their start and end apart: 10, of which 4 were waited for; matrix products, arithmetic and copies ran while one was open for 0% of the time, Pallas kernels for 15%

profile of v6, /device:TPU:0, one launch (start us, length us, event | category | flops | bytes accessed | tf_op | source)
XLA Modules:
  0.0 30.7 jit_solution(8750050744465272825)
XLA Ops:
  0.6 0.0 copy-start
  0.7 1.4 %shard_map.167 = (bf16[2048,128]{1,0:T(8,128)(2,1)S(1)}, bf16[3,2048]{1,0:T(4,128)(2,1)S(1)}, bf16[2048,128]{1,0:T(8,128)(2,1)S(1)}, f32[48,16]{1,0:T(8,128)S(1)...) custom-call(s32[1]{0:T(128)} %bitcast.1.flip_ref, ...), custom_call_target="tpu_custom_call" | custom-call | flops 1320000000 | bytes 4080000 | tf_op jit(solution)/shard_map/pallas_call | solution.py:463
  2.1 0.0 copy-start.4
  2.1 0.0 copy-start.5
  2.2 2.2 %shard_map.168 = (f32[368,128]{1,0:T(8,128)S(1)}, bf16[640,128]{1,0:T(8,128)(2,1)S(1)}, bf16[736,2048]{1,0:T(8,128)(2,1)S(1)}) custom-call(s32[1]{0:T(128)} %bitcast.1.flip_ref, bf16[2048,128]{1,0:T(8,128)(2,1)S(1)} %get-tuple-element.39.feats_ref, bf16[3,2048]{1,0:T(4,128)(2,1)S(1)} %get-tuple-element.40.coords_ref, ...), custom_call_target="tpu_custom_call" | custom-call | flops 110000000 | bytes 340000 | tf_op jit(solution)/shard_map/pallas_call | solution.py:463
  4.4 0.5 %collective-permute-start = (bf16[640,128]{1,0:T(8,128)(2,1)S(1)}, bf16[640,128]{1,0:T(8,128)(2,1)S(1)}, u32[]{:S(2)}, u32[]{:S(2)}) collective-permute-start(bf16[640,128]{1,0:T(8,128)(2,1)S(1)} %get-tuple-element.45.after_ref), channel_id=1, source_target_pairs={{0,1},{1,0},{2,3},{3,2},{4,5},{5,4},{6,7},{7,6},{8,9},{9,8},{10,11... | collective-permute-start | bytes 491528 | tf_op jit(solution)/shard_map/ppermute | solution.py:479
  5.6 0.7 %shard_map.169 = (f32[368,128]{1,0:T(8,128)S(1)}, bf16[128,128]{1,0:T(8,128)(2,1)S(1)}, bf16[256,128]{1,0:T(8,128)(2,1)S(1)}, bf16[128,256]{1,0:T(8,128)(2,1)S(1...) custom-call(s32[1]{0:T(128)} %bitcast.1.flip_ref, ...), custom_call_target="tpu_custom_call", output_to_operand_aliasing={{8}: (10, {})} | custom-call | flops 110000000 | bytes 340000 | tf_op jit(solution)/shard_map/pallas_call | solution.py:463
  6.3 0.0 collective-permute-done.got0
  6.3 2.6 %collective-permute-start.1 = (bf16[368,128]{1,0:T(8,128)(2,1)S(1)}, bf16[368,128]{1,0:T(8,128)(2,1)S(1)}, u32[]{:S(2)}, u32[]{:S(2)}) collective-permute-start(bf16[368,128]{1,0:T(8,128)(2,1)S(1)} %fusion.after_ref), channel_id=1, source_target_pairs={{0,2},{1,3},{2,0},{3,1},{4,6},{5,7},{6,4},{7,5},{8,10},{9,11},{10,... | collective-permute-start | bytes 282632 | tf_op jit(solution)/shard_map/ppermute | solution.py:479
  9.0 2.3 %collective-permute-start.3 = (bf16[272,128]{1,0:T(8,128)(2,1)S(1)}, bf16[272,128]{1,0:T(8,128)(2,1)S(1)}, u32[]{:S(2)}, u32[]{:S(2)}) collective-permute-start(bf16[272,128]{1,0:T(8,128)(2,1)S(1)} %get-tuple-element.48), channel_id=1, source_target_pairs={{0,7},{1,2},{2,1},{3,4},{4,3},{5,6},{6,5},{7,0},{8,15},{9,10},{10,... | collective-permute-start | bytes 208904 | tf_op jit(solution)/shard_map/ppermute | solution.py:479
  11.3 1.5 %collective-permute-start.4 = (bf16[272,128]{1,0:T(8,128)(2,1)S(1)}, bf16[272,128]{1,0:T(8,128)(2,1)S(1)}, u32[]{:S(2)}, u32[]{:S(2)}) collective-permute-start(bf16[272,128]{1,0:T(8,128)(2,1)S(1)} %get-tuple-element.49), channel_id=1, source_target_pairs={{0,8},{8,16},{16,24},{24,0},{1,9},{9,17},{17,25},{25,1},{2,10},{10... | collective-permute-start | bytes 208904 | tf_op jit(solution)/shard_map/ppermute | solution.py:479
  12.8 1.4 %collective-permute-start.5 = (bf16[272,128]{1,0:T(8,128)(2,1)S(1)}, bf16[272,128]{1,0:T(8,128)(2,1)S(1)}, u32[]{:S(2)}, u32[]{:S(2)}) collective-permute-start(bf16[272,128]{1,0:T(8,128)(2,1)S(1)} %get-tuple-element.50), channel_id=1, source_target_pairs={{0,24},{8,0},{16,8},{24,16},{1,25},{9,1},{17,9},{25,17},{2,26},{10... | collective-permute-start | bytes 208904 | tf_op jit(solution)/shard_map/ppermute | solution.py:479
  14.2 0.0 copy-done.5
  14.2 0.8 %shard_map.170 = (bf16[24,128,256]{2,1,0:T(8,128)(2,1)S(1)}, bf16[24,128,16]{2,1,0:T(8,128)(2,1)S(1)}, bf16[16,16,128]{2,1,0:T(8,128)(2,1)S(1)}, bf16[16,256,128]{2,1,0:T(8,128)(2,1)S(1)}) custom-call(bf16[2048,128]{1,0:T(8,128)(2,1)S(1)} %get-tuple-element.39.feats_ref, bf16[3,2048]{1,0:T(4,128)(2,1)S(1)} %get-tuple-element.40.coords_ref, ...), custom_call_target="tpu_custom_call" | custom-call | flops 110000000 | bytes 340000 | tf_op jit(solution)/shard_map/pallas_call | solution.py:463
  15.0 0.0 collective-permute-done.1
  15.0 0.6 %collective-permute-start.2 = (bf16[368,128]{1,0:T(8,128)(2,1)S(1)}, bf16[368,128]{1,0:T(8,128)(2,1)S(1)}, u32[]{:S(2)}, u32[]{:S(2)}) collective-permute-start(bf16[368,128]{1,0:T(8,128)(2,1)S(1)} %fusion.1.after_ref), channel_id=1, source_target_pairs={{0,4},{1,5},{2,6},{3,7},{4,0},{5,1},{6,2},{7,3},{8,12},{9,13},{10,... | collective-permute-start | bytes 282632 | tf_op jit(solution)/shard_map/ppermute | solution.py:479
  15.6 0.0 collective-permute-done.3.got1
  15.6 0.8 %collective-permute-done.4.got2 = bf16[272,128]{1,0:T(8,128)(2,1)S(1)} collective-permute-done((bf16[272,128]{1,0:T(8,128)(2,1)S(1)}, bf16[272,128]{1,0:T(8,128)(2,1)S(1)}, u32[]{:S(2)}, u32[]{:S(2)}) %collective-permute-start.4) | collective-permute-done | bytes 69664 | tf_op jit(solution)/shard_map/ppermute | solution.py:479
  16.5 0.8 %collective-permute-done.5.got3 = bf16[272,128]{1,0:T(8,128)(2,1)S(1)} collective-permute-done((bf16[272,128]{1,0:T(8,128)(2,1)S(1)}, bf16[272,128]{1,0:T(8,128)(2,1)S(1)}, u32[]{:S(2)}, u32[]{:S(2)}) %collective-permute-start.5) | collective-permute-done | bytes 69664 | tf_op jit(solution)/shard_map/ppermute | solution.py:479
  17.3 1.8 %shard_map.171 = (bf16[24,128,256]{2,1,0:T(8,128)(2,1)S(1)}, bf16[24,128,16]{2,1,0:T(8,128)(2,1)S(1)}, f32[17,128,128]{2,1,0:T(8,128)S(1)}, f32[25,128,128]{2,1,...) custom-call(s32[8,96]{1,0:T(8,128)S(1)} %get-tuple-element.46.plan_v, ...), custom_call_target="tpu_custom_call", output_to_operand_aliasing={{0}: (9, {}), {1}: (10, {})} | custom-call | flops 3300000000 | bytes 10200000 | tf_op jit(solution)/shard_map/pallas_call | solution.py:463
  19.1 2.7 %collective-permute-start.6 = (bf16[256,128]{1,0:T(8,128)(2,1)S(1)}, bf16[256,128]{1,0:T(8,128)(2,1)S(1)}, u32[]{:S(2)}, u32[]{:S(2)}) collective-permute-start(bf16[256,128]{1,0:T(8,128)(2,1)S(1)} %get-tuple-element.56), channel_id=1, source_target_pairs={{0,24},{8,0},{16,8},{24,16},{1,25},{9,1},{17,9},{25,17},{2,26},{10... | collective-permute-start | bytes 196616 | tf_op jit(solution)/shard_map/ppermute | solution.py:479
  21.8 0.5 %collective-permute-start.7 = (bf16[256,128]{1,0:T(8,128)(2,1)S(1)}, bf16[256,128]{1,0:T(8,128)(2,1)S(1)}, u32[]{:S(2)}, u32[]{:S(2)}) collective-permute-start(bf16[256,128]{1,0:T(8,128)(2,1)S(1)} %get-tuple-element.57), channel_id=1, source_target_pairs={{0,8},{8,16},{16,24},{24,0},{1,9},{9,17},{17,25},{25,1},{2,10},{10... | collective-permute-start | bytes 196616 | tf_op jit(solution)/shard_map/ppermute | solution.py:479
  22.3 0.2 collective-permute-start.8
  22.5 0.0 collective-permute-done.2
  22.5 0.1 add_convert_fusion.mine_ref
  22.6 0.4 %collective-permute-start.9 = (bf16[624,128]{1,0:T(8,128)(2,1)S(1)}, bf16[624,128]{1,0:T(8,128)(2,1)S(1)}, u32[]{:S(2)}, u32[]{:S(2)}) collective-permute-start(bf16[624,128]{1,0:T(8,128)(2,1)S(1)} %pad_maximum_fusion), channel_id=1, source_target_pairs={{0,1},{1,0},{2,3},{3,2},{4,5},{5,4},{6,7},{7,6},{8,9},{9,8},{10,11... | collective-permute-start | bytes 479240 | tf_op jit(solution)/shard_map/ppermute | solution.py:479
  23.0 1.5 %shard_map.172 = (f32[17,128,128]{2,1,0:T(8,128)S(1)}, f32[25,128,128]{2,1,0:T(8,128)S(1)}) custom-call(s32[8,96]{1,0:T(8,128)S(1)} %get-tuple-element.46.plan_vmem.plan_ref, bf16[24,128,256]{2,1,0:T(8,128)(2,1)S(1)} %get-tuple-element.63.proj_ref, bf16[24,128,16]{2,1,0:T(8,128)(2,1)S(1)} %get-tuple-element.64.far_ref, ...), custom_call_target="tpu_custom_call", output_to_operand_aliasing={{0}: (5, {}), {1}: (6, {})} | custom-call | flops 5500000256 | bytes 17000000 | tf_op jit(solution)/shard_map/pallas_call | solution.py:463
  24.5 0.0 collective-permute-done.6.back2
  24.6 2.4 %collective-permute-done.7.back3 = bf16[256,128]{1,0:T(8,128)(2,1)S(1)} collective-permute-done((bf16[256,128]{1,0:T(8,128)(2,1)S(1)}, bf16[256,128]{1,0:T(8,128)(2,1)S(1)}, u32[]{:S(2)}, u32[]{:S(2)}) %collective-permute-start.7) | collective-permute-done | bytes 65568 | tf_op jit(solution)/shard_map/ppermute | solution.py:479
  27.0 0.8 %collective-permute-done.8.back1 = bf16[256,128]{1,0:T(8,128)(2,1)S(1)} collective-permute-done((bf16[256,128]{1,0:T(8,128)(2,1)S(1)}, bf16[256,128]{1,0:T(8,128)(2,1)S(1)}, u32[]{:S(2)}, u32[]{:S(2)}) %collective-permute-start.8) | collective-permute-done | bytes 65568 | tf_op jit(solution)/shard_map/ppermute | solution.py:479
  27.8 0.0 collective-permute-done.9.back0
  27.8 2.9 %shard_map.173 = (bf16[2048,128]{1,0:T(8,128)(2,1)}, f32[16,128,128]{2,1,0:T(8,128)}, f32[25,128,128]{2,1,0:T(8,128)S(1)}) custom-call(s32[1,2,4]{2,1,0:T(2,128)S(1)} %bitcast.12, s32[8,96]{1,0:T(8,128)S(1)} %get-tuple-element.46.plan_vmem.plan_ref, bf16[368,128]{1,0:T(8,128)(2,1)S(1)} %add_convert_fusion.mine_ref, ...), custom_call_target="tpu_custom_call", output_to_operand_aliasing={{2}: (16, {})} | custom-call | flops 3300000000 | bytes 10200000 | tf_op jit(solution)/shard_map/pallas_call | solution.py:463
  (19 shorter events, 0.1 us)
Async XLA Ops:
  0.6 4.9 %copy-start = (f32[368,1]{1,0:T(8,128)S(1)}, f32[368,1]{1,0:T(8,128)}, u32[]{:S(2)}) copy-start(f32[368,1]{1,0:T(8,128)} %constant.22.clone.norm2_ref) | copy-start | bytes 4420
  0.7 4.9 %copy-start.1 = (bf16[128,256]{1,0:T(8,128)(2,1)S(1)}, bf16[128,256]{1,0:T(8,128)(2,1)}, u32[]{:S(2)}) copy-start(bf16[128,256]{1,0:T(8,128)(2,1)} %w_in_ref.1) | copy-start | bytes 196612
  0.7 4.9 %copy-start.2 = (bf16[256,128]{1,0:T(8,128)(2,1)S(1)}, bf16[256,128]{1,0:T(8,128)(2,1)}, u32[]{:S(2)}) copy-start(bf16[256,128]{1,0:T(8,128)(2,1)} %w_out_ref.1) | copy-start | bytes 196612
  0.7 4.9 %copy-start.3 = (bf16[128,128]{1,0:T(8,128)(2,1)S(1)}, bf16[128,128]{1,0:T(8,128)(2,1)}, u32[]{:S(2)}) copy-start(bf16[128,128]{1,0:T(8,128)(2,1)} %w_long_ref.1) | copy-start | bytes 98308
  0.7 4.9 %copy-start.6 = (s32[512,3]{0,1:T(4,128)S(1)}, s32[512,3]{0,1:T(4,128)}, u32[]{:S(2)}) copy-start(s32[512,3]{0,1:T(4,128)} %param.22) | copy-start | bytes 18436
  0.7 4.9 %copy-start.7 = (s32[1,96,2]{1,2,0:T(2,128)S(1)}, s32[1,96,2]{1,2,0:T(2,128)}, u32[]{:S(2)}) copy-start(s32[1,96,2]{1,2,0:T(2,128)} %param.20) | copy-start | bytes 2308
  0.7 4.9 %copy-start.8 = (f32[128]{0:T(128)S(1)}, f32[128]{0:T(128)}, u32[]{:S(2)}) copy-start(f32[128]{0:T(128)} %param.27) | copy-start | bytes 1540
  2.1 12.1 %copy-start.4 = (bf16[128,128]{1,0:T(8,128)(2,1)S(1)}, bf16[128,128]{1,0:T(8,128)(2,1)}, u32[]{:S(2)}) copy-start(bf16[128,128]{1,0:T(8,128)(2,1)} %wa_ref.3) | copy-start | bytes 98308
  2.1 12.1 %copy-start.5 = (bf16[128,128]{1,0:T(8,128)(2,1)S(1)}, bf16[128,128]{1,0:T(8,128)(2,1)}, u32[]{:S(2)}) copy-start(bf16[128,128]{1,0:T(8,128)(2,1)} %wb_ref.3) | copy-start | bytes 98308
  4.4 1.9 %collective-permute-start = (bf16[640,128]{1,0:T(8,128)(2,1)S(1)}, bf16[640,128]{1,0:T(8,128)(2,1)S(1)}, u32[]{:S(2)}, u32[]{:S(2)}) collective-permute-start(bf16[640,128]{1,0:T(8,128)(2,1)S(1)} %get-tuple-element.45.after_ref), channel_id=1, source_target_pairs={{0,1},{1,0},{2,3},{3,2},{4,5},{5,4},{6,7},{7,6},{8,9},{9,8},{10,11... | collective-permute-start | bytes 491528 | tf_op jit(solution)/shard_map/ppermute | solution.py:479
  6.3 8.6 %collective-permute-start.1 = (bf16[368,128]{1,0:T(8,128)(2,1)S(1)}, bf16[368,128]{1,0:T(8,128)(2,1)S(1)}, u32[]{:S(2)}, u32[]{:S(2)}) collective-permute-start(bf16[368,128]{1,0:T(8,128)(2,1)S(1)} %fusion.after_ref), channel_id=1, source_target_pairs={{0,2},{1,3},{2,0},{3,1},{4,6},{5,7},{6,4},{7,5},{8,10},{9,11},{10,... | collective-permute-start | bytes 282632 | tf_op jit(solution)/shard_map/ppermute | solution.py:479
  9.0 6.7 %collective-permute-start.3 = (bf16[272,128]{1,0:T(8,128)(2,1)S(1)}, bf16[272,128]{1,0:T(8,128)(2,1)S(1)}, u32[]{:S(2)}, u32[]{:S(2)}) collective-permute-start(bf16[272,128]{1,0:T(8,128)(2,1)S(1)} %get-tuple-element.48), channel_id=1, source_target_pairs={{0,7},{1,2},{2,1},{3,4},{4,3},{5,6},{6,5},{7,0},{8,15},{9,10},{10,... | collective-permute-start | bytes 208904 | tf_op jit(solution)/shard_map/ppermute | solution.py:479
  11.3 5.2 %collective-permute-start.4 = (bf16[272,128]{1,0:T(8,128)(2,1)S(1)}, bf16[272,128]{1,0:T(8,128)(2,1)S(1)}, u32[]{:S(2)}, u32[]{:S(2)}) collective-permute-start(bf16[272,128]{1,0:T(8,128)(2,1)S(1)} %get-tuple-element.49), channel_id=1, source_target_pairs={{0,8},{8,16},{16,24},{24,0},{1,9},{9,17},{17,25},{25,1},{2,10},{10... | collective-permute-start | bytes 208904 | tf_op jit(solution)/shard_map/ppermute | solution.py:479
  12.8 4.5 %collective-permute-start.5 = (bf16[272,128]{1,0:T(8,128)(2,1)S(1)}, bf16[272,128]{1,0:T(8,128)(2,1)S(1)}, u32[]{:S(2)}, u32[]{:S(2)}) collective-permute-start(bf16[272,128]{1,0:T(8,128)(2,1)S(1)} %get-tuple-element.50), channel_id=1, source_target_pairs={{0,24},{8,0},{16,8},{24,16},{1,25},{9,1},{17,9},{25,17},{2,26},{10... | collective-permute-start | bytes 208904 | tf_op jit(solution)/shard_map/ppermute | solution.py:479
  15.0 7.5 %collective-permute-start.2 = (bf16[368,128]{1,0:T(8,128)(2,1)S(1)}, bf16[368,128]{1,0:T(8,128)(2,1)S(1)}, u32[]{:S(2)}, u32[]{:S(2)}) collective-permute-start(bf16[368,128]{1,0:T(8,128)(2,1)S(1)} %fusion.1.after_ref), channel_id=1, source_target_pairs={{0,4},{1,5},{2,6},{3,7},{4,0},{5,1},{6,2},{7,3},{8,12},{9,13},{10,... | collective-permute-start | bytes 282632 | tf_op jit(solution)/shard_map/ppermute | solution.py:479
  19.1 5.5 %collective-permute-start.6 = (bf16[256,128]{1,0:T(8,128)(2,1)S(1)}, bf16[256,128]{1,0:T(8,128)(2,1)S(1)}, u32[]{:S(2)}, u32[]{:S(2)}) collective-permute-start(bf16[256,128]{1,0:T(8,128)(2,1)S(1)} %get-tuple-element.56), channel_id=1, source_target_pairs={{0,24},{8,0},{16,8},{24,16},{1,25},{9,1},{17,9},{25,17},{2,26},{10... | collective-permute-start | bytes 196616 | tf_op jit(solution)/shard_map/ppermute | solution.py:479
  21.8 5.2 %collective-permute-start.7 = (bf16[256,128]{1,0:T(8,128)(2,1)S(1)}, bf16[256,128]{1,0:T(8,128)(2,1)S(1)}, u32[]{:S(2)}, u32[]{:S(2)}) collective-permute-start(bf16[256,128]{1,0:T(8,128)(2,1)S(1)} %get-tuple-element.57), channel_id=1, source_target_pairs={{0,8},{8,16},{16,24},{24,0},{1,9},{9,17},{17,25},{25,1},{2,10},{10... | collective-permute-start | bytes 196616 | tf_op jit(solution)/shard_map/ppermute | solution.py:479
  22.3 5.5 %collective-permute-start.8 = (bf16[256,128]{1,0:T(8,128)(2,1)S(1)}, bf16[256,128]{1,0:T(8,128)(2,1)S(1)}, u32[]{:S(2)}, u32[]{:S(2)}) collective-permute-start(bf16[256,128]{1,0:T(8,128)(2,1)S(1)} %get-tuple-element.58), channel_id=1, source_target_pairs={{0,7},{1,2},{2,1},{3,4},{4,3},{5,6},{6,5},{7,0},{8,15},{9,10},{10,... | collective-permute-start | bytes 196616 | tf_op jit(solution)/shard_map/ppermute | solution.py:479
  22.6 5.2 %collective-permute-start.9 = (bf16[624,128]{1,0:T(8,128)(2,1)S(1)}, bf16[624,128]{1,0:T(8,128)(2,1)S(1)}, u32[]{:S(2)}, u32[]{:S(2)}) collective-permute-start(bf16[624,128]{1,0:T(8,128)(2,1)S(1)} %pad_maximum_fusion), channel_id=1, source_target_pairs={{0,1},{1,0},{2,3},{3,2},{4,5},{5,4},{6,7},{7,6},{8,9},{9,8},{10,11... | collective-permute-start | bytes 479240 | tf_op jit(solution)/shard_map/ppermute | solution.py:479
  23.0 4.8 %copy-start.9 = (s32[1,4,2]{1,2,0:T(2,128)S(1)}, s32[1,4,2]{1,2,0:T(2,128)}, u32[]{:S(2)}) copy-start(s32[1,4,2]{1,2,0:T(2,128)} %param.19) | copy-start | bytes 100
